TPU v7x, 512 devices: a whole 4x4x16 slice. The times are simulated.
512 devices in a mesh: dp: 64 (over z, y), mp: 8 (over x, core).
Axes of the slice: x: 4, y: 4, z: 16, core: 2. Of those that a mesh axis runs over, the one named last changes fastest.
Arguments:
- gradient: bfloat16 [4096, 16384], P('dp', 'mp')
- second_moment: float32 [4096, 16384], P('dp', 'mp'), may hold values from 0.001 to 0.1
- owner_table: int32 [256], replicated, may hold values from 0 to 63, as said below
- left_stats: float32 [64, 4, 512, 512], P('dp', None, 'mp'), as said below
- right_stats: float32 [64, 4, 512, 512], P('dp', None, 'mp'), as said below
- left_root: bfloat16 [64, 4, 512, 512], P('dp', None, 'mp'), as said below
- right_root: bfloat16 [64, 4, 512, 512], P('dp', None, 'mp'), as said below
- momentum: bfloat16 [64, 4, 512, 512], P('dp', None, 'mp'), may hold values from -12 to 12
Outputs:
- update: bfloat16 [4096, 16384], P('dp', 'mp')
- new_second_moment: float32 [4096, 16384], P('dp', 'mp')
- new_left_stats: float32 [64, 4, 512, 512], P('dp', None, 'mp')
- new_right_stats: float32 [64, 4, 512, 512], P('dp', None, 'mp')
- new_momentum: bfloat16 [64, 4, 512, 512], P('dp', None, 'mp')
Inputs may be any that keep to these rules, and one draw needn't show every extreme that they name: `owner_table`: every index of dp owns exactly 4 blocks. Within one band of 32 blocks (block ids b with equal b // 32) no index owns more than 1 block, so the 32 blocks of a band have 32 distinct owners. `left_stats`: symmetric in its last two dimensions. `right_stats`: symmetric in its last two dimensions. `left_root`: symmetric in its last two dimensions. `right_root`: symmetric in its last two dimensions.
All inputs are finite; a program needn't handle non-finite values.
Results may differ from a plain program's by a relative error of at most 0.0095.
Values may be sent and summed in bfloat16 or wider, within the bound.
No kernel may reach another device: no remote copies, remote signals or barrier semaphores. Data moves between devices by JAX's collectives and lax.ppermute only.
A program may use at most 64 MiB of HBM per device.

v0:
```python
import math

import jax
import jax.numpy as jnp
from jax import lax
from jax.sharding import PartitionSpec as P

BLK = 512
ROWS = 4096
COLS = 16384


def shards(
    gradient, second_moment, owner_table, left_stats, right_stats, left_root, right_root, momentum
):
    owners = lax.axis_size("dp")
    groups = lax.axis_size("mp")
    owner_index = lax.axis_index("dp")
    group_index = lax.axis_index("mp")
    row_dev, local_width = gradient.shape
    band_devices = BLK // row_dev
    col_blocks = COLS // BLK
    band_count = ROWS // BLK
    all_blocks = band_count * col_blocks
    capacity = (col_blocks + owners - 1) // owners
    blk_own = left_stats.shape[1]
    stat_rows = left_stats.shape[2]
    sub_rows = row_dev // groups
    local_blocks = local_width // BLK
    slot_count = owners * capacity
    grad_f32 = gradient.astype(jnp.float32)
    new_second_moment = 0.999 * second_moment + 0.001 * grad_f32 * grad_f32
    adam_dir = grad_f32 / (jnp.sqrt(new_second_moment) + 1e-08)
    adam_part = jnp.sum((adam_dir * adam_dir).reshape(row_dev, local_blocks, BLK), axis=(0, 2)) / (
        BLK * BLK
    )
    my_band = owner_index // band_devices
    adam_vec = lax.dynamic_update_slice(
        jnp.zeros((all_blocks,), jnp.float32),
        adam_part,
        (my_band * col_blocks + group_index * local_blocks,),
    )
    band_owner = lax.dynamic_slice(owner_table, (my_band * col_blocks,), (col_blocks,))
    col_iota = jnp.arange(col_blocks, dtype=jnp.int32)
    same_owner = band_owner[:, None] == band_owner[None, :]
    earlier = col_iota[None, :] < col_iota[:, None]
    band_rank = jnp.sum((same_owner & earlier).astype(jnp.int32), axis=1)
    send_slot = band_owner * capacity + band_rank
    routing = (jnp.arange(slot_count, dtype=jnp.int32)[:, None] == send_slot[None, :]).astype(
        jnp.bfloat16
    )
    ordering = jnp.argsort(owner_table, stable=True)
    owned_ids = lax.dynamic_slice(ordering, (owner_index * blk_own,), (blk_own,))
    owned_band = owned_ids // col_blocks
    own_iota = jnp.arange(blk_own, dtype=jnp.int32)
    owned_rank = jnp.sum(
        (
            (owned_band[:, None] == owned_band[None, :]) & (own_iota[None, :] < own_iota[:, None])
        ).astype(jnp.int32),
        axis=1,
    )
    row_all = lax.all_gather(gradient, "mp", axis=1, tiled=True)
    pieces = row_all.reshape(row_dev, col_blocks, BLK)
    outgoing = jnp.einsum(
        "qj,rjc->qrc", routing, pieces, preferred_element_type=jnp.float32
    ).astype(jnp.bfloat16)
    incoming = lax.all_to_all(
        outgoing.reshape(owners, capacity, row_dev, BLK),
        "dp",
        split_axis=0,
        concat_axis=0,
        tiled=True,
    )
    incoming = incoming.reshape(band_count, band_devices, capacity, row_dev, BLK)
    gathered = incoming[owned_band, :, owned_rank]
    full_blocks = gathered.reshape(blk_own, BLK, BLK)
    my_rows = lax.dynamic_slice_in_dim(full_blocks, group_index * stat_rows, stat_rows, 1)
    my_cols = lax.dynamic_slice_in_dim(full_blocks, group_index * stat_rows, stat_rows, 2)
    left_new = 0.95 * left_stats[0] + 0.05 * jnp.einsum(
        "trc,tkc->trk", my_rows, full_blocks, preferred_element_type=jnp.float32
    )
    right_new = 0.95 * right_stats[0] + 0.05 * jnp.einsum(
        "tic,tik->tck", my_cols, full_blocks, preferred_element_type=jnp.float32
    )
    left_applied = jnp.einsum(
        "trk,tkc->trc", left_root[0], full_blocks, preferred_element_type=jnp.float32
    ).astype(jnp.bfloat16)
    precond = jnp.einsum(
        "trk,tkc->trc",
        left_applied,
        lax.all_gather(right_root, "mp", axis=2, tiled=True)[0],
        preferred_element_type=jnp.float32,
    )
    moment_old = momentum[0].astype(jnp.float32)
    precond_sq = jnp.sum(precond * precond, axis=(1, 2))
    chooser = (jnp.arange(all_blocks, dtype=jnp.int32)[None, :] == owned_ids[:, None]).astype(
        jnp.float32
    )
    area = BLK * BLK
    adam_total = lax.psum(adam_vec, ("dp", "mp"))
    precond_total = lax.psum(precond_sq, "mp")
    adam_mine = jnp.sum(chooser * adam_total[None, :], axis=1)
    graft_scale = jnp.sqrt(adam_mine) / jnp.sqrt(precond_total / area + 1e-06)
    momentum_new = 0.9 * moment_old + graft_scale[:, None, None] * precond
    total_norm = lax.psum(jnp.sum(momentum_new * momentum_new), ("dp", "mp"))
    clip_factor = jnp.minimum(1.0, 0.5 * math.sqrt(ROWS * COLS) / jnp.sqrt(total_norm))
    update_rows = (clip_factor * momentum_new).astype(jnp.bfloat16)
    regrouped = lax.all_to_all(
        update_rows.reshape(blk_own, groups, sub_rows, BLK),
        "mp",
        split_axis=1,
        concat_axis=1,
        tiled=True,
    )
    span_iota = jnp.arange(band_devices, dtype=jnp.int32)
    dest_flat = (
        (owned_band[:, None] * band_devices + span_iota[None, :]) * capacity + owned_rank[:, None]
    ).reshape(blk_own * band_devices)
    routing_back = (jnp.arange(slot_count, dtype=jnp.int32)[:, None] == dest_flat[None, :]).astype(
        jnp.bfloat16
    )
    outgoing_back = jnp.einsum(
        "qk,kyc->qyc",
        routing_back,
        regrouped.reshape(blk_own * band_devices, sub_rows, BLK),
        preferred_element_type=jnp.float32,
    ).astype(jnp.bfloat16)
    returned = lax.all_to_all(
        outgoing_back.reshape(owners, capacity, sub_rows, BLK),
        "dp",
        split_axis=0,
        concat_axis=0,
        tiled=True,
    )
    placed = jnp.einsum(
        "qj,qyc->yjc",
        routing,
        returned.reshape(slot_count, sub_rows, BLK),
        preferred_element_type=jnp.float32,
    ).astype(jnp.bfloat16)
    update = lax.all_to_all(
        placed.reshape(sub_rows, col_blocks * BLK), "mp", split_axis=1, concat_axis=0, tiled=True
    )
    return (
        update,
        new_second_moment,
        left_new[None],
        right_new[None],
        momentum_new.astype(jnp.bfloat16)[None],
    )


def solution(mesh):
    return jax.shard_map(
        shards,
        mesh=mesh,
        in_specs=(
            P("dp", "mp"),
            P("dp", "mp"),
            P(),
            P("dp", None, "mp", None),
            P("dp", None, "mp", None),
            P("dp", None, "mp", None),
            P("dp", None, "mp", None),
            P("dp", None, "mp", None),
        ),
        out_specs=(
            P("dp", "mp"),
            P("dp", "mp"),
            P("dp", None, "mp", None),
            P("dp", None, "mp", None),
            P("dp", None, "mp", None),
        ),
        check_vma=False,
    )
```

profile of v0, /device:TPU:1, one launch (start us, length us, event | category | flops | bytes accessed | tf_op | source)
XLA Modules:
  0.0 523.0 jit_solution(11526951833004215133)
XLA Ops:
  7.2 0.0 copy-start
  7.2 0.0 all-gather.3.cloned.1.call-start
  7.2 0.7 all-gather.3.cloned.1.call-update
  7.9 0.8 dynamic_slice.13
  8.7 0.2 convert_reduce_fusion
  8.9 0.8 dynamic-slice_add_fusion
  9.6 39.1 %all-gather.3.cloned.1.call-done = bf16[64,16384]{1,0:T(8,128)(2,1)} async-done(((bf16[64,2048]{1,0:T(8,128)(2,1)}), bf16[64,16384]{1,0:T(8,128)(2,1)}) %all-gather.3.cloned.1.call-update) | async-done | bytes 2097168 | tf_op jit(solution)/shard_map/all_gather | solution.py:62
  48.7 2.3 copy.32
  51.1 1.4 convert_bitcast_fusion
  52.4 4.4 copy.24
  56.8 0.0 copy-start.5
  56.8 0.0 copy-start.1
  56.8 0.0 copy-start.3
  56.8 15.8 %all-to-all-start = ((bf16[64,1,64,512]{3,2,1,0:T(8,128)(2,1)}), bf16[64,1,64,512]{3,2,1,0:T(8,128)(2,1)}, u32[]{:S(2)}, u32[]{:S(2)}) async-start(bf16[64,1,64,512]{3,2,1,0:T(8,128)(2,1)} %copy.24), calls=%async_computation | async-start | bytes 8388608 | tf_op jit(solution)/shard_map/all_to_all | solution.py:67
  72.6 0.0 all-gather.5.cloned.1.call-start
  72.6 0.7 all-gather.5.cloned.1.call-update
  73.3 0.0 copy-done.5
  73.4 3.2 sort.17
  76.5 0.0 copy-done.1
  76.5 0.0 copy-done.3
  76.5 1.1 fusion.13
  77.6 0.1 reduce_sum.66
  77.7 0.1 multiply_dynamic-update-slice_fusion
  77.8 248.3 %psum.21 = f32[256]{0:T(256)S(1)} all-reduce(f32[256]{0:T(256)S(1)} %multiply_dynamic-update-slice_fusion), channel_id=1, replica_groups=mesh['dp'=64,'mp'=8] {'dp','mp'}, use_global_device_ids=true, to_apply=%region_4.5 | all-reduce | flops 256 | bytes 2048 | tf_op jit(solution)/shard_map/psum | solution.py:100
  326.1 0.1 broadcast_multiply_fusion
  326.2 0.2 convert_reduce_fusion.1
  326.4 0.2 select_reduce_fusion
  326.6 0.0 all-to-all-done
  326.6 2.9 gather_fusion
  329.5 0.0 all-gather.5.cloned.1.call-done
  329.5 0.0 copy-done
  329.5 0.0 copy-start.2
  329.5 2.6 multiply_reduce_fusion.1
  332.1 12.4 %psum.22 = f32[4]{0:T(128)S(1)} all-reduce(f32[4]{0:T(128)S(1)} %get-tuple-element.14), channel_id=1, replica_groups=mesh['dp'=64,'mp'=8] {'mp'}, use_global_device_ids=true, to_apply=%region_8.9 | all-reduce | flops 4 | bytes 32 | tf_op jit(solution)/shard_map/psum | solution.py:101
  344.6 0.0 copy-done.2
  344.6 0.8 multiply_reduce_fusion
  345.4 100.3 %psum.23 = f32[]{:T(128)} all-reduce(f32[]{:T(128)} %multiply_reduce_fusion), channel_id=1, replica_groups=mesh['dp'=64,'mp'=8] {'dp','mp'}, use_global_device_ids=true, to_apply=%region_10.11 | all-reduce | flops 1 | bytes 8 | tf_op jit(solution)/shard_map/psum | solution.py:105
  446.4 0.9 convert_bitcast_fusion.1
  447.2 0.0 copy-start.4
  447.2 0.7 copy.25
  448.0 4.4 all-to-all-start.1
  452.4 0.1 add_add_fusion
  452.5 0.1 add.100
  452.6 6.3 %all-to-all-done.1 = bf16[4,8,8,512]{3,2,0,1:T(8,128)(2,1)S(1)} async-done(((bf16[4,8,8,512]{3,2,0,1:T(8,128)(2,1)}), bf16[4,8,8,512]{3,2,0,1:T(8,128)(2,1)S(1)}, u32[]{:S(2)}, u32[]{:S(2)}) %all-to-all-start.1) | async-done | bytes 262176 | tf_op jit(solution)/shard_map/all_to_all | solution.py:108
  458.9 0.4 fusion.2
  459.3 1.1 copy.27
  460.4 10.1 %all-to-all-start.2 = ((bf16[64,1,8,512]{3,2,1,0:T(8,128)(2,1)}), bf16[64,1,8,512]{3,2,1,0:T(8,128)(2,1)S(1)}, u32[]{:S(2)}, u32[]{:S(2)}) async-start(bf16[64,1,8,512]{3,2,1,0:T(8,128)(2,1)} %copy.27), calls=%async_computation.2 | async-start | bytes 1048576 | tf_op jit(solution)/shard_map/all_to_all | solution.py:128
  470.5 0.0 copy-done.4
  470.5 1.5 fusion.4
  472.0 27.7 %all-to-all-done.2 = bf16[64,1,8,512]{3,2,1,0:T(8,128)(2,1)S(1)} async-done(((bf16[64,1,8,512]{3,2,1,0:T(8,128)(2,1)}), bf16[64,1,8,512]{3,2,1,0:T(8,128)(2,1)S(1)}, u32[]{:S(2)}, u32[]{:S(2)}) %all-to-all-start.2) | async-done | bytes 524320 | tf_op jit(solution)/shard_map/all_to_all | solution.py:128
  499.7 0.3 fusion.7
  499.9 0.2 all_to_all.26
  500.1 0.9 copy.29
  501.0 7.9 %all-to-all-start.3 = ((bf16[8,8,2048]{2,0,1:T(8,128)(2,1)}), bf16[8,8,2048]{2,0,1:T(8,128)(2,1)S(1)}, u32[]{:S(2)}, u32[]{:S(2)}) async-start(bf16[8,8,2048]{2,0,1:T(8,128)(2,1)} %copy.29), calls=%async_computation.3 | async-start | bytes 524288 | tf_op jit(solution)/shard_map/all_to_all | solution.py:141
  508.9 2.6 fusion.6
  511.5 3.9 all-to-all-done.3
  515.4 0.7 copy.43
  (5 shorter events, 0.0 us)
Async XLA Ops:
  7.2 322.3 %copy-start = (bf16[1,4,64,512]{3,2,1,0:T(8,128)(2,1)S(1)}, bf16[1,4,64,512]{3,2,1,0:T(8,128)(2,1)}, u32[]{:S(2)}) copy-start(bf16[1,4,64,512]{3,2,1,0:T(8,128)(2,1)} %param.13) | copy-start | bytes 786436
  7.2 41.5 %all-gather.3.cloned.1.call-start = ((), (), s32[]{:S(2)}) async-start(), calls=%async_computation.4 | async-start | bytes 2359296 | tf_op jit(solution)/shard_map/all_gather | solution.py:62
  56.8 16.6 %copy-start.5 = (s32[256]{0:T(256)S(1)}, s32[256]{0:T(256)}, u32[]{:S(2)}) copy-start(s32[256]{0:T(256)} %param.10) | copy-start | bytes 3076
  56.8 19.7 %copy-start.1 = (bf16[64,2048]{1,0:T(8,128)(2,1)S(1)}, bf16[64,2048]{1,0:T(8,128)(2,1)}, u32[]{:S(2)}) copy-start(bf16[64,2048]{1,0:T(8,128)(2,1)} %param.8) | copy-start | bytes 786436
  56.8 19.7 %copy-start.3 = (f32[64,2048]{1,0:T(8,128)S(1)}, f32[64,2048]{1,0:T(8,128)}, u32[]{:S(2)}) copy-start(f32[64,2048]{1,0:T(8,128)} %param.9) | copy-start | bytes 1572868
  56.8 269.8 %all-to-all-start = ((bf16[64,1,64,512]{3,2,1,0:T(8,128)(2,1)}), bf16[64,1,64,512]{3,2,1,0:T(8,128)(2,1)}, u32[]{:S(2)}, u32[]{:S(2)}) async-start(bf16[64,1,64,512]{3,2,1,0:T(8,128)(2,1)} %copy.24), calls=%async_computation | async-start | bytes 8388608 | tf_op jit(solution)/shard_map/all_to_all | solution.py:67
  72.6 256.9 %all-gather.5.cloned.1.call-start = ((), (), s32[]{:S(2)}) async-start(), calls=%async_computation.5 | async-start | bytes 2359296 | tf_op jit(solution)/shard_map/all_gather | solution.py:91
  329.5 15.0 %copy-start.2 = (bf16[1,4,64,512]{3,2,1,0:T(8,128)(2,1)S(1)}, bf16[1,4,64,512]{3,2,1,0:T(8,128)(2,1)}, u32[]{:S(2)}) copy-start(bf16[1,4,64,512]{3,2,1,0:T(8,128)(2,1)} %param.15) | copy-start | bytes 786436
  447.2 23.2 %copy-start.4 = (f32[1,4,64,512]{3,2,1,0:T(8,128)S(1)}, f32[1,4,64,512]{3,2,1,0:T(8,128)}, u32[]{:S(2)}) copy-start(f32[1,4,64,512]{3,2,1,0:T(8,128)} %param.12) | copy-start | bytes 1572868
  448.0 10.9 %all-to-all-start.1 = ((bf16[4,8,8,512]{3,2,0,1:T(8,128)(2,1)}), bf16[4,8,8,512]{3,2,0,1:T(8,128)(2,1)S(1)}, u32[]{:S(2)}, u32[]{:S(2)}) async-start(bf16[4,8,8,512]{3,2,0,1:T(8,128)(2,1)} %copy.25), calls=%async_computation.1 | async-start | bytes 524288 | tf_op jit(solution)/shard_map/all_to_all | solution.py:108
  460.4 39.2 %all-to-all-start.2 = ((bf16[64,1,8,512]{3,2,1,0:T(8,128)(2,1)}), bf16[64,1,8,512]{3,2,1,0:T(8,128)(2,1)S(1)}, u32[]{:S(2)}, u32[]{:S(2)}) async-start(bf16[64,1,8,512]{3,2,1,0:T(8,128)(2,1)} %copy.27), calls=%async_computation.2 | async-start | bytes 1048576 | tf_op jit(solution)/shard_map/all_to_all | solution.py:128
  501.0 14.4 %all-to-all-start.3 = ((bf16[8,8,2048]{2,0,1:T(8,128)(2,1)}), bf16[8,8,2048]{2,0,1:T(8,128)(2,1)S(1)}, u32[]{:S(2)}, u32[]{:S(2)}) async-start(bf16[8,8,2048]{2,0,1:T(8,128)(2,1)} %copy.29), calls=%async_computation.3 | async-start | bytes 524288 | tf_op jit(solution)/shard_map/all_to_all | solution.py:141
Sparse Core Ops, SparseCore 0:
  10.1 38.5 all-gather.2
  75.5 33.0 all-gather.4
where the time goes:
time: 524 us; the launch traced here: 523 us
  blocking collectives  361 us (69%)
  waiting for transfers between devices  78.4 us (15%)
  starting transfers between devices  38.3 us (7%)
  between operations  14.9 us (3%)
  local copies, waits for them, and re-layouts  14 us (3%)
  matrix products  8.68 us (2%)
  other arithmetic  7.62 us (1%)
    psum x1, blocking collectives, shards(): adam_total = lax.psum(adam_vec, ('dp', 'mp'))  248 us
    psum x1, blocking collectives, shards(): total_norm = lax.psum(jnp.sum(momentum_new * momentum_new), ('dp', 'mp'))  100 us
    all_gather x1, waiting for transfers between devices, shards(): row_all = lax.all_gather(gradient, 'mp', axis=1, tiled=True)  39.1 us
    all_to_all x1, waiting for transfers between devices, shards(): lax.all_to_all(outgoing_back.reshape(owners, capacity, sub_rows, BLK), 'd...  27.7 us
    all_to_all x1, starting transfers between devices, shards(): lax.all_to_all(outgoing.reshape(owners, capacity, row_dev, BLK), 'dp', sp...  15.8 us
    psum x1, blocking collectives, shards(): precond_total = lax.psum(precond_sq, 'mp')  12.4 us
  transfers between devices with their start and end apart: 6, of which 4 were waited for; matrix products, arithmetic and copies ran while one was open for 3% of the time, Pallas kernels for 0%

commit v1 on v0

v1 whole, which is shorter than its diff:
```python
import math

import jax
import jax.numpy as jnp
from jax import lax
from jax.experimental import pallas as pl
from jax.experimental.pallas import tpu as pltpu
from jax.sharding import Mesh
from jax.sharding import PartitionSpec as P

BLK = 512
ROWS = 4096
COLS = 16384
YDIM = 4
AXES = ("z", "y", "m")

ZD, MD = 16, 8
OWNERS = ZD * YDIM
BANDS = ROWS // BLK
CB = COLS // BLK
ZZ = ZD // BANDS
SUB = 8
ROW_DEV = 64
LOCAL = COLS // MD
LB = LOCAL // BLK
LANES = 128
TB = BLK // LANES
SLOTS = 4
AREA = BLK * BLK
INV, BAND, OUT, IN, OTHER = 0, 64, 96, 104, 112
PLAN = 128

BF16, F32 = jnp.bfloat16, jnp.float32


def struct(*shape, dtype=BF16):
    return jax.ShapeDtypeStruct(shape, dtype)


def call(body, specs, outs, args, scratch=(), vmem=16, flops=0, name=None):
    space = {"v": pltpu.VMEM, "s": pltpu.SMEM, "a": pl.ANY}
    size = sum(o.size * o.dtype.itemsize for o in outs)
    size += sum(a.size * a.dtype.itemsize for a, k in zip(args, specs) if k == "v")
    return pl.pallas_call(
        body,
        out_shape=tuple(outs),
        in_specs=[pl.BlockSpec(memory_space=space[k]) for k in specs],
        out_specs=tuple(pl.BlockSpec(memory_space=pltpu.VMEM) for _ in outs),
        scratch_shapes=list(scratch),
        compiler_params=pltpu.CompilerParams(vmem_limit_bytes=vmem * 1024 * 1024),
        cost_estimate=pl.CostEstimate(flops=flops, bytes_accessed=size, transcendentals=0),
        name=name,
    )(*args)


def encode(value):
    value = jnp.broadcast_to(value, (SUB, LANES))
    row = lax.broadcasted_iota(jnp.int32, (SUB, LANES), 0)
    high = value.astype(BF16).astype(F32)
    mid = (value - high).astype(BF16).astype(F32)
    low = value - high - mid
    return jnp.where(
        row == 0, high, jnp.where(row == 1, mid, jnp.where(row == 2, low, 0.0))
    ).astype(BF16)


def decode(tile):
    return jnp.sum(tile.astype(F32), axis=0, keepdims=True)


def adam_body(index, grad, second, new_second, pay, sums):
    step = pl.program_id(0)

    @pl.when(step == 0)
    def _():
        sums[...] = jnp.zeros_like(sums)

    g = grad[...].astype(F32)
    ns = 0.999 * second[...] + 0.001 * g * g
    new_second[...] = ns
    d = g / (jnp.sqrt(ns) + 1e-08)
    q = d * d
    for c in range(LB * TB):
        cols = slice(c * LANES, (c + 1) * LANES)
        pay[2 * step, c] = g[:SUB, cols].astype(BF16)
        pay[2 * step + 1, c] = g[SUB:, cols].astype(BF16)
        sums[c // TB] += q[:SUB, cols] + q[SUB:, cols]

    @pl.when(step == ROW_DEV // 16 - 1)
    def _():
        lane = lax.broadcasted_iota(jnp.int32, (1, LANES), 1)
        first = index[0] * LB
        value = jnp.zeros((1, LANES), F32)
        for j in range(LB):
            value = jnp.where(lane == first + j, jnp.sum(sums[j]), value)
        tile = encode(value)
        for g in range(MD):
            pay[g, LB * TB] = tile


def adam(index, gradient, second_moment):
    rows = pl.BlockSpec((16, LOCAL), lambda i: (i, 0))
    pay = (MD, LB * TB + 1, SUB, LANES)
    return pl.pallas_call(
        adam_body,
        grid=(ROW_DEV // 16,),
        out_shape=(struct(ROW_DEV, LOCAL, dtype=F32), struct(*pay)),
        in_specs=[pl.BlockSpec(memory_space=pltpu.SMEM), rows, rows],
        out_specs=(rows, pl.BlockSpec(pay, lambda i: (0, 0, 0, 0))),
        scratch_shapes=[pltpu.VMEM((LB, SUB, LANES), F32)],
        compiler_params=pltpu.CompilerParams(vmem_limit_bytes=16 * 1024 * 1024),
        name="adam",
    )(index, gradient, second_moment)


def spread_body(plan, got, out):
    tile = got[0, LB * TB].astype(F32)
    for m in range(1, MD):
        tile += got[m, LB * TB].astype(F32)
    tile = tile.astype(BF16)
    for z in range(ZD):
        for y in range(YDIM):
            j = plan[INV + z * YDIM + y]
            out[z, y * TB : (y + 1) * TB] = got[j // LB, pl.ds(lax.rem(j, LB) * TB, TB)]
        out[z, YDIM * TB] = tile


def pack_body(plan, left, right, moment, after, *outs):
    for s in range(MD):
        t = plan[OUT + s]
        outs[s][0] = left[t]
        outs[s][1] = right[t]
        outs[s][2] = moment[t]


def plane_body(got, *refs):
    out = refs[-1]
    for b in range(BANDS):
        total = decode(got[b * ZZ, YDIM * TB])
        for k in range(1, ZZ):
            total += decode(got[b * ZZ + k, YDIM * TB])
        tile = encode(total)
        for y in range(YDIM):
            for k in range(ZZ):
                out[y * BANDS + b, k * TB : (k + 1) * TB] = got[
                    b * ZZ + k, y * TB : (y + 1) * TB
                ]
            out[y * BANDS + b, ZZ * TB] = tile


def block_body(plan, got, *refs):
    packed, (back, block, moment), (left, right, applied, prod) = (
        refs[:MD],
        refs[MD : MD + 3],
        refs[MD + 3 :],
    )
    me = plan[OTHER]
    for k in range(ZZ):
        for y in range(YDIM):
            for g in range(0, MD, 2):
                row = (k * YDIM + y) * ROW_DEV + g * SUB
                for c in range(TB):
                    pair = [got[y * MD + g + i, k * TB + c].astype(F32) for i in range(2)]
                    block[row : row + 16, c * LANES : (c + 1) * LANES] = jnp.concatenate(
                        pair, axis=0
                    ).astype(BF16)
    for s in range(MD):
        rows = pl.ds(pl.multiple_of(lax.rem(me - s + MD, MD) * ROW_DEV, ROW_DEV), ROW_DEV)
        left[rows, :] = packed[s][0]
        right[rows, :] = packed[s][1]
    adam = decode(got[0, ZZ * TB])
    for y in range(1, YDIM):
        adam += decode(got[y * MD, ZZ * TB])
    lane = lax.broadcasted_iota(jnp.int32, (1, LANES), 1)
    adam = jnp.sum(jnp.where(lane == plan[OTHER + 1], adam, 0.0), keepdims=True)
    applied[...] = jnp.dot(left[...], block[...], preferred_element_type=F32).astype(BF16)
    p = jnp.dot(applied[...], right[...], preferred_element_type=F32)
    prod[...] = p
    norm = jnp.sum(p * p, keepdims=True)
    graft = jnp.sqrt(adam / AREA) / jnp.sqrt(norm / AREA + 1e-06)
    total = jnp.zeros((ROW_DEV, BLK), F32)
    for s in range(MD):
        rows = pl.ds(pl.multiple_of(lax.rem(me - s + MD, MD) * ROW_DEV, ROW_DEV), ROW_DEV)
        f = 0.9 * packed[s][2].astype(F32) + graft * prod[rows, :]
        total += f * f
        moment[rows, :] = f.astype(BF16)
    square = jnp.sum(total, keepdims=True)
    square = jnp.where(plan[OTHER + 2] > 0, square, 0.0)
    tile = encode(jnp.broadcast_to(square, (1, LANES)))
    for y in range(YDIM):
        for g in range(0, MD, 2):
            for k in range(ZZ):
                row = (k * YDIM + y) * ROW_DEV + g * SUB
                for c in range(TB):
                    both = moment[row : row + 16, c * LANES : (c + 1) * LANES].astype(F32)
                    back[y * MD + g, k * TB + c] = both[:SUB].astype(BF16)
                    back[y * MD + g + 1, k * TB + c] = both[SUB:].astype(BF16)
            back[y * MD + g, ZZ * TB] = tile
            back[y * MD + g + 1, ZZ * TB] = tile


def stats_body(plan, block, moment, after, *refs):
    outs, (left, right) = refs[:MD], refs[MD:]
    me = plan[OTHER]
    left[...] = lax.dot_general(
        block[...], block[...], (((1,), (1,)), ((), ())), preferred_element_type=F32
    ).astype(BF16)
    right[...] = lax.dot_general(
        block[...], block[...], (((0,), (0,)), ((), ())), preferred_element_type=F32
    ).astype(BF16)
    for s in range(MD):
        rows = pl.ds(pl.multiple_of(lax.rem(me + s, MD) * ROW_DEV, ROW_DEV), ROW_DEV)
        outs[s][0] = left[rows, :]
        outs[s][1] = right[rows, :]
        outs[s][2] = moment[rows, :]


def unplane_body(got, out):
    total = decode(got[0, ZZ * TB])
    for i in range(1, YDIM * BANDS):
        total += decode(got[i, ZZ * TB])
    tile = encode(total)
    for b in range(BANDS):
        for k in range(ZZ):
            for y in range(YDIM):
                out[b * ZZ + k, y * TB : (y + 1) * TB] = got[
                    y * BANDS + b, k * TB : (k + 1) * TB
                ]
            out[b * ZZ + k, YDIM * TB] = tile


def place_body(plan, got, *refs):
    out = refs[-1]
    total = decode(got[0, YDIM * TB])
    for z in range(1, ZD):
        total += decode(got[z, YDIM * TB])
    clip = jnp.minimum(1.0, 0.5 * math.sqrt(ROWS * COLS) / jnp.sqrt(total))
    for m in range(MD):
        for i in range(LB):
            o = plan[BAND + m * LB + i]
            z, y = o // YDIM, lax.rem(o, YDIM)
            piece = got[z, pl.ds(y * TB, TB)].astype(F32)
            for c in range(TB):
                col = (i * TB + c) * LANES
                out[m, :, col : col + LANES] = (clip * piece[c]).astype(BF16)


def finish_body(plan, left, right, *refs):
    parts, (new_left, new_right, new_moment) = refs[:MD], refs[MD:]
    for s in range(MD):
        t = plan[IN + s]

        @pl.when(t >= 0)
        def _():
            new_left[t] = 0.95 * left[t] + 0.05 * parts[s][0].astype(F32)
            new_right[t] = 0.95 * right[t] + 0.05 * parts[s][1].astype(F32)
            new_moment[t] = parts[s][2]


def make_plan(owner_table):
    z = lax.axis_index("z")
    m = lax.axis_index("m")
    owner = z * YDIM + lax.axis_index("y")
    table = owner_table.reshape(BANDS, CB)
    band_owner = lax.dynamic_index_in_dim(table, z // ZZ, 0, keepdims=False)
    iota = lambda n: jnp.arange(n, dtype=jnp.int32)
    held = band_owner[None, :] == iota(OWNERS)[:, None]
    inverse = jnp.sum(jnp.where(held, iota(CB)[None, :], 0), axis=1)
    mine = table == owner
    has = jnp.sum(mine.astype(jnp.int32), axis=1)
    column = jnp.sum(jnp.where(mine, iota(CB)[None, :], 0), axis=1)
    slot = jnp.sum(jnp.where(iota(BANDS)[None, :] < iota(BANDS)[:, None], has[None, :], 0), axis=1)
    slot = jnp.minimum(slot, SLOTS - 1)
    pick = lambda at, values: jnp.sum(
        jnp.where(iota(BANDS)[None, :] == at[:, None], values[None, :], 0), axis=1
    )
    to = pick(lax.rem(m + iota(MD), MD), slot)
    source = pick(lax.rem(m - iota(MD) + MD, MD), jnp.where(has > 0, slot, -1))
    self = m[None]
    other = jnp.concatenate([self, pick(self, column), pick(self, has)])
    plan = jnp.concatenate([inverse, band_owner, to, source, other])
    return jnp.pad(plan, (0, PLAN - plan.shape[0])).astype(jnp.int32)


def shift(parts):
    moved = [parts[0]]
    for s in range(1, MD):
        moved.append(lax.ppermute(parts[s], "m", [(i, (i + s) % MD) for i in range(MD)]))
    return moved


def shards(
    gradient, second_moment, owner_table, left_stats, right_stats, left_root, right_root, momentum
):
    plan = make_plan(owner_table)
    slab = [struct(3, ROW_DEV, BLK)] * MD
    square = (BLK, BLK)

    index = lax.axis_index("m")[None]
    new_second, pay = adam(index, gradient, second_moment)
    got = lax.all_to_all(pay, "m", 0, 0, tiled=True)
    (pay,) = call(
        spread_body, "sv", [struct(ZD, YDIM * TB + 1, SUB, LANES)], [plan, got], name="spread"
    )
    packed = call(
        pack_body,
        "svvva",
        slab,
        [plan, left_root[0], right_root[0], momentum[0], pay],
        name="pack",
    )
    got = lax.all_to_all(pay, "z", 0, 0, tiled=True)
    packed = shift(packed)
    (pay,) = call(
        plane_body,
        "v" + "a" * (MD - 1),
        [struct(YDIM * BANDS, ZZ * TB + 1, SUB, LANES)],
        [got, *packed[1:]],
        name="plane",
    )
    got = lax.all_to_all(pay, ("y", "m"), 0, 0, tiled=True)
    back, block, moment = call(
        block_body,
        "sv" + "v" * MD,
        [struct(YDIM * MD, ZZ * TB + 1, SUB, LANES), struct(*square), struct(*square)],
        [plan, got, *packed],
        scratch=[pltpu.VMEM(square, BF16)] * 3 + [pltpu.VMEM(square, F32)],
        flops=4 * BLK**3,
        vmem=24,
        name="block",
    )
    got = lax.all_to_all(back, ("y", "m"), 0, 0, tiled=True)
    (pay,) = call(
        unplane_body, "v", [struct(ZD, YDIM * TB + 1, SUB, LANES)], [got], name="unplane"
    )
    results = call(
        stats_body,
        "svva",
        slab,
        [plan, block, moment, pay],
        scratch=[pltpu.VMEM(square, BF16)] * 2,
        flops=4 * BLK**3,
        name="stats",
    )
    got = lax.all_to_all(pay, "z", 0, 0, tiled=True)
    results = shift(results)
    (pay,) = call(
        place_body,
        "sv" + "a" * (MD - 1),
        [struct(MD, SUB, LOCAL)],
        [plan, got, *results[1:]],
        name="place",
    )
    update = lax.all_to_all(pay, "m", 0, 0, tiled=True).reshape(ROW_DEV, LOCAL)
    stat = struct(SLOTS, ROW_DEV, BLK, dtype=F32)
    new_left, new_right, new_moment = call(
        finish_body,
        "svv" + "v" * MD,
        [stat, stat, struct(SLOTS, ROW_DEV, BLK)],
        [plan, left_stats[0], right_stats[0], *results],
        name="finish",
    )
    return update, new_second, new_left[None], new_right[None], new_moment[None]


def solution(mesh):
    owners, groups = mesh.devices.shape
    inner = Mesh(mesh.devices.reshape(owners // YDIM, YDIM, groups), AXES)
    wide = P(("z", "y"), "m")
    stats = P(("z", "y"), None, "m", None)
    return jax.shard_map(
        shards,
        mesh=inner,
        in_specs=(wide, wide, P(), stats, stats, stats, stats, stats),
        out_specs=(wide, wide, stats, stats, stats),
        check_vma=False,
    )
```

time: 524 us -> 155 us (0.30)
  blocking collectives: 361 us -> 36.4 us
  waiting for transfers between devices: 78.4 us -> 26 us
  starting transfers between devices: 38.3 us -> 73.2 us
  between operations: 14.9 us -> 0.87 us
  Pallas kernels: 0 us -> 11.8 us
  local copies, waits for them, and re-layouts: 14 us -> 4.86 us
  matrix products: 8.68 us -> 0 us
  other arithmetic: 7.62 us -> 1.37 us
    psum x3 -> x0, blocking collectives: 361 us -> none  [the longest x1 248 us: shards(): adam_total = lax.psum(adam_vec, ('dp', 'mp'))]
    all_gather x2 -> x0, waiting for transfers between devices: 39.1 us -> none  [the longest x1 39.1 us: shards(): row_all = lax.all_gather(gradient, 'mp', axis=1, tiled=True)]
    all_to_all x0 -> x2, blocking collectives: none -> 36.4 us  [the longest x1 20.5 us: shards(): got = lax.all_to_all(pay, ('y', 'm'), 0, 0, tiled=True)]
    ppermute x0 -> x14, starting transfers between devices: none -> 34.8 us  [shift(): lax.ppermute(parts[s], 'm', [(i, (i + s) % MD) for i in range(MD)])]
    all_to_all x4, waiting for transfers between devices: 38 us -> 7.86 us  [the longest x1 4.7 us: shards(): update = lax.all_to_all(pay, 'm', 0, 0, tiled=True).reshape(ROW_DEV, LOCAL)]
    ppermute x0 -> x14, waiting for transfers between devices: none -> 18.1 us  [shift(): lax.ppermute(parts[s], 'm', [(i, (i + s) % MD) for i in range(MD)])]
    pallas_call x0 -> x9, Pallas kernels: none -> 11.8 us  [the longest x8 9.92 us: call(): pl.pallas_call(body, out_shape=tuple(outs), in_specs=[pl.BlockSpec(memory...]
    dot_general x6 -> x0, matrix products: 8.68 us -> none  [the longest x1 2.59 us: shards(): jnp.einsum('trc,tkc->trk', my_rows, full_blocks, preferred_element_type=j...]
  transfers between devices with their start and end apart: 6 -> 18, of which waited for: 4 -> 8; matrix products, arithmetic and copies ran while one was open for 3% -> 2% of each run, Pallas kernels for 0% -> 2%
where the time goes in v1:
time: 155 us; the launch traced here: 154 us
  starting transfers between devices  73.2 us (47%)
  blocking collectives  36.4 us (23%)
  waiting for transfers between devices  26 us (17%)
  Pallas kernels  11.8 us (8%)
  local copies, waits for them, and re-layouts  4.86 us (3%)
    ppermute x14, starting transfers between devices, shift(): lax.ppermute(parts[s], 'm', [(i, (i + s) % MD) for i in range(MD)])  34.8 us
    all_to_all x2, starting transfers between devices, shards(): got = lax.all_to_all(pay, 'z', 0, 0, tiled=True)  21.5 us
    all_to_all x1, blocking collectives, shards(): got = lax.all_to_all(pay, ('y', 'm'), 0, 0, tiled=True)  20.5 us
    ppermute x14, waiting for transfers between devices, shift(): lax.ppermute(parts[s], 'm', [(i, (i + s) % MD) for i in range(MD)])  18.1 us
    all_to_all x1, blocking collectives, shards(): got = lax.all_to_all(back, ('y', 'm'), 0, 0, tiled=True)  15.9 us
    all_to_all x1, starting transfers between devices, shards(): got = lax.all_to_all(pay, 'm', 0, 0, tiled=True)  10.2 us
    pallas_call x8, Pallas kernels, call(): pl.pallas_call(body, out_shape=tuple(outs), in_specs=[pl.BlockSpec(memory...  9.92 us
    all_to_all x1, starting transfers between devices, shards(): update = lax.all_to_all(pay, 'm', 0, 0, tiled=True).reshape(ROW_DEV, LOCAL)  6.69 us
  transfers between devices with their start and end apart: 18, of which 8 were waited for; matrix products, arithmetic and copies ran while one was open for 2% of the time, Pallas kernels for 2%

profile of v1, /device:TPU:1, one launch (start us, length us, event | category | flops | bytes accessed | tf_op | source)
XLA Modules:
  0.0 154.4 jit_solution(6442541268875769113)
XLA Ops:
  0.6 1.0 copy-done
  1.7 0.9 copy-done.6
  2.6 1.8 %adam.1 = (f32[64,2048]{1,0:T(8,128)}, bf16[8,17,8,128]{3,2,1,0:T(8,128)(2,1)}) custom-call(s32[1]{0:T(128)} %bitcast.1.index, bf16[64,2048]{1,0:T(8,128)(2,1)S(1)} %copy-done.6, f32[64,2048]{1,0:T(8,128)S(1)} %copy-done), custom_call_target="tpu_custom_call" | custom-call | tf_op jit(solution)/shard_map/adam/pallas_call | solution.py:104
  4.5 10.2 %all-to-all-start = ((bf16[8,17,8,128]{3,2,1,0:T(8,128)(2,1)}), bf16[8,17,8,128]{3,2,1,0:T(8,128)(2,1)S(1)}, u32[]{:S(2)}, u32[]{:S(2)}) async-start(bf16[8,17,8,128]{3,2,1,0:T(8,128)(2,1)} %get-tuple-element.29), calls=%async_computation | async-start | bytes 557056 | tf_op jit(solution)/shard_map/all_to_all | solution.py:301
  14.7 0.7 copy-done.9
  15.3 0.1 reshape.60
  15.4 0.1 select_reduce_fusion.1
  15.6 0.1 select_reduce_fusion.4
  15.7 0.1 select_reduce_fusion
  15.8 0.6 fusion.1
  16.4 0.2 select_reduce_fusion.2
  16.6 0.2 select_reduce_fusion.3
  16.8 1.4 concatenate.3
  18.2 3.2 %all-to-all-done.got = bf16[8,17,8,128]{3,2,1,0:T(8,128)(2,1)S(1)} async-done(((bf16[8,17,8,128]{3,2,1,0:T(8,128)(2,1)}), bf16[8,17,8,128]{3,2,1,0:T(8,128)(2,1)S(1)}, u32[]{:S(2)}, u32[]{:S(2)}) %all-to-all-start) | async-done | bytes 278560 | tf_op jit(solution)/shard_map/all_to_all | solution.py:301
  21.3 1.7 %spread.1.after = bf16[16,17,8,128]{3,2,1,0:T(8,128)(2,1)} custom-call(s32[128]{0:T(128)S(1)} %pad.4.plan, bf16[8,17,8,128]{3,2,1,0:T(8,128)(2,1)S(1)} %all-to-all-done.got), custom_call_target="tpu_custom_call" | custom-call | bytes 835584 | tf_op jit(solution)/shard_map/spread/pallas_call | solution.py:44
  23.1 10.6 %all-to-all-start.1 = ((bf16[16,17,8,128]{3,2,1,0:T(8,128)(2,1)}), bf16[16,17,8,128]{3,2,1,0:T(8,128)(2,1)S(1)}, u32[]{:S(2)}, u32[]{:S(2)}) async-start(bf16[16,17,8,128]{3,2,1,0:T(8,128)(2,1)} %spread.1.after), calls=%async_computation.1 | async-start | bytes 1114112 | tf_op jit(solution)/shard_map/all_to_all | solution.py:312
  33.7 0.0 copy-done.3
  33.7 0.0 copy-done.4
  33.7 0.0 copy-done.5
  33.7 0.7 pack.1
  34.4 1.5 collective-permute-start
  35.9 1.9 %collective-permute-start.1 = (bf16[3,64,512]{2,1,0:T(8,128)(2,1)S(1)}, bf16[3,64,512]{2,1,0:T(8,128)(2,1)S(1)}, u32[]{:S(2)}, u32[]{:S(2)}) collective-permute-start(bf16[3,64,512]{2,1,0:T(8,128)(2,1)S(1)} %get-tuple-element.31), channel_id=1, source_target_pairs={{0,2},{1,3},{2,4},{3,5},{4,6},{5,7},{6,0},{7,1},{8,10},{9,11},{10,... | collective-permute-start | bytes 589832 | tf_op jit(solution)/shard_map/ppermute | solution.py:288
  37.8 4.0 %collective-permute-start.2 = (bf16[3,64,512]{2,1,0:T(8,128)(2,1)S(1)}, bf16[3,64,512]{2,1,0:T(8,128)(2,1)S(1)}, u32[]{:S(2)}, u32[]{:S(2)}) collective-permute-start(bf16[3,64,512]{2,1,0:T(8,128)(2,1)S(1)} %get-tuple-element.32), channel_id=1, source_target_pairs={{0,3},{1,4},{2,5},{3,6},{4,7},{5,0},{6,1},{7,2},{8,11},{9,12},{10,... | collective-permute-start | bytes 589832 | tf_op jit(solution)/shard_map/ppermute | solution.py:288
  41.8 3.4 %collective-permute-start.3 = (bf16[3,64,512]{2,1,0:T(8,128)(2,1)S(1)}, bf16[3,64,512]{2,1,0:T(8,128)(2,1)S(1)}, u32[]{:S(2)}, u32[]{:S(2)}) collective-permute-start(bf16[3,64,512]{2,1,0:T(8,128)(2,1)S(1)} %get-tuple-element.33), channel_id=1, source_target_pairs={{0,4},{1,5},{2,6},{3,7},{4,0},{5,1},{6,2},{7,3},{8,12},{9,13},{10,... | collective-permute-start | bytes 589832 | tf_op jit(solution)/shard_map/ppermute | solution.py:288
  45.3 4.5 %collective-permute-start.4 = (bf16[3,64,512]{2,1,0:T(8,128)(2,1)S(1)}, bf16[3,64,512]{2,1,0:T(8,128)(2,1)S(1)}, u32[]{:S(2)}, u32[]{:S(2)}) collective-permute-start(bf16[3,64,512]{2,1,0:T(8,128)(2,1)S(1)} %get-tuple-element.34), channel_id=1, source_target_pairs={{0,5},{1,6},{2,7},{3,0},{4,1},{5,2},{6,3},{7,4},{8,13},{9,14},{10,... | collective-permute-start | bytes 589832 | tf_op jit(solution)/shard_map/ppermute | solution.py:288
  49.8 0.0 collective-permute-done.refs_0_.refs_1_
  49.8 1.9 %collective-permute-start.5 = (bf16[3,64,512]{2,1,0:T(8,128)(2,1)S(1)}, bf16[3,64,512]{2,1,0:T(8,128)(2,1)S(1)}, u32[]{:S(2)}, u32[]{:S(2)}) collective-permute-start(bf16[3,64,512]{2,1,0:T(8,128)(2,1)S(1)} %get-tuple-element.35), channel_id=1, source_target_pairs={{0,6},{1,7},{2,0},{3,1},{4,2},{5,3},{6,4},{7,5},{8,14},{9,15},{10,... | collective-permute-start | bytes 589832 | tf_op jit(solution)/shard_map/ppermute | solution.py:288
  51.7 0.0 collective-permute-done.1.refs_1_.refs_2_
  51.7 0.4 collective-permute-start.6
  52.1 4.3 %collective-permute-done.2.refs_2_.refs_3_ = bf16[3,64,512]{2,1,0:T(8,128)(2,1)S(1)} collective-permute-done((bf16[3,64,512]{2,1,0:T(8,128)(2,1)S(1)}, bf16[3,64,512]{2,1,0:T(8,128)(2,1)S(1)}, u32[]{:S(2)}, u32[]{:S(2)}) %collective-permute-start.2) | collective-permute-done | bytes 196640 | tf_op jit(solution)/shard_map/ppermute | solution.py:288
  56.5 0.0 collective-permute-done.3.refs_3_.refs_4_
  56.5 0.0 collective-permute-done.4.refs_4_.refs_5_
  56.5 2.8 %collective-permute-done.5.refs_5_.refs_6_ = bf16[3,64,512]{2,1,0:T(8,128)(2,1)S(1)} collective-permute-done((bf16[3,64,512]{2,1,0:T(8,128)(2,1)S(1)}, bf16[3,64,512]{2,1,0:T(8,128)(2,1)S(1)}, u32[]{:S(2)}, u32[]{:S(2)}) %collective-permute-start.5) | collective-permute-done | bytes 196640 | tf_op jit(solution)/shard_map/ppermute | solution.py:288
  59.3 1.9 %collective-permute-done.6.refs_6_.refs_7_ = bf16[3,64,512]{2,1,0:T(8,128)(2,1)S(1)} collective-permute-done((bf16[3,64,512]{2,1,0:T(8,128)(2,1)S(1)}, bf16[3,64,512]{2,1,0:T(8,128)(2,1)S(1)}, u32[]{:S(2)}, u32[]{:S(2)}) %collective-permute-start.6) | collective-permute-done | bytes 196640 | tf_op jit(solution)/shard_map/ppermute | solution.py:288
  61.2 0.0 all-to-all-done.1.got
  61.2 0.1 plane.1
  61.3 20.5 %all_to_all.30.got = bf16[32,9,8,128]{3,2,1,0:T(8,128)(2,1)S(1)} all-to-all(bf16[32,9,8,128]{3,2,1,0:T(8,128)(2,1)S(1)} %plane.1), channel_id=1, replica_groups=mesh['z'=16,'y'=4,'m'=8] {'y','m'}, dimensions={0} | all-to-all | bytes 1179648 | tf_op jit(solution)/shard_map/all_to_all | solution.py:321
  81.8 2.0 %block.1 = (bf16[32,9,8,128]{3,2,1,0:T(8,128)(2,1)S(1)}, bf16[512,512]{1,0:T(8,128)(2,1)S(1)}, bf16[512,512]{1,0:T(8,128)(2,1)S(1)}) custom-call(s32[128]{0:T(128)S(1)} %pad.4.plan, bf16[32,9,8,128]{3,2,1,0:T(8,128)(2,1)S(1)} %all_to_all.30.got, bf16[3,64,512]{2,1,0:T(8,128)(2,1)S(1)} %get-tuple-element.37.refs_0_, ...), custom_call_target="tpu_custom_call" | custom-call | flops 536870912 | bytes 3801088 | tf_op jit(solution)/shard_map/block/pallas_call | solution.py:44
  83.8 0.0 copy-start.7
  83.9 15.9 %all_to_all.31.got = bf16[32,9,8,128]{3,2,1,0:T(8,128)(2,1)S(1)} all-to-all(bf16[32,9,8,128]{3,2,1,0:T(8,128)(2,1)S(1)} %get-tuple-element.38), channel_id=1, replica_groups=mesh['z'=16,'y'=4,'m'=8] {'y','m'}, dimensions={0} | all-to-all | bytes 1179648 | tf_op jit(solution)/shard_map/all_to_all | solution.py:332
  99.7 0.9 unplane.1.after
  100.6 10.9 %all-to-all-start.4 = ((bf16[16,17,8,128]{3,2,1,0:T(8,128)(2,1)}), bf16[16,17,8,128]{3,2,1,0:T(8,128)(2,1)S(1)}, u32[]{:S(2)}, u32[]{:S(2)}) async-start(bf16[16,17,8,128]{3,2,1,0:T(8,128)(2,1)} %unplane.1.after), calls=%async_computation.4 | async-start | bytes 1114112 | tf_op jit(solution)/shard_map/all_to_all | solution.py:345
  111.5 1.3 stats.1
  112.8 0.9 collective-permute-start.7
  113.7 2.2 %collective-permute-start.8 = (bf16[3,64,512]{2,1,0:T(8,128)(2,1)S(1)}, bf16[3,64,512]{2,1,0:T(8,128)(2,1)S(1)}, u32[]{:S(2)}, u32[]{:S(2)}) collective-permute-start(bf16[3,64,512]{2,1,0:T(8,128)(2,1)S(1)} %get-tuple-element.42), channel_id=1, source_target_pairs={{0,2},{1,3},{2,4},{3,5},{4,6},{5,7},{6,0},{7,1},{8,10},{9,11},{10,... | collective-permute-start | bytes 589832 | tf_op jit(solution)/shard_map/ppermute | solution.py:288
  116.0 3.9 %collective-permute-start.9 = (bf16[3,64,512]{2,1,0:T(8,128)(2,1)S(1)}, bf16[3,64,512]{2,1,0:T(8,128)(2,1)S(1)}, u32[]{:S(2)}, u32[]{:S(2)}) collective-permute-start(bf16[3,64,512]{2,1,0:T(8,128)(2,1)S(1)} %get-tuple-element.43), channel_id=1, source_target_pairs={{0,3},{1,4},{2,5},{3,6},{4,7},{5,0},{6,1},{7,2},{8,11},{9,12},{10,... | collective-permute-start | bytes 589832 | tf_op jit(solution)/shard_map/ppermute | solution.py:288
  119.8 3.3 %collective-permute-start.10 = (bf16[3,64,512]{2,1,0:T(8,128)(2,1)S(1)}, bf16[3,64,512]{2,1,0:T(8,128)(2,1)S(1)}, u32[]{:S(2)}, u32[]{:S(2)}) collective-permute-start(bf16[3,64,512]{2,1,0:T(8,128)(2,1)S(1)} %get-tuple-element.44), channel_id=1, source_target_pairs={{0,4},{1,5},{2,6},{3,7},{4,0},{5,1},{6,2},{7,3},{8,12},{9,13},{10,... | collective-permute-start | bytes 589832 | tf_op jit(solution)/shard_map/ppermute | solution.py:288
  123.1 4.5 %collective-permute-start.11 = (bf16[3,64,512]{2,1,0:T(8,128)(2,1)S(1)}, bf16[3,64,512]{2,1,0:T(8,128)(2,1)S(1)}, u32[]{:S(2)}, u32[]{:S(2)}) collective-permute-start(bf16[3,64,512]{2,1,0:T(8,128)(2,1)S(1)} %get-tuple-element.45), channel_id=1, source_target_pairs={{0,5},{1,6},{2,7},{3,0},{4,1},{5,2},{6,3},{7,4},{8,13},{9,14},{10,... | collective-permute-start | bytes 589832 | tf_op jit(solution)/shard_map/ppermute | solution.py:288
  127.7 0.0 collective-permute-done.7.refs_0_.refs_1_
  127.7 1.9 %collective-permute-start.12 = (bf16[3,64,512]{2,1,0:T(8,128)(2,1)S(1)}, bf16[3,64,512]{2,1,0:T(8,128)(2,1)S(1)}, u32[]{:S(2)}, u32[]{:S(2)}) collective-permute-start(bf16[3,64,512]{2,1,0:T(8,128)(2,1)S(1)} %get-tuple-element.46), channel_id=1, source_target_pairs={{0,6},{1,7},{2,0},{3,1},{4,2},{5,3},{6,4},{7,5},{8,14},{9,15},{10,... | collective-permute-start | bytes 589832 | tf_op jit(solution)/shard_map/ppermute | solution.py:288
  129.6 0.0 collective-permute-done.8.refs_1_.refs_2_
  129.6 0.4 collective-permute-start.13
  130.0 4.3 %collective-permute-done.9.refs_2_.refs_3_ = bf16[3,64,512]{2,1,0:T(8,128)(2,1)S(1)} collective-permute-done((bf16[3,64,512]{2,1,0:T(8,128)(2,1)S(1)}, bf16[3,64,512]{2,1,0:T(8,128)(2,1)S(1)}, u32[]{:S(2)}, u32[]{:S(2)}) %collective-permute-start.9) | collective-permute-done | bytes 196640 | tf_op jit(solution)/shard_map/ppermute | solution.py:288
  134.3 0.0 collective-permute-done.10.refs_3_.refs_4_
  134.3 0.0 collective-permute-done.11.refs_4_.refs_5_
  134.3 2.9 %collective-permute-done.12.refs_5_.refs_6_ = bf16[3,64,512]{2,1,0:T(8,128)(2,1)S(1)} collective-permute-done((bf16[3,64,512]{2,1,0:T(8,128)(2,1)S(1)}, bf16[3,64,512]{2,1,0:T(8,128)(2,1)S(1)}, u32[]{:S(2)}, u32[]{:S(2)}) %collective-permute-start.12) | collective-permute-done | bytes 196640 | tf_op jit(solution)/shard_map/ppermute | solution.py:288
  137.2 1.8 %collective-permute-done.13.refs_6_.refs_7_ = bf16[3,64,512]{2,1,0:T(8,128)(2,1)S(1)} collective-permute-done((bf16[3,64,512]{2,1,0:T(8,128)(2,1)S(1)}, bf16[3,64,512]{2,1,0:T(8,128)(2,1)S(1)}, u32[]{:S(2)}, u32[]{:S(2)}) %collective-permute-start.13) | collective-permute-done | bytes 196640 | tf_op jit(solution)/shard_map/ppermute | solution.py:288
  139.0 0.0 all-to-all-done.4.got
  139.0 1.4 place.1
  140.5 6.7 %all-to-all-start.5 = ((bf16[8,8,2048]{2,1,0:T(8,128)(2,1)}), bf16[8,8,2048]{2,1,0:T(8,128)(2,1)S(1)}, u32[]{:S(2)}, u32[]{:S(2)}) async-start(bf16[8,8,2048]{2,1,0:T(8,128)(2,1)} %place.1), calls=%async_computation.5 | async-start | bytes 524288 | tf_op jit(solution)/shard_map/all_to_all | solution.py:354
  147.2 0.0 copy-done.1
  147.2 1.8 %finish.1 = (f32[4,64,512]{2,1,0:T(8,128)}, f32[4,64,512]{2,1,0:T(8,128)}, bf16[4,64,512]{2,1,0:T(8,128)(2,1)}) custom-call(s32[128]{0:T(128)S(1)} %pad.4.plan, f32[4,64,512]{2,1,0:T(8,128)S(1)} %bitcast.14, f32[4,64,512]{2,1,0:T(8,128)S(1)} %bitcast.15, bf16[3,64,512]{2,1,0:T(8,128)(2,1)S(1)} %get-tuple-element.49.refs_0_, ...), custom_call_target="tpu_custom_call" | custom-call | bytes 3932160 | tf_op jit(solution)/shard_map/finish/pallas_call | solution.py:44
  149.0 4.7 %all-to-all-done.5 = bf16[8,8,2048]{2,1,0:T(8,128)(2,1)S(1)} async-done(((bf16[8,8,2048]{2,1,0:T(8,128)(2,1)}), bf16[8,8,2048]{2,1,0:T(8,128)(2,1)S(1)}, u32[]{:S(2)}, u32[]{:S(2)}) %all-to-all-start.5) | async-done | bytes 262176 | tf_op jit(solution)/shard_map/all_to_all | solution.py:354
  153.7 0.7 copy.14
  (15 shorter events, 0.0 us)
Async XLA Ops:
  0.6 1.0 copy-start
  1.7 0.9 copy-start.6
  4.5 16.9 %all-to-all-start = ((bf16[8,17,8,128]{3,2,1,0:T(8,128)(2,1)}), bf16[8,17,8,128]{3,2,1,0:T(8,128)(2,1)S(1)}, u32[]{:S(2)}, u32[]{:S(2)}) async-start(bf16[8,17,8,128]{3,2,1,0:T(8,128)(2,1)} %get-tuple-element.29), calls=%async_computation | async-start | bytes 557056 | tf_op jit(solution)/shard_map/all_to_all | solution.py:301
  14.7 0.7 copy-start.9
  23.1 10.6 %copy-start.3 = (bf16[1,4,64,512]{3,2,1,0:T(8,128)(2,1)S(1)}, bf16[1,4,64,512]{3,2,1,0:T(8,128)(2,1)}, u32[]{:S(2)}) copy-start(bf16[1,4,64,512]{3,2,1,0:T(8,128)(2,1)} %param.13) | copy-start | bytes 786436
  23.1 10.7 %copy-start.4 = (bf16[1,4,64,512]{3,2,1,0:T(8,128)(2,1)S(1)}, bf16[1,4,64,512]{3,2,1,0:T(8,128)(2,1)}, u32[]{:S(2)}) copy-start(bf16[1,4,64,512]{3,2,1,0:T(8,128)(2,1)} %param.14) | copy-start | bytes 786436
  23.1 10.7 %copy-start.5 = (bf16[1,4,64,512]{3,2,1,0:T(8,128)(2,1)S(1)}, bf16[1,4,64,512]{3,2,1,0:T(8,128)(2,1)}, u32[]{:S(2)}) copy-start(bf16[1,4,64,512]{3,2,1,0:T(8,128)(2,1)} %param.15) | copy-start | bytes 786436
  23.1 38.1 %all-to-all-start.1 = ((bf16[16,17,8,128]{3,2,1,0:T(8,128)(2,1)}), bf16[16,17,8,128]{3,2,1,0:T(8,128)(2,1)S(1)}, u32[]{:S(2)}, u32[]{:S(2)}) async-start(bf16[16,17,8,128]{3,2,1,0:T(8,128)(2,1)} %spread.1.after), calls=%async_computation.1 | async-start | bytes 1114112 | tf_op jit(solution)/shard_map/all_to_all | solution.py:312
  34.4 15.4 %collective-permute-start = (bf16[3,64,512]{2,1,0:T(8,128)(2,1)S(1)}, bf16[3,64,512]{2,1,0:T(8,128)(2,1)S(1)}, u32[]{:S(2)}, u32[]{:S(2)}) collective-permute-start(bf16[3,64,512]{2,1,0:T(8,128)(2,1)S(1)} %get-tuple-element.30), channel_id=1, source_target_pairs={{0,1},{1,2},{2,3},{3,4},{4,5},{5,6},{6,7},{7,0},{8,9},{9,10},{10,1... | collective-permute-start | bytes 589832 | tf_op jit(solution)/shard_map/ppermute | solution.py:288
  35.9 15.8 %collective-permute-start.1 = (bf16[3,64,512]{2,1,0:T(8,128)(2,1)S(1)}, bf16[3,64,512]{2,1,0:T(8,128)(2,1)S(1)}, u32[]{:S(2)}, u32[]{:S(2)}) collective-permute-start(bf16[3,64,512]{2,1,0:T(8,128)(2,1)S(1)} %get-tuple-element.31), channel_id=1, source_target_pairs={{0,2},{1,3},{2,4},{3,5},{4,6},{5,7},{6,0},{7,1},{8,10},{9,11},{10,... | collective-permute-start | bytes 589832 | tf_op jit(solution)/shard_map/ppermute | solution.py:288
  37.8 18.6 %collective-permute-start.2 = (bf16[3,64,512]{2,1,0:T(8,128)(2,1)S(1)}, bf16[3,64,512]{2,1,0:T(8,128)(2,1)S(1)}, u32[]{:S(2)}, u32[]{:S(2)}) collective-permute-start(bf16[3,64,512]{2,1,0:T(8,128)(2,1)S(1)} %get-tuple-element.32), channel_id=1, source_target_pairs={{0,3},{1,4},{2,5},{3,6},{4,7},{5,0},{6,1},{7,2},{8,11},{9,12},{10,... | collective-permute-start | bytes 589832 | tf_op jit(solution)/shard_map/ppermute | solution.py:288
  41.8 14.6 %collective-permute-start.3 = (bf16[3,64,512]{2,1,0:T(8,128)(2,1)S(1)}, bf16[3,64,512]{2,1,0:T(8,128)(2,1)S(1)}, u32[]{:S(2)}, u32[]{:S(2)}) collective-permute-start(bf16[3,64,512]{2,1,0:T(8,128)(2,1)S(1)} %get-tuple-element.33), channel_id=1, source_target_pairs={{0,4},{1,5},{2,6},{3,7},{4,0},{5,1},{6,2},{7,3},{8,12},{9,13},{10,... | collective-permute-start | bytes 589832 | tf_op jit(solution)/shard_map/ppermute | solution.py:288
  45.3 11.2 %collective-permute-start.4 = (bf16[3,64,512]{2,1,0:T(8,128)(2,1)S(1)}, bf16[3,64,512]{2,1,0:T(8,128)(2,1)S(1)}, u32[]{:S(2)}, u32[]{:S(2)}) collective-permute-start(bf16[3,64,512]{2,1,0:T(8,128)(2,1)S(1)} %get-tuple-element.34), channel_id=1, source_target_pairs={{0,5},{1,6},{2,7},{3,0},{4,1},{5,2},{6,3},{7,4},{8,13},{9,14},{10,... | collective-permute-start | bytes 589832 | tf_op jit(solution)/shard_map/ppermute | solution.py:288
  49.8 9.5 %collective-permute-start.5 = (bf16[3,64,512]{2,1,0:T(8,128)(2,1)S(1)}, bf16[3,64,512]{2,1,0:T(8,128)(2,1)S(1)}, u32[]{:S(2)}, u32[]{:S(2)}) collective-permute-start(bf16[3,64,512]{2,1,0:T(8,128)(2,1)S(1)} %get-tuple-element.35), channel_id=1, source_target_pairs={{0,6},{1,7},{2,0},{3,1},{4,2},{5,3},{6,4},{7,5},{8,14},{9,15},{10,... | collective-permute-start | bytes 589832 | tf_op jit(solution)/shard_map/ppermute | solution.py:288
  51.7 9.5 %collective-permute-start.6 = (bf16[3,64,512]{2,1,0:T(8,128)(2,1)S(1)}, bf16[3,64,512]{2,1,0:T(8,128)(2,1)S(1)}, u32[]{:S(2)}, u32[]{:S(2)}) collective-permute-start(bf16[3,64,512]{2,1,0:T(8,128)(2,1)S(1)} %get-tuple-element.36), channel_id=1, source_target_pairs={{0,7},{1,0},{2,1},{3,2},{4,3},{5,4},{6,5},{7,6},{8,15},{9,8},{10,9... | collective-permute-start | bytes 589832 | tf_op jit(solution)/shard_map/ppermute | solution.py:288
  83.8 15.9 %copy-start.7 = (bf16[512,512]{1,0:T(8,128)(2,1)}, bf16[512,512]{1,0:T(8,128)(2,1)S(1)}, u32[]{:S(2)}) copy-start(bf16[512,512]{1,0:T(8,128)(2,1)S(1)} %get-tuple-element.40.moment) | copy-start | bytes 1572868
  100.6 10.9 %copy-start.8 = (bf16[512,512]{1,0:T(8,128)(2,1)S(1)}, bf16[512,512]{1,0:T(8,128)(2,1)}, u32[]{:S(2)}) copy-start(bf16[512,512]{1,0:T(8,128)(2,1)} %copy-done.7) | copy-start | bytes 1572868
  100.6 38.4 %all-to-all-start.4 = ((bf16[16,17,8,128]{3,2,1,0:T(8,128)(2,1)}), bf16[16,17,8,128]{3,2,1,0:T(8,128)(2,1)S(1)}, u32[]{:S(2)}, u32[]{:S(2)}) async-start(bf16[16,17,8,128]{3,2,1,0:T(8,128)(2,1)} %unplane.1.after), calls=%async_computation.4 | async-start | bytes 1114112 | tf_op jit(solution)/shard_map/all_to_all | solution.py:345
  112.8 14.8 %collective-permute-start.7 = (bf16[3,64,512]{2,1,0:T(8,128)(2,1)S(1)}, bf16[3,64,512]{2,1,0:T(8,128)(2,1)S(1)}, u32[]{:S(2)}, u32[]{:S(2)}) collective-permute-start(bf16[3,64,512]{2,1,0:T(8,128)(2,1)S(1)} %get-tuple-element.41), channel_id=1, source_target_pairs={{0,1},{1,2},{2,3},{3,4},{4,5},{5,6},{6,7},{7,0},{8,9},{9,10},{10,1... | collective-permute-start | bytes 589832 | tf_op jit(solution)/shard_map/ppermute | solution.py:288
  113.7 15.9 %collective-permute-start.8 = (bf16[3,64,512]{2,1,0:T(8,128)(2,1)S(1)}, bf16[3,64,512]{2,1,0:T(8,128)(2,1)S(1)}, u32[]{:S(2)}, u32[]{:S(2)}) collective-permute-start(bf16[3,64,512]{2,1,0:T(8,128)(2,1)S(1)} %get-tuple-element.42), channel_id=1, source_target_pairs={{0,2},{1,3},{2,4},{3,5},{4,6},{5,7},{6,0},{7,1},{8,10},{9,11},{10,... | collective-permute-start | bytes 589832 | tf_op jit(solution)/shard_map/ppermute | solution.py:288
  116.0 18.3 %collective-permute-start.9 = (bf16[3,64,512]{2,1,0:T(8,128)(2,1)S(1)}, bf16[3,64,512]{2,1,0:T(8,128)(2,1)S(1)}, u32[]{:S(2)}, u32[]{:S(2)}) collective-permute-start(bf16[3,64,512]{2,1,0:T(8,128)(2,1)S(1)} %get-tuple-element.43), channel_id=1, source_target_pairs={{0,3},{1,4},{2,5},{3,6},{4,7},{5,0},{6,1},{7,2},{8,11},{9,12},{10,... | collective-permute-start | bytes 589832 | tf_op jit(solution)/shard_map/ppermute | solution.py:288
  119.8 14.5 %collective-permute-start.10 = (bf16[3,64,512]{2,1,0:T(8,128)(2,1)S(1)}, bf16[3,64,512]{2,1,0:T(8,128)(2,1)S(1)}, u32[]{:S(2)}, u32[]{:S(2)}) collective-permute-start(bf16[3,64,512]{2,1,0:T(8,128)(2,1)S(1)} %get-tuple-element.44), channel_id=1, source_target_pairs={{0,4},{1,5},{2,6},{3,7},{4,0},{5,1},{6,2},{7,3},{8,12},{9,13},{10,... | collective-permute-start | bytes 589832 | tf_op jit(solution)/shard_map/ppermute | solution.py:288
  123.1 11.2 %collective-permute-start.11 = (bf16[3,64,512]{2,1,0:T(8,128)(2,1)S(1)}, bf16[3,64,512]{2,1,0:T(8,128)(2,1)S(1)}, u32[]{:S(2)}, u32[]{:S(2)}) collective-permute-start(bf16[3,64,512]{2,1,0:T(8,128)(2,1)S(1)} %get-tuple-element.45), channel_id=1, source_target_pairs={{0,5},{1,6},{2,7},{3,0},{4,1},{5,2},{6,3},{7,4},{8,13},{9,14},{10,... | collective-permute-start | bytes 589832 | tf_op jit(solution)/shard_map/ppermute | solution.py:288
  127.7 9.5 %collective-permute-start.12 = (bf16[3,64,512]{2,1,0:T(8,128)(2,1)S(1)}, bf16[3,64,512]{2,1,0:T(8,128)(2,1)S(1)}, u32[]{:S(2)}, u32[]{:S(2)}) collective-permute-start(bf16[3,64,512]{2,1,0:T(8,128)(2,1)S(1)} %get-tuple-element.46), channel_id=1, source_target_pairs={{0,6},{1,7},{2,0},{3,1},{4,2},{5,3},{6,4},{7,5},{8,14},{9,15},{10,... | collective-permute-start | bytes 589832 | tf_op jit(solution)/shard_map/ppermute | solution.py:288
  129.6 9.4 %collective-permute-start.13 = (bf16[3,64,512]{2,1,0:T(8,128)(2,1)S(1)}, bf16[3,64,512]{2,1,0:T(8,128)(2,1)S(1)}, u32[]{:S(2)}, u32[]{:S(2)}) collective-permute-start(bf16[3,64,512]{2,1,0:T(8,128)(2,1)S(1)} %get-tuple-element.47), channel_id=1, source_target_pairs={{0,7},{1,0},{2,1},{3,2},{4,3},{5,4},{6,5},{7,6},{8,15},{9,8},{10,9... | collective-permute-start | bytes 589832 | tf_op jit(solution)/shard_map/ppermute | solution.py:288
  139.0 8.1 %copy-start.2 = (f32[1,4,64,512]{3,2,1,0:T(8,128)S(1)}, f32[1,4,64,512]{3,2,1,0:T(8,128)}, u32[]{:S(2)}) copy-start(f32[1,4,64,512]{3,2,1,0:T(8,128)} %param.12) | copy-start | bytes 1572868
  140.5 6.7 %copy-start.1 = (f32[1,4,64,512]{3,2,1,0:T(8,128)S(1)}, f32[1,4,64,512]{3,2,1,0:T(8,128)}, u32[]{:S(2)}) copy-start(f32[1,4,64,512]{3,2,1,0:T(8,128)} %param.11) | copy-start | bytes 1572868
  140.5 13.2 %all-to-all-start.5 = ((bf16[8,8,2048]{2,1,0:T(8,128)(2,1)}), bf16[8,8,2048]{2,1,0:T(8,128)(2,1)S(1)}, u32[]{:S(2)}, u32[]{:S(2)}) async-start(bf16[8,8,2048]{2,1,0:T(8,128)(2,1)} %place.1), calls=%async_computation.5 | async-start | bytes 524288 | tf_op jit(solution)/shard_map/all_to_all | solution.py:354

commit v2 on v1

v2 whole, which is shorter than its diff:
```python
import math

import jax
import jax.numpy as jnp
from jax import lax
from jax.experimental import pallas as pl
from jax.experimental.pallas import tpu as pltpu
from jax.sharding import Mesh
from jax.sharding import PartitionSpec as P

BLK = 512
ROWS = 4096
COLS = 16384
YDIM = 4
AXES = ("z", "y", "m")

ZD, MD = 16, 8
OWNERS = ZD * YDIM
BANDS = ROWS // BLK
CB = COLS // BLK
ZZ = ZD // BANDS
SUB = 8
ROW_DEV = 64
LOCAL = COLS // MD
LB = LOCAL // BLK
LANES = 128
TB = BLK // LANES
SLOTS = 4
AREA = BLK * BLK
SHIFTS = (4, 5, 3, 6, 2, 7, 1)
CHUNKS = 4

BF16, F32 = jnp.bfloat16, jnp.float32


def struct(*shape, dtype=BF16):
    return jax.ShapeDtypeStruct(shape, dtype)


def hold_shapes(hold):
    return [struct(*a.shape, dtype=a.dtype) for a in hold]


def call(body, specs, outs, args, scratch=(), vmem=16, flops=0, name=None, stream=False, hold=()):
    space = {"v": pltpu.VMEM, "s": pltpu.SMEM, "a": pl.ANY}
    size = sum(o.size * o.dtype.itemsize for o in outs)
    size += sum(a.size * a.dtype.itemsize for a, k in zip(args, specs) if k == "v")
    first = len(args)
    specs, args, outs = specs + "a" * len(hold), [*args, *hold], [*outs, *hold_shapes(hold)]
    scratch = list(scratch)
    if stream:
        scratch += [pltpu.VMEM(outs[0].shape, outs[0].dtype), pltpu.SemaphoreType.DMA((CHUNKS + 1,))]
    return pl.pallas_call(
        body,
        out_shape=tuple(outs),
        in_specs=[pl.BlockSpec(memory_space=space[k]) for k in specs],
        out_specs=tuple(pl.BlockSpec(memory_space=space["a" if stream else "v"]) for _ in outs),
        input_output_aliases={first + i: 1 + i for i in range(len(hold))},
        scratch_shapes=scratch,
        compiler_params=pltpu.CompilerParams(vmem_limit_bytes=vmem * 1024 * 1024),
        cost_estimate=pl.CostEstimate(flops=flops, bytes_accessed=size, transcendentals=0),
        name=name,
    )(*args)


def stream(fill, out, buffer, sems):
    size = buffer.shape[0] // CHUNKS
    copies = []
    for i in range(CHUNKS):
        for row in range(i * size, (i + 1) * size):
            fill(row)
        rows = pl.ds(i * size, size)
        copy = pltpu.make_async_copy(buffer.at[rows], out.at[rows], sems.at[i])
        copy.start()
        copies.append(copy)
    for copy in copies:
        copy.wait()


def join(first, second):
    return jnp.concatenate([first, second], axis=0)


def encode(value):
    value = jnp.broadcast_to(value, (SUB, LANES))
    row = lax.broadcasted_iota(jnp.int32, (SUB, LANES), 0)
    high = value.astype(BF16).astype(F32)
    mid = (value - high).astype(BF16).astype(F32)
    low = value - high - mid
    return jnp.where(
        row == 0, high, jnp.where(row == 1, mid, jnp.where(row == 2, low, 0.0))
    ).astype(BF16)


def decode(tile):
    return jnp.sum(tile.astype(F32), axis=0, keepdims=True)


def adam_body(index, grad, second, new_second, tile, sums):
    step = pl.program_id(0)

    @pl.when(step == 0)
    def _():
        sums[...] = jnp.zeros_like(sums)

    g = grad[...].astype(F32)
    ns = 0.999 * second[...] + 0.001 * g * g
    new_second[...] = ns
    d = g / (jnp.sqrt(ns) + 1e-08)
    q = d * d
    for c in range(LB * TB):
        cols = slice(c * LANES, (c + 1) * LANES)
        sums[c // TB] += q[:SUB, cols] + q[SUB:, cols]

    @pl.when(step == ROW_DEV // 16 - 1)
    def _():
        lane = lax.broadcasted_iota(jnp.int32, (1, LANES), 1)
        first = index[0] * LB
        value = jnp.zeros((1, LANES), F32)
        for j in range(LB):
            value = jnp.where(lane == first + j, jnp.sum(sums[j]), value)
        tile[...] = encode(value)


def adam(index, gradient, second_moment):
    rows = pl.BlockSpec((16, LOCAL), lambda i: (i, 0))
    return pl.pallas_call(
        adam_body,
        grid=(ROW_DEV // 16,),
        out_shape=(struct(ROW_DEV, LOCAL, dtype=F32), struct(SUB, LANES)),
        in_specs=[pl.BlockSpec(memory_space=pltpu.SMEM), rows, rows],
        out_specs=(rows, pl.BlockSpec((SUB, LANES), lambda i: (0, 0))),
        scratch_shapes=[pltpu.VMEM((LB, SUB, LANES), F32)],
        compiler_params=pltpu.CompilerParams(vmem_limit_bytes=16 * 1024 * 1024),
        name="adam",
    )(index, gradient, second_moment)


def spread_body(inverse, tile, got, out, buffer, sems):
    def fill(z):
        for y in range(YDIM):
            j = inverse[z * YDIM + y]
            lanes = pl.ds(pl.multiple_of((j & (LB - 1)) * BLK, BLK), BLK)
            piece = got[j >> 2, :, lanes]
            for c in range(TB):
                buffer[z, y * TB + c] = piece[:, c * LANES : (c + 1) * LANES]
        buffer[z, YDIM * TB] = tile[...]

    stream(fill, out, buffer, sems)


def pack_body(to, left, right, moment, after, *outs):
    for s in range(MD):
        t = to[s]
        outs[s][0] = left[t]
        outs[s][1] = right[t]
        outs[s][2] = moment[t]


def plane_body(got, *refs):
    out, buffer, sems = refs[-3:]
    tiles = []
    for b in range(BANDS):
        total = decode(got[b * ZZ, YDIM * TB])
        for k in range(1, ZZ):
            total += decode(got[b * ZZ + k, YDIM * TB])
        tiles.append(encode(total))

    def fill(row):
        y, b = divmod(row, BANDS)
        for k in range(ZZ):
            buffer[row, k * TB : (k + 1) * TB] = got[b * ZZ + k, y * TB : (y + 1) * TB]
        buffer[row, ZZ * TB] = tiles[b]

    stream(fill, out, buffer, sems)


def roots_body(other, *refs):
    parts, outs = refs[:MD], refs[MD:]
    for s in range(MD):
        source = lax.rem(other[0] - s + MD, MD)
        rows = pl.ds(pl.multiple_of(source * ROW_DEV, ROW_DEV), ROW_DEV)
        for i in range(3):
            outs[i][rows, :] = parts[s][i]


def assemble(got, block):
    for k in range(ZZ):
        for y in range(YDIM):
            for g in range(0, MD, 2):
                row = (k * YDIM + y) * ROW_DEV + g * SUB
                for c in range(TB):
                    block[row : row + 16, c * LANES : (c + 1) * LANES] = join(
                        got[y * MD + g, k * TB + c], got[y * MD + g + 1, k * TB + c]
                    )


def block_body(masks, got, left, right, old, out, block, applied, prod, buffer, sems):
    assemble(got, block)
    adam = got[0, ZZ * TB].astype(F32)
    for i in range(1, YDIM * MD):
        adam += got[i, ZZ * TB].astype(F32)
    adam = jnp.sum(jnp.where(masks[:1, :] > 0, decode(adam), 0.0), keepdims=True)
    applied[...] = jnp.dot(left[...], block[...], preferred_element_type=F32).astype(BF16)
    p = jnp.dot(applied[...], right[...], preferred_element_type=F32)
    prod[...] = p
    norm = jnp.sum(p * p, keepdims=True)
    graft = jnp.sqrt(adam / AREA) / jnp.sqrt(norm / AREA + 1e-06)
    total = jnp.zeros((16, BLK), F32)
    copies = []
    for y in range(YDIM):
        for g in range(0, MD, 2):
            for k in range(ZZ):
                row = (k * YDIM + y) * ROW_DEV + g * SUB
                rows = slice(row, row + 16)
                f = 0.9 * old[rows, :].astype(F32) + graft * prod[rows, :]
                total += f * f
                for c in range(TB):
                    cols = slice(c * LANES, (c + 1) * LANES)
                    buffer[y * MD + g, k * TB + c] = f[:SUB, cols].astype(BF16)
                    buffer[y * MD + g + 1, k * TB + c] = f[SUB:, cols].astype(BF16)
        if y < YDIM - 1:
            part = (pl.ds(y * MD, MD), pl.ds(0, ZZ * TB))
            copies.append(pltpu.make_async_copy(buffer.at[part], out.at[part], sems.at[y]))
            copies[-1].start()
    square = jnp.broadcast_to(jnp.sum(total, keepdims=True), (1, LANES))
    tile = encode(jnp.where(masks[1:2, :] > 0, square, 0.0))
    for slot in range(YDIM * MD):
        buffer[slot, ZZ * TB] = tile
    last = (YDIM - 1) * MD
    rest = pl.ds(last, MD)
    copies.append(pltpu.make_async_copy(buffer.at[rest], out.at[rest], sems.at[YDIM - 1]))
    part = (pl.ds(0, last), pl.ds(ZZ * TB, 1))
    copies.append(pltpu.make_async_copy(buffer.at[part], out.at[part], sems.at[YDIM]))
    for copy in copies[-2:]:
        copy.start()
    for copy in copies:
        copy.wait()


def stats_body(other, got, moment, *refs):
    outs, (block, left, right) = refs[:MD], refs[MD:]
    assemble(got, block)
    left[...] = lax.dot_general(
        block[...], block[...], (((1,), (1,)), ((), ())), preferred_element_type=F32
    ).astype(BF16)
    right[...] = lax.dot_general(
        block[...], block[...], (((0,), (0,)), ((), ())), preferred_element_type=F32
    ).astype(BF16)
    for s, out in enumerate(outs):
        to = lax.rem(other[0] + s, MD)
        rows = pl.ds(pl.multiple_of(to * ROW_DEV, ROW_DEV), ROW_DEV)
        out[0] = left[rows, :]
        out[1] = right[rows, :]
        first, tiles = lax.rem(to, YDIM) * MD, (to // YDIM) * TB
        for g in range(0, MD, 2):
            for c in range(TB):
                out[2, g * SUB : g * SUB + 16, c * LANES : (c + 1) * LANES] = join(
                    moment[first + g, tiles + c], moment[first + g + 1, tiles + c]
                )


def unplane_body(got, *refs):
    out, (buffer, sems) = refs[MD - 1], refs[-2:]
    total = got[0, ZZ * TB].astype(F32)
    for i in range(1, YDIM * BANDS):
        total += got[i, ZZ * TB].astype(F32)
    tile = encode(decode(total))

    def fill(z):
        b, k = divmod(z, ZZ)
        for y in range(YDIM):
            buffer[z, y * TB : (y + 1) * TB] = got[y * BANDS + b, k * TB : (k + 1) * TB]
        buffer[z, YDIM * TB] = tile

    stream(fill, out, buffer, sems)


def place_body(band_owner, got, *refs):
    out, buffer, sems = refs[-3:]

    def fill(m):
        for i in range(LB):
            o = band_owner[m * LB + i]
            z, first = o >> 2, (o & (YDIM - 1)) * TB
            for c in range(TB):
                col = (i * TB + c) * LANES
                buffer[m, :, col : col + LANES] = got[z, first + c]

    stream(fill, out, buffer, sems)


def norm_body(got, out):
    total = got[0, YDIM * TB].astype(F32)
    for z in range(1, ZD):
        total += got[z, YDIM * TB].astype(F32)
    out[...] = jnp.minimum(1.0, 0.5 * math.sqrt(ROWS * COLS) / jnp.sqrt(decode(total)))


def finish_body(source, left, right, *refs):
    parts, (new_left, new_right, new_moment) = refs[:MD], refs[MD:]
    for s in range(MD):
        t = source[s]

        @pl.when(t >= 0)
        def _():
            new_left[t] = 0.95 * left[t] + 0.05 * parts[s][0].astype(F32)
            new_right[t] = 0.95 * right[t] + 0.05 * parts[s][1].astype(F32)
            new_moment[t] = parts[s][2]


def make_plan(owner_table):
    z = lax.axis_index("z")
    m = lax.axis_index("m")
    owner = z * YDIM + lax.axis_index("y")
    table = owner_table.reshape(BANDS, CB)
    band_owner = lax.dynamic_index_in_dim(table, z // ZZ, 0, keepdims=False)
    iota = lambda n: jnp.arange(n, dtype=jnp.int32)
    held = band_owner[None, :] == iota(OWNERS)[:, None]
    inverse = jnp.sum(jnp.where(held, iota(CB)[None, :], 0), axis=1)
    mine = table == owner
    has = jnp.sum(mine.astype(jnp.int32), axis=1)
    column = jnp.sum(jnp.where(mine, iota(CB)[None, :], 0), axis=1)
    slot = jnp.sum(jnp.where(iota(BANDS)[None, :] < iota(BANDS)[:, None], has[None, :], 0), axis=1)
    slot = jnp.minimum(slot, SLOTS - 1)
    pick = lambda at, values: jnp.sum(
        jnp.where(iota(BANDS)[None, :] == at[:, None], values[None, :], 0), axis=1
    )
    to = pick(lax.rem(m + iota(MD), MD), slot)
    source = pick(lax.rem(m - iota(MD) + MD, MD), jnp.where(has > 0, slot, -1))
    self = m[None]
    lane = jnp.where(iota(LANES) == pick(self, column), 1.0, 0.0)
    held = jnp.broadcast_to(pick(self, has), (LANES,)).astype(F32)
    masks = jnp.pad(jnp.stack([lane, held]), ((0, SUB - 2), (0, 0)))
    return inverse, band_owner, to, source, self, masks


def shift(part, s):
    return lax.ppermute(part, "m", [(i, (i + s) % MD) for i in range(MD)])


def shards(
    gradient, second_moment, owner_table, left_stats, right_stats, left_root, right_root, momentum
):
    inverse, band_owner, to, source, other, masks = make_plan(owner_table)
    square = (BLK, BLK)

    got = lax.all_to_all(gradient.reshape(MD, SUB, LOCAL), "m", 0, 0, tiled=True)
    new_second, tile = adam(lax.axis_index("m")[None], gradient, second_moment)
    (pay,) = call(
        spread_body,
        "svv",
        [struct(ZD, YDIM * TB + 1, SUB, LANES)],
        [inverse, tile, got],
        name="spread",
        stream=True,
    )
    packed = call(
        pack_body,
        "svvva",
        [struct(3, ROW_DEV, BLK)] * MD,
        [to, left_root[0], right_root[0], momentum[0], pay],
        name="pack",
    )
    got = lax.all_to_all(pay, "z", 0, 0, tiled=True)
    moved = {0: packed[0]}
    for s in SHIFTS:
        moved[s] = shift(packed[s], s)
    (pay,) = call(
        plane_body,
        "v" + "a" * len(SHIFTS),
        [struct(YDIM * BANDS, ZZ * TB + 1, SUB, LANES)],
        [got, *(moved[s] for s in SHIFTS)],
        name="plane",
        stream=True,
    )
    got = lax.all_to_all(pay, ("y", "m"), 0, 0, tiled=True)
    left, right, old = call(
        roots_body,
        "s" + "v" * MD,
        [struct(*square)] * 3,
        [other, *(moved[s] for s in range(MD))],
        name="roots",
    )
    whole = got
    (back,) = call(
        block_body,
        "vvvvv",
        [struct(YDIM * MD, ZZ * TB + 1, SUB, LANES)],
        [masks, whole, left, right, old],
        scratch=[
            pltpu.VMEM(square, BF16),
            pltpu.VMEM(square, BF16),
            pltpu.VMEM(square, F32),
        ],
        flops=4 * BLK**3,
        vmem=24,
        name="block",
        stream=True,
    )
    got = lax.all_to_all(back, ("y", "m"), 0, 0, tiled=True)
    parts = call(
        stats_body,
        "svv",
        [struct(3, ROW_DEV, BLK)] * MD,
        [other, whole, back],
        scratch=[pltpu.VMEM(square, BF16)] * 3,
        flops=4 * BLK**3,
        name="stats",
    )
    pay, *held = call(
        unplane_body,
        "v",
        [struct(ZD, YDIM * TB + 1, SUB, LANES)],
        [got],
        name="unplane",
        stream=True,
        hold=parts[1:],
    )
    got = lax.all_to_all(pay, "z", 0, 0, tiled=True)
    results = {0: parts[0]}
    for s in SHIFTS:
        results[s] = shift(held[s - 1], s)
    (pay,) = call(
        place_body,
        "sv" + "a" * len(SHIFTS),
        [struct(MD, SUB, LOCAL)],
        [band_owner, got, *(results[s] for s in SHIFTS)],
        name="place",
        stream=True,
    )
    (clip,) = call(norm_body, "v", [struct(1, LANES, dtype=F32)], [got], name="norm")
    placed = lax.all_to_all(pay, "m", 0, 0, tiled=True).reshape(ROW_DEV, LOCAL)
    update = (clip[0, 0] * placed.astype(F32)).astype(BF16)
    stat = struct(SLOTS, ROW_DEV, BLK, dtype=F32)
    new_left, new_right, new_moment = call(
        finish_body,
        "svv" + "v" * MD,
        [stat, stat, struct(SLOTS, ROW_DEV, BLK)],
        [source, left_stats[0], right_stats[0], *(results[s] for s in range(MD))],
        name="finish",
    )
    return update, new_second, new_left[None], new_right[None], new_moment[None]


def solution(mesh):
    owners, groups = mesh.devices.shape
    inner = Mesh(mesh.devices.reshape(owners // YDIM, YDIM, groups), AXES)
    wide = P(("z", "y"), "m")
    stats = P(("z", "y"), None, "m", None)
    return jax.shard_map(
        shards,
        mesh=inner,
        in_specs=(wide, wide, P(), stats, stats, stats, stats, stats),
        out_specs=(wide, wide, stats, stats, stats),
        check_vma=False,
    )
```

time: 155 us -> 151 us (0.974)
  blocking collectives: 36.4 us -> 0 us
  starting transfers between devices: 73.2 us -> 90.2 us
  waiting for transfers between devices: 26 us -> 39.1 us
    all_to_all x2 -> x0, blocking collectives: 36.4 us -> none  [the longest x1 20.5 us: shards(): got = lax.all_to_all(pay, ('y', 'm'), 0, 0, tiled=True)]
    all_to_all x2 -> x4, waiting for transfers between devices: 7.86 us -> 27.6 us  [the longest x1 10.4 us: shards(): got = lax.all_to_all(back, ('y', 'm'), 0, 0, tiled=True)]
    all_to_all x2 -> x4, starting transfers between devices: 16.9 us -> 35.9 us  [the longest x1 11.2 us: shards(): got = lax.all_to_all(pay, ('y', 'm'), 0, 0, tiled=True)]
    ppermute x14, waiting for transfers between devices: 18.1 us -> 10.2 us  [shift(): return lax.ppermute(part, 'm', [(i, (i + s) % MD) for i in range(MD)])]
    all_to_all x2, starting transfers between devices: 21.5 us -> 19.5 us  [shards(): got = lax.all_to_all(pay, 'z', 0, 0, tiled=True)]
    pallas_call x8 -> x10, Pallas kernels: 9.92 us -> 11.4 us  [call(): pl.pallas_call(body, out_shape=tuple(outs), in_specs=[pl.BlockSpec(memory...]
    unnamed x21 -> x20, local copies, waits for them, and re-layouts: 3.39 us -> 3.35 us
  transfers between devices with their start and end apart: 18 -> 20, of which waited for: 8 -> 12; matrix products, arithmetic and copies ran while one was open for 2% -> 1% of each run, Pallas kernels for 2% -> 4%
where the time goes in v2:
time: 151 us; the launch traced here: 150 us
  starting transfers between devices  90.2 us (60%)
  waiting for transfers between devices  39.1 us (26%)
  Pallas kernels  13.1 us (9%)
  local copies, waits for them, and re-layouts  3.43 us (2%)
  other arithmetic  2.82 us (2%)
  between operations  1.6 us (1%)
    ppermute x14, starting transfers between devices, shift(): return lax.ppermute(part, 'm', [(i, (i + s) % MD) for i in range(MD)])  34.7 us
    all_to_all x2, starting transfers between devices, shards(): got = lax.all_to_all(pay, 'z', 0, 0, tiled=True)  19.5 us
    pallas_call x10, Pallas kernels, call(): pl.pallas_call(body, out_shape=tuple(outs), in_specs=[pl.BlockSpec(memory...  11.4 us
    all_to_all x1, starting transfers between devices, shards(): got = lax.all_to_all(pay, ('y', 'm'), 0, 0, tiled=True)  11.2 us
    all_to_all x1, waiting for transfers between devices, shards(): got = lax.all_to_all(back, ('y', 'm'), 0, 0, tiled=True)  10.4 us
    all_to_all x1, starting transfers between devices, shards(): lax.all_to_all(gradient.reshape(MD, SUB, LOCAL), 'm', 0, 0, tiled=True)  10.3 us
    all_to_all x1, starting transfers between devices, shards(): placed = lax.all_to_all(pay, 'm', 0, 0, tiled=True).reshape(ROW_DEV, LOCAL)  10.3 us
    ppermute x14, waiting for transfers between devices, shift(): return lax.ppermute(part, 'm', [(i, (i + s) % MD) for i in range(MD)])  10.2 us
  transfers between devices with their start and end apart: 20, of which 12 were waited for; matrix products, arithmetic and copies ran while one was open for 1% of the time, Pallas kernels for 4%

profile of v2, /device:TPU:1, one launch (start us, length us, event | category | flops | bytes accessed | tf_op | source)
XLA Modules:
  0.0 150.2 jit_solution(5859052352855443181)
XLA Ops:
  0.6 10.3 %all-to-all-start = ((bf16[8,8,2048]{2,1,0:T(8,128)(2,1)}), bf16[8,8,2048]{2,1,0:T(8,128)(2,1)S(1)}, u32[]{:S(2)}, u32[]{:S(2)}) async-start(bf16[8,8,2048]{2,1,0:T(8,128)(2,1)} %bitcast.16), calls=%async_computation | async-start | bytes 524288 | tf_op jit(solution)/shard_map/all_to_all | solution.py:348
  11.0 0.7 copy-done.9
  11.7 0.1 reshape.77
  11.7 1.0 copy-done.1
  12.8 1.7 %adam.1 = (f32[64,2048]{1,0:T(8,128)}, bf16[8,128]{1,0:T(8,128)(2,1)S(1)}) custom-call(s32[1]{0:T(128)} %bitcast.1.index.other, bf16[64,2048]{1,0:T(8,128)(2,1)S(1)} %copy-done, f32[64,2048]{1,0:T(8,128)S(1)} %copy-done.1), custom_call_target="tpu_custom_call" | custom-call | tf_op jit(solution)/shard_map/adam/pallas_call | solution.py:127
  14.5 0.1 select_reduce_fusion.inverse
  14.6 2.9 %all-to-all-done.got = bf16[8,8,2048]{2,1,0:T(8,128)(2,1)S(1)} async-done(((bf16[8,8,2048]{2,1,0:T(8,128)(2,1)}), bf16[8,8,2048]{2,1,0:T(8,128)(2,1)S(1)}, u32[]{:S(2)}, u32[]{:S(2)}) %all-to-all-start) | async-done | bytes 262176 | tf_op jit(solution)/shard_map/all_to_all | solution.py:348
  17.5 1.4 spread.1.after
  18.9 0.0 copy-start.4
  19.0 0.0 copy-start.5
  19.0 0.0 copy-start.6
  19.0 10.6 %all-to-all-start.1 = ((bf16[16,17,8,128]{3,2,1,0:T(8,128)(2,1)}), bf16[16,17,8,128]{3,2,1,0:T(8,128)(2,1)S(1)}, u32[]{:S(2)}, u32[]{:S(2)}) async-start(bf16[16,17,8,128]{3,2,1,0:T(8,128)(2,1)} %spread.1.after), calls=%async_computation.1 | async-start | bytes 1114112 | tf_op jit(solution)/shard_map/all_to_all | solution.py:365
  29.7 0.1 convert_reduce_fusion
  29.8 0.1 select_reduce_fusion.3
  29.9 0.6 compare_select_fusion.4
  30.6 0.2 select_reduce_fusion.2.to
  30.8 0.7 pack.1
  31.4 0.0 copy-start.7
  31.4 0.7 copy-done.7
  32.1 2.4 %collective-permute-start = (bf16[3,64,512]{2,1,0:T(8,128)(2,1)S(1)}, bf16[3,64,512]{2,1,0:T(8,128)(2,1)S(1)}, u32[]{:S(2)}, u32[]{:S(2)}) collective-permute-start(bf16[3,64,512]{2,1,0:T(8,128)(2,1)S(1)} %get-tuple-element.38), channel_id=1, source_target_pairs={{0,4},{1,5},{2,6},{3,7},{4,0},{5,1},{6,2},{7,3},{8,12},{9,13},{10,... | collective-permute-start | bytes 589832 | tf_op jit(solution)/shard_map/ppermute | solution.py:339
  34.6 5.5 %collective-permute-start.1 = (bf16[3,64,512]{2,1,0:T(8,128)(2,1)S(1)}, bf16[3,64,512]{2,1,0:T(8,128)(2,1)S(1)}, u32[]{:S(2)}, u32[]{:S(2)}) collective-permute-start(bf16[3,64,512]{2,1,0:T(8,128)(2,1)S(1)} %get-tuple-element.39), channel_id=1, source_target_pairs={{0,5},{1,6},{2,7},{3,0},{4,1},{5,2},{6,3},{7,4},{8,13},{9,14},{10,... | collective-permute-start | bytes 589832 | tf_op jit(solution)/shard_map/ppermute | solution.py:339
  40.1 2.2 %collective-permute-start.2 = (bf16[3,64,512]{2,1,0:T(8,128)(2,1)S(1)}, bf16[3,64,512]{2,1,0:T(8,128)(2,1)S(1)}, u32[]{:S(2)}, u32[]{:S(2)}) collective-permute-start(bf16[3,64,512]{2,1,0:T(8,128)(2,1)S(1)} %get-tuple-element.40), channel_id=1, source_target_pairs={{0,3},{1,4},{2,5},{3,6},{4,7},{5,0},{6,1},{7,2},{8,11},{9,12},{10,... | collective-permute-start | bytes 589832 | tf_op jit(solution)/shard_map/ppermute | solution.py:339
  42.3 3.4 %collective-permute-start.3 = (bf16[3,64,512]{2,1,0:T(8,128)(2,1)S(1)}, bf16[3,64,512]{2,1,0:T(8,128)(2,1)S(1)}, u32[]{:S(2)}, u32[]{:S(2)}) collective-permute-start(bf16[3,64,512]{2,1,0:T(8,128)(2,1)S(1)} %get-tuple-element.41), channel_id=1, source_target_pairs={{0,6},{1,7},{2,0},{3,1},{4,2},{5,3},{6,4},{7,5},{8,14},{9,15},{10,... | collective-permute-start | bytes 589832 | tf_op jit(solution)/shard_map/ppermute | solution.py:339
  45.7 1.9 %collective-permute-start.4 = (bf16[3,64,512]{2,1,0:T(8,128)(2,1)S(1)}, bf16[3,64,512]{2,1,0:T(8,128)(2,1)S(1)}, u32[]{:S(2)}, u32[]{:S(2)}) collective-permute-start(bf16[3,64,512]{2,1,0:T(8,128)(2,1)S(1)} %get-tuple-element.42), channel_id=1, source_target_pairs={{0,2},{1,3},{2,4},{3,5},{4,6},{5,7},{6,0},{7,1},{8,10},{9,11},{10,... | collective-permute-start | bytes 589832 | tf_op jit(solution)/shard_map/ppermute | solution.py:339
  47.6 0.0 collective-permute-done.refs_0_.refs_4_
  47.6 1.6 %collective-permute-start.5 = (bf16[3,64,512]{2,1,0:T(8,128)(2,1)S(1)}, bf16[3,64,512]{2,1,0:T(8,128)(2,1)S(1)}, u32[]{:S(2)}, u32[]{:S(2)}) collective-permute-start(bf16[3,64,512]{2,1,0:T(8,128)(2,1)S(1)} %get-tuple-element.43), channel_id=1, source_target_pairs={{0,7},{1,0},{2,1},{3,2},{4,3},{5,4},{6,5},{7,6},{8,15},{9,8},{10,9... | collective-permute-start | bytes 589832 | tf_op jit(solution)/shard_map/ppermute | solution.py:339
  49.2 0.0 collective-permute-done.1.refs_1_.refs_5_
  49.2 0.2 collective-permute-start.6
  49.4 0.6 collective-permute-done.2.refs_2_.refs_3_
  50.0 2.0 %collective-permute-done.3.refs_3_.refs_6_ = bf16[3,64,512]{2,1,0:T(8,128)(2,1)S(1)} collective-permute-done((bf16[3,64,512]{2,1,0:T(8,128)(2,1)S(1)}, bf16[3,64,512]{2,1,0:T(8,128)(2,1)S(1)}, u32[]{:S(2)}, u32[]{:S(2)}) %collective-permute-start.3) | collective-permute-done | bytes 196640 | tf_op jit(solution)/shard_map/ppermute | solution.py:339
  52.0 1.6 %collective-permute-done.4.refs_4_.refs_2_ = bf16[3,64,512]{2,1,0:T(8,128)(2,1)S(1)} collective-permute-done((bf16[3,64,512]{2,1,0:T(8,128)(2,1)S(1)}, bf16[3,64,512]{2,1,0:T(8,128)(2,1)S(1)}, u32[]{:S(2)}, u32[]{:S(2)}) %collective-permute-start.4) | collective-permute-done | bytes 196640 | tf_op jit(solution)/shard_map/ppermute | solution.py:339
  53.6 0.8 collective-permute-done.6.refs_6_.refs_1_
  54.4 0.9 plane.1
  55.4 11.2 %all-to-all-start.2 = ((bf16[32,9,8,128]{3,2,1,0:T(8,128)(2,1)}), bf16[32,9,8,128]{3,2,1,0:T(8,128)(2,1)S(1)}, u32[]{:S(2)}, u32[]{:S(2)}) async-start(bf16[32,9,8,128]{3,2,1,0:T(8,128)(2,1)} %plane.1), calls=%async_computation.2 | async-start | bytes 1179648 | tf_op jit(solution)/shard_map/all_to_all | solution.py:377
  67.2 0.7 compare_select_fusion.5
  67.9 0.0 copy-start.8
  67.9 0.9 copy-done.8
  68.8 0.1 roots.1
  69.0 9.9 %all-to-all-done.2.got = bf16[32,9,8,128]{3,2,1,0:T(8,128)(2,1)S(1)} async-done(((bf16[32,9,8,128]{3,2,1,0:T(8,128)(2,1)}), bf16[32,9,8,128]{3,2,1,0:T(8,128)(2,1)S(1)}, u32[]{:S(2)}, u32[]{:S(2)}) %all-to-all-start.2) | async-done | bytes 589856 | tf_op jit(solution)/shard_map/all_to_all | solution.py:377
  78.8 2.2 %block.1.moment = bf16[32,9,8,128]{3,2,1,0:T(8,128)(2,1)} custom-call(f32[8,128]{1,0:T(8,128)S(1)} %pad_select_fusion.masks, bf16[32,9,8,128]{3,2,1,0:T(8,128)(2,1)S(1)} %all-to-all-done.2.got, bf16[512,512]{1,0:T(8,128)(2,1)S(1)} %get-tuple-element.46.left, bf16[512,512]{1,0:T(8,128)(2,1)S(1)} %get-tuple-element.47.right, ...), custom_call_target="tpu_custom_call" | custom-call | flops 536870912 | bytes 2756608 | tf_op jit(solution)/shard_map/block/pallas_call | solution.py:53
  81.0 4.1 %all-to-all-start.3 = ((bf16[32,9,8,128]{3,2,1,0:T(8,128)(2,1)}), bf16[32,9,8,128]{3,2,1,0:T(8,128)(2,1)S(1)}, u32[]{:S(2)}, u32[]{:S(2)}) async-start(bf16[32,9,8,128]{3,2,1,0:T(8,128)(2,1)} %block.1.moment), calls=%async_computation.3 | async-start | bytes 1179648 | tf_op jit(solution)/shard_map/all_to_all | solution.py:401
  85.1 2.0 %stats.1 = (bf16[3,64,512]{2,1,0:T(8,128)(2,1)S(1)}, bf16[3,64,512]{2,1,0:T(8,128)(2,1)S(1)}, bf16[3,64,512]{2,1,0:T(8,128)(2,1)S(1)}, bf16[3,64,512]{2,1,0:T(8,...) custom-call(s32[1]{0:T(128)} %bitcast.1.index.other, ...), custom_call_target="tpu_custom_call" | custom-call | flops 536870912 | bytes 2752512 | tf_op jit(solution)/shard_map/stats/pallas_call | solution.py:53
  87.1 10.4 %all-to-all-done.3.got = bf16[32,9,8,128]{3,2,1,0:T(8,128)(2,1)S(1)} async-done(((bf16[32,9,8,128]{3,2,1,0:T(8,128)(2,1)}), bf16[32,9,8,128]{3,2,1,0:T(8,128)(2,1)S(1)}, u32[]{:S(2)}, u32[]{:S(2)}) %all-to-all-start.3) | async-done | bytes 589856 | tf_op jit(solution)/shard_map/all_to_all | solution.py:401
  97.5 0.9 unplane.1
  98.4 8.9 %all-to-all-start.4 = ((bf16[16,17,8,128]{3,2,1,0:T(8,128)(2,1)}), bf16[16,17,8,128]{3,2,1,0:T(8,128)(2,1)S(1)}, u32[]{:S(2)}, u32[]{:S(2)}) async-start(bf16[16,17,8,128]{3,2,1,0:T(8,128)(2,1)} %get-tuple-element.56), calls=%async_computation.4 | async-start | bytes 1114112 | tf_op jit(solution)/shard_map/all_to_all | solution.py:420
  107.3 2.7 %collective-permute-start.7 = (bf16[3,64,512]{2,1,0:T(8,128)(2,1)S(1)}, bf16[3,64,512]{2,1,0:T(8,128)(2,1)S(1)}, u32[]{:S(2)}, u32[]{:S(2)}) collective-permute-start(bf16[3,64,512]{2,1,0:T(8,128)(2,1)S(1)} %get-tuple-element.57), channel_id=1, source_target_pairs={{0,4},{1,5},{2,6},{3,7},{4,0},{5,1},{6,2},{7,3},{8,12},{9,13},{10,... | collective-permute-start | bytes 589832 | tf_op jit(solution)/shard_map/ppermute | solution.py:339
  110.0 4.6 %collective-permute-start.8 = (bf16[3,64,512]{2,1,0:T(8,128)(2,1)S(1)}, bf16[3,64,512]{2,1,0:T(8,128)(2,1)S(1)}, u32[]{:S(2)}, u32[]{:S(2)}) collective-permute-start(bf16[3,64,512]{2,1,0:T(8,128)(2,1)S(1)} %get-tuple-element.58), channel_id=1, source_target_pairs={{0,5},{1,6},{2,7},{3,0},{4,1},{5,2},{6,3},{7,4},{8,13},{9,14},{10,... | collective-permute-start | bytes 589832 | tf_op jit(solution)/shard_map/ppermute | solution.py:339
  114.7 2.4 %collective-permute-start.9 = (bf16[3,64,512]{2,1,0:T(8,128)(2,1)S(1)}, bf16[3,64,512]{2,1,0:T(8,128)(2,1)S(1)}, u32[]{:S(2)}, u32[]{:S(2)}) collective-permute-start(bf16[3,64,512]{2,1,0:T(8,128)(2,1)S(1)} %get-tuple-element.59), channel_id=1, source_target_pairs={{0,3},{1,4},{2,5},{3,6},{4,7},{5,0},{6,1},{7,2},{8,11},{9,12},{10,... | collective-permute-start | bytes 589832 | tf_op jit(solution)/shard_map/ppermute | solution.py:339
  117.1 4.0 %collective-permute-start.10 = (bf16[3,64,512]{2,1,0:T(8,128)(2,1)S(1)}, bf16[3,64,512]{2,1,0:T(8,128)(2,1)S(1)}, u32[]{:S(2)}, u32[]{:S(2)}) collective-permute-start(bf16[3,64,512]{2,1,0:T(8,128)(2,1)S(1)} %get-tuple-element.60), channel_id=1, source_target_pairs={{0,6},{1,7},{2,0},{3,1},{4,2},{5,3},{6,4},{7,5},{8,14},{9,15},{10,... | collective-permute-start | bytes 589832 | tf_op jit(solution)/shard_map/ppermute | solution.py:339
  121.1 1.9 %collective-permute-start.11 = (bf16[3,64,512]{2,1,0:T(8,128)(2,1)S(1)}, bf16[3,64,512]{2,1,0:T(8,128)(2,1)S(1)}, u32[]{:S(2)}, u32[]{:S(2)}) collective-permute-start(bf16[3,64,512]{2,1,0:T(8,128)(2,1)S(1)} %get-tuple-element.61), channel_id=1, source_target_pairs={{0,2},{1,3},{2,4},{3,5},{4,6},{5,7},{6,0},{7,1},{8,10},{9,11},{10,... | collective-permute-start | bytes 589832 | tf_op jit(solution)/shard_map/ppermute | solution.py:339
  123.1 0.0 collective-permute-done.7.refs_0_.refs_4_
  123.1 0.7 collective-permute-start.12
  123.8 1.0 collective-permute-start.13
  124.8 0.2 collective-permute-done.9.refs_2_.refs_3_
  125.0 2.7 %collective-permute-done.10.refs_3_.refs_6_ = bf16[3,64,512]{2,1,0:T(8,128)(2,1)S(1)} collective-permute-done((bf16[3,64,512]{2,1,0:T(8,128)(2,1)S(1)}, bf16[3,64,512]{2,1,0:T(8,128)(2,1)S(1)}, u32[]{:S(2)}, u32[]{:S(2)}) %collective-permute-start.10) | collective-permute-done | bytes 196640 | tf_op jit(solution)/shard_map/ppermute | solution.py:339
  127.7 2.3 %collective-permute-done.11.refs_4_.refs_2_ = bf16[3,64,512]{2,1,0:T(8,128)(2,1)S(1)} collective-permute-done((bf16[3,64,512]{2,1,0:T(8,128)(2,1)S(1)}, bf16[3,64,512]{2,1,0:T(8,128)(2,1)S(1)}, u32[]{:S(2)}, u32[]{:S(2)}) %collective-permute-start.11) | collective-permute-done | bytes 196640 | tf_op jit(solution)/shard_map/ppermute | solution.py:339
  130.0 1.3 all-to-all-done.4.got
  131.3 1.3 place.1
  132.6 0.0 copy-start.2
  132.6 10.3 %all-to-all-start.5 = ((bf16[8,8,2048]{2,1,0:T(8,128)(2,1)}), bf16[8,8,2048]{2,1,0:T(8,128)(2,1)S(1)}, u32[]{:S(2)}, u32[]{:S(2)}) async-start(bf16[8,8,2048]{2,1,0:T(8,128)(2,1)} %place.1), calls=%async_computation.5 | async-start | bytes 524288 | tf_op jit(solution)/shard_map/all_to_all | solution.py:433
  142.9 0.2 select_reduce_fusion.1.source
  143.1 1.8 %finish.1 = (f32[4,64,512]{2,1,0:T(8,128)}, f32[4,64,512]{2,1,0:T(8,128)}, bf16[4,64,512]{2,1,0:T(8,128)(2,1)}) custom-call(s32[8]{0:T(128)S(1)} %select_reduce_fusion.1.source, f32[4,64,512]{2,1,0:T(8,128)S(1)} %bitcast.17, f32[4,64,512]{2,1,0:T(8,128)S(1)} %bitcast.18, bf16[3,64,512]{2,1,0:T(8,128)(2,1)S(1)} %get-tuple-element.65.refs_0_, ...), custom_call_target="tpu_custom_call" | custom-call | bytes 3932160 | tf_op jit(solution)/shard_map/finish/pallas_call | solution.py:53
  144.9 4.5 %all-to-all-done.5 = bf16[8,8,2048]{2,1,0:T(8,128)(2,1)S(1)} async-done(((bf16[8,8,2048]{2,1,0:T(8,128)(2,1)}), bf16[8,8,2048]{2,1,0:T(8,128)(2,1)S(1)}, u32[]{:S(2)}, u32[]{:S(2)}) %all-to-all-start.5) | async-done | bytes 262176 | tf_op jit(solution)/shard_map/all_to_all | solution.py:433
  149.4 0.8 fusion
  (20 shorter events, 0.1 us)
Async XLA Ops:
  0.6 11.1 %copy-start = (bf16[64,2048]{1,0:T(8,128)(2,1)S(1)}, bf16[64,2048]{1,0:T(8,128)(2,1)}, u32[]{:S(2)}) copy-start(bf16[64,2048]{1,0:T(8,128)(2,1)} %grad.1) | copy-start | bytes 786436
  0.6 16.9 %all-to-all-start = ((bf16[8,8,2048]{2,1,0:T(8,128)(2,1)}), bf16[8,8,2048]{2,1,0:T(8,128)(2,1)S(1)}, u32[]{:S(2)}, u32[]{:S(2)}) async-start(bf16[8,8,2048]{2,1,0:T(8,128)(2,1)} %bitcast.16), calls=%async_computation | async-start | bytes 524288 | tf_op jit(solution)/shard_map/all_to_all | solution.py:348
  11.0 0.7 copy-start.9
  11.7 1.0 copy-start.1
  18.9 11.8 %copy-start.4 = (bf16[1,4,64,512]{3,2,1,0:T(8,128)(2,1)S(1)}, bf16[1,4,64,512]{3,2,1,0:T(8,128)(2,1)}, u32[]{:S(2)}) copy-start(bf16[1,4,64,512]{3,2,1,0:T(8,128)(2,1)} %param.13) | copy-start | bytes 786436
  19.0 11.8 %copy-start.5 = (bf16[1,4,64,512]{3,2,1,0:T(8,128)(2,1)S(1)}, bf16[1,4,64,512]{3,2,1,0:T(8,128)(2,1)}, u32[]{:S(2)}) copy-start(bf16[1,4,64,512]{3,2,1,0:T(8,128)(2,1)} %param.14) | copy-start | bytes 786436
  19.0 11.8 %copy-start.6 = (bf16[1,4,64,512]{3,2,1,0:T(8,128)(2,1)S(1)}, bf16[1,4,64,512]{3,2,1,0:T(8,128)(2,1)}, u32[]{:S(2)}) copy-start(bf16[1,4,64,512]{3,2,1,0:T(8,128)(2,1)} %param.15) | copy-start | bytes 786436
  19.0 35.4 %all-to-all-start.1 = ((bf16[16,17,8,128]{3,2,1,0:T(8,128)(2,1)}), bf16[16,17,8,128]{3,2,1,0:T(8,128)(2,1)S(1)}, u32[]{:S(2)}, u32[]{:S(2)}) async-start(bf16[16,17,8,128]{3,2,1,0:T(8,128)(2,1)} %spread.1.after), calls=%async_computation.1 | async-start | bytes 1114112 | tf_op jit(solution)/shard_map/all_to_all | solution.py:365
  31.4 0.7 copy-start.7
  32.1 15.5 %collective-permute-start = (bf16[3,64,512]{2,1,0:T(8,128)(2,1)S(1)}, bf16[3,64,512]{2,1,0:T(8,128)(2,1)S(1)}, u32[]{:S(2)}, u32[]{:S(2)}) collective-permute-start(bf16[3,64,512]{2,1,0:T(8,128)(2,1)S(1)} %get-tuple-element.38), channel_id=1, source_target_pairs={{0,4},{1,5},{2,6},{3,7},{4,0},{5,1},{6,2},{7,3},{8,12},{9,13},{10,... | collective-permute-start | bytes 589832 | tf_op jit(solution)/shard_map/ppermute | solution.py:339
  34.6 14.7 %collective-permute-start.1 = (bf16[3,64,512]{2,1,0:T(8,128)(2,1)S(1)}, bf16[3,64,512]{2,1,0:T(8,128)(2,1)S(1)}, u32[]{:S(2)}, u32[]{:S(2)}) collective-permute-start(bf16[3,64,512]{2,1,0:T(8,128)(2,1)S(1)} %get-tuple-element.39), channel_id=1, source_target_pairs={{0,5},{1,6},{2,7},{3,0},{4,1},{5,2},{6,3},{7,4},{8,13},{9,14},{10,... | collective-permute-start | bytes 589832 | tf_op jit(solution)/shard_map/ppermute | solution.py:339
  40.1 9.9 %collective-permute-start.2 = (bf16[3,64,512]{2,1,0:T(8,128)(2,1)S(1)}, bf16[3,64,512]{2,1,0:T(8,128)(2,1)S(1)}, u32[]{:S(2)}, u32[]{:S(2)}) collective-permute-start(bf16[3,64,512]{2,1,0:T(8,128)(2,1)S(1)} %get-tuple-element.40), channel_id=1, source_target_pairs={{0,3},{1,4},{2,5},{3,6},{4,7},{5,0},{6,1},{7,2},{8,11},{9,12},{10,... | collective-permute-start | bytes 589832 | tf_op jit(solution)/shard_map/ppermute | solution.py:339
  42.3 9.7 %collective-permute-start.3 = (bf16[3,64,512]{2,1,0:T(8,128)(2,1)S(1)}, bf16[3,64,512]{2,1,0:T(8,128)(2,1)S(1)}, u32[]{:S(2)}, u32[]{:S(2)}) collective-permute-start(bf16[3,64,512]{2,1,0:T(8,128)(2,1)S(1)} %get-tuple-element.41), channel_id=1, source_target_pairs={{0,6},{1,7},{2,0},{3,1},{4,2},{5,3},{6,4},{7,5},{8,14},{9,15},{10,... | collective-permute-start | bytes 589832 | tf_op jit(solution)/shard_map/ppermute | solution.py:339
  45.7 7.9 %collective-permute-start.4 = (bf16[3,64,512]{2,1,0:T(8,128)(2,1)S(1)}, bf16[3,64,512]{2,1,0:T(8,128)(2,1)S(1)}, u32[]{:S(2)}, u32[]{:S(2)}) collective-permute-start(bf16[3,64,512]{2,1,0:T(8,128)(2,1)S(1)} %get-tuple-element.42), channel_id=1, source_target_pairs={{0,2},{1,3},{2,4},{3,5},{4,6},{5,7},{6,0},{7,1},{8,10},{9,11},{10,... | collective-permute-start | bytes 589832 | tf_op jit(solution)/shard_map/ppermute | solution.py:339
  47.6 6.0 %collective-permute-start.5 = (bf16[3,64,512]{2,1,0:T(8,128)(2,1)S(1)}, bf16[3,64,512]{2,1,0:T(8,128)(2,1)S(1)}, u32[]{:S(2)}, u32[]{:S(2)}) collective-permute-start(bf16[3,64,512]{2,1,0:T(8,128)(2,1)S(1)} %get-tuple-element.43), channel_id=1, source_target_pairs={{0,7},{1,0},{2,1},{3,2},{4,3},{5,4},{6,5},{7,6},{8,15},{9,8},{10,9... | collective-permute-start | bytes 589832 | tf_op jit(solution)/shard_map/ppermute | solution.py:339
  49.2 5.2 %collective-permute-start.6 = (bf16[3,64,512]{2,1,0:T(8,128)(2,1)S(1)}, bf16[3,64,512]{2,1,0:T(8,128)(2,1)S(1)}, u32[]{:S(2)}, u32[]{:S(2)}) collective-permute-start(bf16[3,64,512]{2,1,0:T(8,128)(2,1)S(1)} %get-tuple-element.44), channel_id=1, source_target_pairs={{0,1},{1,2},{2,3},{3,4},{4,5},{5,6},{6,7},{7,0},{8,9},{9,10},{10,1... | collective-permute-start | bytes 589832 | tf_op jit(solution)/shard_map/ppermute | solution.py:339
  55.4 23.5 %all-to-all-start.2 = ((bf16[32,9,8,128]{3,2,1,0:T(8,128)(2,1)}), bf16[32,9,8,128]{3,2,1,0:T(8,128)(2,1)S(1)}, u32[]{:S(2)}, u32[]{:S(2)}) async-start(bf16[32,9,8,128]{3,2,1,0:T(8,128)(2,1)} %plane.1), calls=%async_computation.2 | async-start | bytes 1179648 | tf_op jit(solution)/shard_map/all_to_all | solution.py:377
  67.9 0.9 copy-start.8
  81.0 16.4 %all-to-all-start.3 = ((bf16[32,9,8,128]{3,2,1,0:T(8,128)(2,1)}), bf16[32,9,8,128]{3,2,1,0:T(8,128)(2,1)S(1)}, u32[]{:S(2)}, u32[]{:S(2)}) async-start(bf16[32,9,8,128]{3,2,1,0:T(8,128)(2,1)} %block.1.moment), calls=%async_computation.3 | async-start | bytes 1179648 | tf_op jit(solution)/shard_map/all_to_all | solution.py:401
  98.4 32.9 %all-to-all-start.4 = ((bf16[16,17,8,128]{3,2,1,0:T(8,128)(2,1)}), bf16[16,17,8,128]{3,2,1,0:T(8,128)(2,1)S(1)}, u32[]{:S(2)}, u32[]{:S(2)}) async-start(bf16[16,17,8,128]{3,2,1,0:T(8,128)(2,1)} %get-tuple-element.56), calls=%async_computation.4 | async-start | bytes 1114112 | tf_op jit(solution)/shard_map/all_to_all | solution.py:420
  107.3 15.8 %collective-permute-start.7 = (bf16[3,64,512]{2,1,0:T(8,128)(2,1)S(1)}, bf16[3,64,512]{2,1,0:T(8,128)(2,1)S(1)}, u32[]{:S(2)}, u32[]{:S(2)}) collective-permute-start(bf16[3,64,512]{2,1,0:T(8,128)(2,1)S(1)} %get-tuple-element.57), channel_id=1, source_target_pairs={{0,4},{1,5},{2,6},{3,7},{4,0},{5,1},{6,2},{7,3},{8,12},{9,13},{10,... | collective-permute-start | bytes 589832 | tf_op jit(solution)/shard_map/ppermute | solution.py:339
  110.0 13.8 %collective-permute-start.8 = (bf16[3,64,512]{2,1,0:T(8,128)(2,1)S(1)}, bf16[3,64,512]{2,1,0:T(8,128)(2,1)S(1)}, u32[]{:S(2)}, u32[]{:S(2)}) collective-permute-start(bf16[3,64,512]{2,1,0:T(8,128)(2,1)S(1)} %get-tuple-element.58), channel_id=1, source_target_pairs={{0,5},{1,6},{2,7},{3,0},{4,1},{5,2},{6,3},{7,4},{8,13},{9,14},{10,... | collective-permute-start | bytes 589832 | tf_op jit(solution)/shard_map/ppermute | solution.py:339
  114.7 10.3 %collective-permute-start.9 = (bf16[3,64,512]{2,1,0:T(8,128)(2,1)S(1)}, bf16[3,64,512]{2,1,0:T(8,128)(2,1)S(1)}, u32[]{:S(2)}, u32[]{:S(2)}) collective-permute-start(bf16[3,64,512]{2,1,0:T(8,128)(2,1)S(1)} %get-tuple-element.59), channel_id=1, source_target_pairs={{0,3},{1,4},{2,5},{3,6},{4,7},{5,0},{6,1},{7,2},{8,11},{9,12},{10,... | collective-permute-start | bytes 589832 | tf_op jit(solution)/shard_map/ppermute | solution.py:339
  117.1 10.6 %collective-permute-start.10 = (bf16[3,64,512]{2,1,0:T(8,128)(2,1)S(1)}, bf16[3,64,512]{2,1,0:T(8,128)(2,1)S(1)}, u32[]{:S(2)}, u32[]{:S(2)}) collective-permute-start(bf16[3,64,512]{2,1,0:T(8,128)(2,1)S(1)} %get-tuple-element.60), channel_id=1, source_target_pairs={{0,6},{1,7},{2,0},{3,1},{4,2},{5,3},{6,4},{7,5},{8,14},{9,15},{10,... | collective-permute-start | bytes 589832 | tf_op jit(solution)/shard_map/ppermute | solution.py:339
  121.1 8.8 %collective-permute-start.11 = (bf16[3,64,512]{2,1,0:T(8,128)(2,1)S(1)}, bf16[3,64,512]{2,1,0:T(8,128)(2,1)S(1)}, u32[]{:S(2)}, u32[]{:S(2)}) collective-permute-start(bf16[3,64,512]{2,1,0:T(8,128)(2,1)S(1)} %get-tuple-element.61), channel_id=1, source_target_pairs={{0,2},{1,3},{2,4},{3,5},{4,6},{5,7},{6,0},{7,1},{8,10},{9,11},{10,... | collective-permute-start | bytes 589832 | tf_op jit(solution)/shard_map/ppermute | solution.py:339
  123.1 6.9 %collective-permute-start.12 = (bf16[3,64,512]{2,1,0:T(8,128)(2,1)S(1)}, bf16[3,64,512]{2,1,0:T(8,128)(2,1)S(1)}, u32[]{:S(2)}, u32[]{:S(2)}) collective-permute-start(bf16[3,64,512]{2,1,0:T(8,128)(2,1)S(1)} %get-tuple-element.62), channel_id=1, source_target_pairs={{0,7},{1,0},{2,1},{3,2},{4,3},{5,4},{6,5},{7,6},{8,15},{9,8},{10,9... | collective-permute-start | bytes 589832 | tf_op jit(solution)/shard_map/ppermute | solution.py:339
  123.8 6.2 %collective-permute-start.13 = (bf16[3,64,512]{2,1,0:T(8,128)(2,1)S(1)}, bf16[3,64,512]{2,1,0:T(8,128)(2,1)S(1)}, u32[]{:S(2)}, u32[]{:S(2)}) collective-permute-start(bf16[3,64,512]{2,1,0:T(8,128)(2,1)S(1)} %get-tuple-element.63), channel_id=1, source_target_pairs={{0,1},{1,2},{2,3},{3,4},{4,5},{5,6},{6,7},{7,0},{8,9},{9,10},{10,1... | collective-permute-start | bytes 589832 | tf_op jit(solution)/shard_map/ppermute | solution.py:339
  131.3 11.8 %copy-start.3 = (f32[1,4,64,512]{3,2,1,0:T(8,128)S(1)}, f32[1,4,64,512]{3,2,1,0:T(8,128)}, u32[]{:S(2)}) copy-start(f32[1,4,64,512]{3,2,1,0:T(8,128)} %param.12) | copy-start | bytes 1572868
  132.6 10.5 %copy-start.2 = (f32[1,4,64,512]{3,2,1,0:T(8,128)S(1)}, f32[1,4,64,512]{3,2,1,0:T(8,128)}, u32[]{:S(2)}) copy-start(f32[1,4,64,512]{3,2,1,0:T(8,128)} %param.11) | copy-start | bytes 1572868
  132.6 16.8 %all-to-all-start.5 = ((bf16[8,8,2048]{2,1,0:T(8,128)(2,1)}), bf16[8,8,2048]{2,1,0:T(8,128)(2,1)S(1)}, u32[]{:S(2)}, u32[]{:S(2)}) async-start(bf16[8,8,2048]{2,1,0:T(8,128)(2,1)} %place.1), calls=%async_computation.5 | async-start | bytes 524288 | tf_op jit(solution)/shard_map/all_to_all | solution.py:433

commit v3 on v2

--- a/solution.py
+++ b/solution.py
@@ -41,7 +41,19 @@
     return [struct(*a.shape, dtype=a.dtype) for a in hold]
 
 
-def call(body, specs, outs, args, scratch=(), vmem=16, flops=0, name=None, stream=False, hold=()):
+def call(
+    body,
+    specs,
+    outs,
+    args,
+    scratch=(),
+    vmem=16,
+    flops=0,
+    name=None,
+    stream=False,
+    hold=(),
+    prefetch=False,
+):
     space = {"v": pltpu.VMEM, "s": pltpu.SMEM, "a": pl.ANY}
     size = sum(o.size * o.dtype.itemsize for o in outs)
     size += sum(a.size * a.dtype.itemsize for a, k in zip(args, specs) if k == "v")
@@ -50,13 +62,20 @@
     scratch = list(scratch)
     if stream:
         scratch += [pltpu.VMEM(outs[0].shape, outs[0].dtype), pltpu.SemaphoreType.DMA((CHUNKS + 1,))]
+    count = specs.count("s") if prefetch else 0
     return pl.pallas_call(
         body,
         out_shape=tuple(outs),
-        in_specs=[pl.BlockSpec(memory_space=space[k]) for k in specs],
-        out_specs=tuple(pl.BlockSpec(memory_space=space["a" if stream else "v"]) for _ in outs),
+        grid_spec=pltpu.PrefetchScalarGridSpec(
+            num_scalar_prefetch=count,
+            grid=(),
+            in_specs=[pl.BlockSpec(memory_space=space[k]) for k in specs[count:]],
+            out_specs=tuple(
+                pl.BlockSpec(memory_space=space["a" if stream else "v"]) for _ in outs
+            ),
+            scratch_shapes=scratch,
+        ),
         input_output_aliases={first + i: 1 + i for i in range(len(hold))},
-        scratch_shapes=scratch,
         compiler_params=pltpu.CompilerParams(vmem_limit_bytes=vmem * 1024 * 1024),
         cost_estimate=pl.CostEstimate(flops=flops, bytes_accessed=size, transcendentals=0),
         name=name,
@@ -136,7 +155,7 @@
     )(index, gradient, second_moment)
 
 
-def spread_body(inverse, tile, got, out, buffer, sems):
+def spread_body(inverse, tile, got, before, out, buffer, sems):
     def fill(z):
         for y in range(YDIM):
             j = inverse[z * YDIM + y]
@@ -349,10 +368,11 @@
     new_second, tile = adam(lax.axis_index("m")[None], gradient, second_moment)
     (pay,) = call(
         spread_body,
-        "svv",
+        "svva",
         [struct(ZD, YDIM * TB + 1, SUB, LANES)],
-        [inverse, tile, got],
+        [inverse, tile, got, to],
         name="spread",
+        prefetch=True,
         stream=True,
     )
     packed = call(
@@ -361,6 +381,7 @@
         [struct(3, ROW_DEV, BLK)] * MD,
         [to, left_root[0], right_root[0], momentum[0], pay],
         name="pack",
+        prefetch=True,
     )
     got = lax.all_to_all(pay, "z", 0, 0, tiled=True)
     moved = {0: packed[0]}
@@ -427,6 +448,7 @@
         [struct(MD, SUB, LOCAL)],
         [band_owner, got, *(results[s] for s in SHIFTS)],
         name="place",
+        prefetch=True,
         stream=True,
     )
     (clip,) = call(norm_body, "v", [struct(1, LANES, dtype=F32)], [got], name="norm")

time: 151 us -> 150 us (level)
  transfers between devices with their start and end apart: 20 -> 20, of which waited for: 12 -> 13; matrix products, arithmetic and copies ran while one was open for 1% -> 1% of each run, Pallas kernels for 4% -> 4%
where the time goes in v3:
time: 150 us; the launch traced here: 149 us
  starting transfers between devices  90 us (60%)
  waiting for transfers between devices  38.2 us (25%)
  Pallas kernels  13.1 us (9%)
  local copies, waits for them, and re-layouts  3.41 us (2%)
  other arithmetic  2.82 us (2%)
  between operations  1.6 us (1%)
    ppermute x14, starting transfers between devices, shift(): return lax.ppermute(part, 'm', [(i, (i + s) % MD) for i in range(MD)])  34.7 us
    all_to_all x2, starting transfers between devices, shards(): got = lax.all_to_all(pay, 'z', 0, 0, tiled=True)  18.3 us
    all_to_all x1, starting transfers between devices, shards(): got = lax.all_to_all(pay, ('y', 'm'), 0, 0, tiled=True)  12.3 us
    pallas_call x10, Pallas kernels, call(): pl.pallas_call(body, out_shape=tuple(outs), grid_spec=pltpu.PrefetchScala...  11.4 us
    all_to_all x1, waiting for transfers between devices, shards(): got = lax.all_to_all(back, ('y', 'm'), 0, 0, tiled=True)  10.4 us
    all_to_all x1, starting transfers between devices, shards(): lax.all_to_all(gradient.reshape(MD, SUB, LOCAL), 'm', 0, 0, tiled=True)  10.3 us
    all_to_all x1, starting transfers between devices, shards(): placed = lax.all_to_all(pay, 'm', 0, 0, tiled=True).reshape(ROW_DEV, LOCAL)  10.3 us
    ppermute x14, waiting for transfers between devices, shift(): return lax.ppermute(part, 'm', [(i, (i + s) % MD) for i in range(MD)])  10.2 us
  transfers between devices with their start and end apart: 20, of which 13 were waited for; matrix products, arithmetic and copies ran while one was open for 1% of the time, Pallas kernels for 4%

profile of v3, /device:TPU:1, one launch (start us, length us, event | category | flops | bytes accessed | tf_op | source)
XLA Modules:
  0.0 149.1 jit_solution(9634311562247241719)
XLA Ops:
  0.6 10.3 %all-to-all-start = ((bf16[8,8,2048]{2,1,0:T(8,128)(2,1)}), bf16[8,8,2048]{2,1,0:T(8,128)(2,1)S(1)}, u32[]{:S(2)}, u32[]{:S(2)}) async-start(bf16[8,8,2048]{2,1,0:T(8,128)(2,1)} %bitcast.16), calls=%async_computation | async-start | bytes 524288 | tf_op jit(solution)/shard_map/all_to_all | solution.py:367
  11.0 0.7 copy-done.9
  11.7 0.1 reshape.77
  11.7 0.1 convert_reduce_fusion
  11.9 0.1 select_reduce_fusion.3
  12.0 0.6 compare_select_fusion.4
  12.7 1.0 copy-done.1
  13.7 1.7 %adam.1 = (f32[64,2048]{1,0:T(8,128)}, bf16[8,128]{1,0:T(8,128)(2,1)S(1)}) custom-call(s32[1]{0:T(128)} %bitcast.1.index.other, bf16[64,2048]{1,0:T(8,128)(2,1)S(1)} %copy-done, f32[64,2048]{1,0:T(8,128)S(1)} %copy-done.1), custom_call_target="tpu_custom_call" | custom-call | tf_op jit(solution)/shard_map/adam/pallas_call | solution.py:146
  15.4 0.1 select_reduce_fusion.inverse
  15.5 0.2 select_reduce_fusion.2.before.to
  15.7 1.8 %all-to-all-done.got = bf16[8,8,2048]{2,1,0:T(8,128)(2,1)S(1)} async-done(((bf16[8,8,2048]{2,1,0:T(8,128)(2,1)}), bf16[8,8,2048]{2,1,0:T(8,128)(2,1)S(1)}, u32[]{:S(2)}, u32[]{:S(2)}) %all-to-all-start) | async-done | bytes 262176 | tf_op jit(solution)/shard_map/all_to_all | solution.py:367
  17.5 1.4 spread.1.after
  18.9 0.0 copy-start.4
  19.0 0.0 copy-start.5
  19.0 0.0 copy-start.6
  19.0 10.6 %all-to-all-start.1 = ((bf16[16,17,8,128]{3,2,1,0:T(8,128)(2,1)}), bf16[16,17,8,128]{3,2,1,0:T(8,128)(2,1)S(1)}, u32[]{:S(2)}, u32[]{:S(2)}) async-start(bf16[16,17,8,128]{3,2,1,0:T(8,128)(2,1)} %spread.1.after), calls=%async_computation.1 | async-start | bytes 1114112 | tf_op jit(solution)/shard_map/all_to_all | solution.py:386
  29.7 0.6 pack.1
  30.3 0.0 copy-start.7
  30.3 0.7 copy-done.7
  31.0 3.0 %collective-permute-start = (bf16[3,64,512]{2,1,0:T(8,128)(2,1)S(1)}, bf16[3,64,512]{2,1,0:T(8,128)(2,1)S(1)}, u32[]{:S(2)}, u32[]{:S(2)}) collective-permute-start(bf16[3,64,512]{2,1,0:T(8,128)(2,1)S(1)} %get-tuple-element.38), channel_id=1, source_target_pairs={{0,4},{1,5},{2,6},{3,7},{4,0},{5,1},{6,2},{7,3},{8,12},{9,13},{10,... | collective-permute-start | bytes 589832 | tf_op jit(solution)/shard_map/ppermute | solution.py:358
  34.0 5.0 %collective-permute-start.1 = (bf16[3,64,512]{2,1,0:T(8,128)(2,1)S(1)}, bf16[3,64,512]{2,1,0:T(8,128)(2,1)S(1)}, u32[]{:S(2)}, u32[]{:S(2)}) collective-permute-start(bf16[3,64,512]{2,1,0:T(8,128)(2,1)S(1)} %get-tuple-element.39), channel_id=1, source_target_pairs={{0,5},{1,6},{2,7},{3,0},{4,1},{5,2},{6,3},{7,4},{8,13},{9,14},{10,... | collective-permute-start | bytes 589832 | tf_op jit(solution)/shard_map/ppermute | solution.py:358
  39.0 2.2 %collective-permute-start.2 = (bf16[3,64,512]{2,1,0:T(8,128)(2,1)S(1)}, bf16[3,64,512]{2,1,0:T(8,128)(2,1)S(1)}, u32[]{:S(2)}, u32[]{:S(2)}) collective-permute-start(bf16[3,64,512]{2,1,0:T(8,128)(2,1)S(1)} %get-tuple-element.40), channel_id=1, source_target_pairs={{0,3},{1,4},{2,5},{3,6},{4,7},{5,0},{6,1},{7,2},{8,11},{9,12},{10,... | collective-permute-start | bytes 589832 | tf_op jit(solution)/shard_map/ppermute | solution.py:358
  41.2 3.4 %collective-permute-start.3 = (bf16[3,64,512]{2,1,0:T(8,128)(2,1)S(1)}, bf16[3,64,512]{2,1,0:T(8,128)(2,1)S(1)}, u32[]{:S(2)}, u32[]{:S(2)}) collective-permute-start(bf16[3,64,512]{2,1,0:T(8,128)(2,1)S(1)} %get-tuple-element.41), channel_id=1, source_target_pairs={{0,6},{1,7},{2,0},{3,1},{4,2},{5,3},{6,4},{7,5},{8,14},{9,15},{10,... | collective-permute-start | bytes 589832 | tf_op jit(solution)/shard_map/ppermute | solution.py:358
  44.6 1.9 %collective-permute-start.4 = (bf16[3,64,512]{2,1,0:T(8,128)(2,1)S(1)}, bf16[3,64,512]{2,1,0:T(8,128)(2,1)S(1)}, u32[]{:S(2)}, u32[]{:S(2)}) collective-permute-start(bf16[3,64,512]{2,1,0:T(8,128)(2,1)S(1)} %get-tuple-element.42), channel_id=1, source_target_pairs={{0,2},{1,3},{2,4},{3,5},{4,6},{5,7},{6,0},{7,1},{8,10},{9,11},{10,... | collective-permute-start | bytes 589832 | tf_op jit(solution)/shard_map/ppermute | solution.py:358
  46.5 0.0 collective-permute-done.refs_0_.refs_4_
  46.5 1.6 %collective-permute-start.5 = (bf16[3,64,512]{2,1,0:T(8,128)(2,1)S(1)}, bf16[3,64,512]{2,1,0:T(8,128)(2,1)S(1)}, u32[]{:S(2)}, u32[]{:S(2)}) collective-permute-start(bf16[3,64,512]{2,1,0:T(8,128)(2,1)S(1)} %get-tuple-element.43), channel_id=1, source_target_pairs={{0,7},{1,0},{2,1},{3,2},{4,3},{5,4},{6,5},{7,6},{8,15},{9,8},{10,9... | collective-permute-start | bytes 589832 | tf_op jit(solution)/shard_map/ppermute | solution.py:358
  48.1 0.0 collective-permute-done.1.refs_1_.refs_5_
  48.1 0.2 collective-permute-start.6
  48.3 0.6 collective-permute-done.2.refs_2_.refs_3_
  48.9 2.1 %collective-permute-done.3.refs_3_.refs_6_ = bf16[3,64,512]{2,1,0:T(8,128)(2,1)S(1)} collective-permute-done((bf16[3,64,512]{2,1,0:T(8,128)(2,1)S(1)}, bf16[3,64,512]{2,1,0:T(8,128)(2,1)S(1)}, u32[]{:S(2)}, u32[]{:S(2)}) %collective-permute-start.3) | collective-permute-done | bytes 196640 | tf_op jit(solution)/shard_map/ppermute | solution.py:358
  50.9 1.6 %collective-permute-done.4.refs_4_.refs_2_ = bf16[3,64,512]{2,1,0:T(8,128)(2,1)S(1)} collective-permute-done((bf16[3,64,512]{2,1,0:T(8,128)(2,1)S(1)}, bf16[3,64,512]{2,1,0:T(8,128)(2,1)S(1)}, u32[]{:S(2)}, u32[]{:S(2)}) %collective-permute-start.4) | collective-permute-done | bytes 196640 | tf_op jit(solution)/shard_map/ppermute | solution.py:358
  52.5 0.8 collective-permute-done.6.refs_6_.refs_1_
  53.3 0.2 all-to-all-done.1.got
  53.5 0.9 plane.1
  54.4 12.3 %all-to-all-start.2 = ((bf16[32,9,8,128]{3,2,1,0:T(8,128)(2,1)}), bf16[32,9,8,128]{3,2,1,0:T(8,128)(2,1)S(1)}, u32[]{:S(2)}, u32[]{:S(2)}) async-start(bf16[32,9,8,128]{3,2,1,0:T(8,128)(2,1)} %plane.1), calls=%async_computation.2 | async-start | bytes 1179648 | tf_op jit(solution)/shard_map/all_to_all | solution.py:398
  67.4 0.7 compare_select_fusion.5
  68.1 0.0 copy-start.8
  68.1 0.9 copy-done.8
  69.0 0.1 roots.1
  69.2 9.9 %all-to-all-done.2.got = bf16[32,9,8,128]{3,2,1,0:T(8,128)(2,1)S(1)} async-done(((bf16[32,9,8,128]{3,2,1,0:T(8,128)(2,1)}), bf16[32,9,8,128]{3,2,1,0:T(8,128)(2,1)S(1)}, u32[]{:S(2)}, u32[]{:S(2)}) %all-to-all-start.2) | async-done | bytes 589856 | tf_op jit(solution)/shard_map/all_to_all | solution.py:398
  79.0 2.2 %block.1.moment = bf16[32,9,8,128]{3,2,1,0:T(8,128)(2,1)} custom-call(f32[8,128]{1,0:T(8,128)S(1)} %pad_select_fusion.masks, bf16[32,9,8,128]{3,2,1,0:T(8,128)(2,1)S(1)} %all-to-all-done.2.got, bf16[512,512]{1,0:T(8,128)(2,1)S(1)} %get-tuple-element.46.left, bf16[512,512]{1,0:T(8,128)(2,1)S(1)} %get-tuple-element.47.right, ...), custom_call_target="tpu_custom_call" | custom-call | flops 536870912 | bytes 2756608 | tf_op jit(solution)/shard_map/block/pallas_call | solution.py:66
  81.2 4.1 %all-to-all-start.3 = ((bf16[32,9,8,128]{3,2,1,0:T(8,128)(2,1)}), bf16[32,9,8,128]{3,2,1,0:T(8,128)(2,1)S(1)}, u32[]{:S(2)}, u32[]{:S(2)}) async-start(bf16[32,9,8,128]{3,2,1,0:T(8,128)(2,1)} %block.1.moment), calls=%async_computation.3 | async-start | bytes 1179648 | tf_op jit(solution)/shard_map/all_to_all | solution.py:422
  85.3 2.0 %stats.1 = (bf16[3,64,512]{2,1,0:T(8,128)(2,1)S(1)}, bf16[3,64,512]{2,1,0:T(8,128)(2,1)S(1)}, bf16[3,64,512]{2,1,0:T(8,128)(2,1)S(1)}, bf16[3,64,512]{2,1,0:T(8,...) custom-call(s32[1]{0:T(128)} %bitcast.1.index.other, ...), custom_call_target="tpu_custom_call" | custom-call | flops 536870912 | bytes 2752512 | tf_op jit(solution)/shard_map/stats/pallas_call | solution.py:66
  87.3 10.4 %all-to-all-done.3.got = bf16[32,9,8,128]{3,2,1,0:T(8,128)(2,1)S(1)} async-done(((bf16[32,9,8,128]{3,2,1,0:T(8,128)(2,1)}), bf16[32,9,8,128]{3,2,1,0:T(8,128)(2,1)S(1)}, u32[]{:S(2)}, u32[]{:S(2)}) %all-to-all-start.3) | async-done | bytes 589856 | tf_op jit(solution)/shard_map/all_to_all | solution.py:422
  97.7 0.9 unplane.1
  98.6 7.6 %all-to-all-start.4 = ((bf16[16,17,8,128]{3,2,1,0:T(8,128)(2,1)}), bf16[16,17,8,128]{3,2,1,0:T(8,128)(2,1)S(1)}, u32[]{:S(2)}, u32[]{:S(2)}) async-start(bf16[16,17,8,128]{3,2,1,0:T(8,128)(2,1)} %get-tuple-element.56), calls=%async_computation.4 | async-start | bytes 1114112 | tf_op jit(solution)/shard_map/all_to_all | solution.py:441
  106.2 2.7 %collective-permute-start.7 = (bf16[3,64,512]{2,1,0:T(8,128)(2,1)S(1)}, bf16[3,64,512]{2,1,0:T(8,128)(2,1)S(1)}, u32[]{:S(2)}, u32[]{:S(2)}) collective-permute-start(bf16[3,64,512]{2,1,0:T(8,128)(2,1)S(1)} %get-tuple-element.57), channel_id=1, source_target_pairs={{0,4},{1,5},{2,6},{3,7},{4,0},{5,1},{6,2},{7,3},{8,12},{9,13},{10,... | collective-permute-start | bytes 589832 | tf_op jit(solution)/shard_map/ppermute | solution.py:358
  108.9 4.6 %collective-permute-start.8 = (bf16[3,64,512]{2,1,0:T(8,128)(2,1)S(1)}, bf16[3,64,512]{2,1,0:T(8,128)(2,1)S(1)}, u32[]{:S(2)}, u32[]{:S(2)}) collective-permute-start(bf16[3,64,512]{2,1,0:T(8,128)(2,1)S(1)} %get-tuple-element.58), channel_id=1, source_target_pairs={{0,5},{1,6},{2,7},{3,0},{4,1},{5,2},{6,3},{7,4},{8,13},{9,14},{10,... | collective-permute-start | bytes 589832 | tf_op jit(solution)/shard_map/ppermute | solution.py:358
  113.6 2.4 %collective-permute-start.9 = (bf16[3,64,512]{2,1,0:T(8,128)(2,1)S(1)}, bf16[3,64,512]{2,1,0:T(8,128)(2,1)S(1)}, u32[]{:S(2)}, u32[]{:S(2)}) collective-permute-start(bf16[3,64,512]{2,1,0:T(8,128)(2,1)S(1)} %get-tuple-element.59), channel_id=1, source_target_pairs={{0,3},{1,4},{2,5},{3,6},{4,7},{5,0},{6,1},{7,2},{8,11},{9,12},{10,... | collective-permute-start | bytes 589832 | tf_op jit(solution)/shard_map/ppermute | solution.py:358
  116.0 4.0 %collective-permute-start.10 = (bf16[3,64,512]{2,1,0:T(8,128)(2,1)S(1)}, bf16[3,64,512]{2,1,0:T(8,128)(2,1)S(1)}, u32[]{:S(2)}, u32[]{:S(2)}) collective-permute-start(bf16[3,64,512]{2,1,0:T(8,128)(2,1)S(1)} %get-tuple-element.60), channel_id=1, source_target_pairs={{0,6},{1,7},{2,0},{3,1},{4,2},{5,3},{6,4},{7,5},{8,14},{9,15},{10,... | collective-permute-start | bytes 589832 | tf_op jit(solution)/shard_map/ppermute | solution.py:358
  120.0 1.9 %collective-permute-start.11 = (bf16[3,64,512]{2,1,0:T(8,128)(2,1)S(1)}, bf16[3,64,512]{2,1,0:T(8,128)(2,1)S(1)}, u32[]{:S(2)}, u32[]{:S(2)}) collective-permute-start(bf16[3,64,512]{2,1,0:T(8,128)(2,1)S(1)} %get-tuple-element.61), channel_id=1, source_target_pairs={{0,2},{1,3},{2,4},{3,5},{4,6},{5,7},{6,0},{7,1},{8,10},{9,11},{10,... | collective-permute-start | bytes 589832 | tf_op jit(solution)/shard_map/ppermute | solution.py:358
  122.0 0.7 collective-permute-start.12
  122.7 1.0 collective-permute-start.13
  123.7 0.2 collective-permute-done.9.refs_2_.refs_3_
  123.9 2.7 %collective-permute-done.10.refs_3_.refs_6_ = bf16[3,64,512]{2,1,0:T(8,128)(2,1)S(1)} collective-permute-done((bf16[3,64,512]{2,1,0:T(8,128)(2,1)S(1)}, bf16[3,64,512]{2,1,0:T(8,128)(2,1)S(1)}, u32[]{:S(2)}, u32[]{:S(2)}) %collective-permute-start.10) | collective-permute-done | bytes 196640 | tf_op jit(solution)/shard_map/ppermute | solution.py:358
  126.6 2.3 %collective-permute-done.11.refs_4_.refs_2_ = bf16[3,64,512]{2,1,0:T(8,128)(2,1)S(1)} collective-permute-done((bf16[3,64,512]{2,1,0:T(8,128)(2,1)S(1)}, bf16[3,64,512]{2,1,0:T(8,128)(2,1)S(1)}, u32[]{:S(2)}, u32[]{:S(2)}) %collective-permute-start.11) | collective-permute-done | bytes 196640 | tf_op jit(solution)/shard_map/ppermute | solution.py:358
  128.9 1.3 all-to-all-done.4.got
  130.2 1.3 place.1
  131.5 0.0 copy-start.2
  131.5 10.3 %all-to-all-start.5 = ((bf16[8,8,2048]{2,1,0:T(8,128)(2,1)}), bf16[8,8,2048]{2,1,0:T(8,128)(2,1)S(1)}, u32[]{:S(2)}, u32[]{:S(2)}) async-start(bf16[8,8,2048]{2,1,0:T(8,128)(2,1)} %place.1), calls=%async_computation.5 | async-start | bytes 524288 | tf_op jit(solution)/shard_map/all_to_all | solution.py:455
  141.8 0.2 select_reduce_fusion.1.source
  142.0 1.8 %finish.1 = (f32[4,64,512]{2,1,0:T(8,128)}, f32[4,64,512]{2,1,0:T(8,128)}, bf16[4,64,512]{2,1,0:T(8,128)(2,1)}) custom-call(s32[8]{0:T(128)S(1)} %select_reduce_fusion.1.source, f32[4,64,512]{2,1,0:T(8,128)S(1)} %bitcast.17, f32[4,64,512]{2,1,0:T(8,128)S(1)} %bitcast.18, bf16[3,64,512]{2,1,0:T(8,128)(2,1)S(1)} %get-tuple-element.65.refs_0_, ...), custom_call_target="tpu_custom_call" | custom-call | bytes 3932160 | tf_op jit(solution)/shard_map/finish/pallas_call | solution.py:66
  143.8 4.5 %all-to-all-done.5 = bf16[8,8,2048]{2,1,0:T(8,128)(2,1)S(1)} async-done(((bf16[8,8,2048]{2,1,0:T(8,128)(2,1)}), bf16[8,8,2048]{2,1,0:T(8,128)(2,1)S(1)}, u32[]{:S(2)}, u32[]{:S(2)}) %all-to-all-start.5) | async-done | bytes 262176 | tf_op jit(solution)/shard_map/all_to_all | solution.py:455
  148.3 0.8 fusion
  (20 shorter events, 0.1 us)
Async XLA Ops:
  0.6 12.0 %copy-start = (bf16[64,2048]{1,0:T(8,128)(2,1)S(1)}, bf16[64,2048]{1,0:T(8,128)(2,1)}, u32[]{:S(2)}) copy-start(bf16[64,2048]{1,0:T(8,128)(2,1)} %grad.1) | copy-start | bytes 786436
  0.6 16.9 %all-to-all-start = ((bf16[8,8,2048]{2,1,0:T(8,128)(2,1)}), bf16[8,8,2048]{2,1,0:T(8,128)(2,1)S(1)}, u32[]{:S(2)}, u32[]{:S(2)}) async-start(bf16[8,8,2048]{2,1,0:T(8,128)(2,1)} %bitcast.16), calls=%async_computation | async-start | bytes 524288 | tf_op jit(solution)/shard_map/all_to_all | solution.py:367
  11.0 0.7 copy-start.9
  12.6 1.0 copy-start.1
  18.9 10.7 %copy-start.4 = (bf16[1,4,64,512]{3,2,1,0:T(8,128)(2,1)S(1)}, bf16[1,4,64,512]{3,2,1,0:T(8,128)(2,1)}, u32[]{:S(2)}) copy-start(bf16[1,4,64,512]{3,2,1,0:T(8,128)(2,1)} %param.13) | copy-start | bytes 786436
  19.0 10.7 %copy-start.5 = (bf16[1,4,64,512]{3,2,1,0:T(8,128)(2,1)S(1)}, bf16[1,4,64,512]{3,2,1,0:T(8,128)(2,1)}, u32[]{:S(2)}) copy-start(bf16[1,4,64,512]{3,2,1,0:T(8,128)(2,1)} %param.14) | copy-start | bytes 786436
  19.0 10.7 %copy-start.6 = (bf16[1,4,64,512]{3,2,1,0:T(8,128)(2,1)S(1)}, bf16[1,4,64,512]{3,2,1,0:T(8,128)(2,1)}, u32[]{:S(2)}) copy-start(bf16[1,4,64,512]{3,2,1,0:T(8,128)(2,1)} %param.15) | copy-start | bytes 786436
  19.0 34.5 %all-to-all-start.1 = ((bf16[16,17,8,128]{3,2,1,0:T(8,128)(2,1)}), bf16[16,17,8,128]{3,2,1,0:T(8,128)(2,1)S(1)}, u32[]{:S(2)}, u32[]{:S(2)}) async-start(bf16[16,17,8,128]{3,2,1,0:T(8,128)(2,1)} %spread.1.after), calls=%async_computation.1 | async-start | bytes 1114112 | tf_op jit(solution)/shard_map/all_to_all | solution.py:386
  30.3 0.7 copy-start.7
  31.0 15.5 %collective-permute-start = (bf16[3,64,512]{2,1,0:T(8,128)(2,1)S(1)}, bf16[3,64,512]{2,1,0:T(8,128)(2,1)S(1)}, u32[]{:S(2)}, u32[]{:S(2)}) collective-permute-start(bf16[3,64,512]{2,1,0:T(8,128)(2,1)S(1)} %get-tuple-element.38), channel_id=1, source_target_pairs={{0,4},{1,5},{2,6},{3,7},{4,0},{5,1},{6,2},{7,3},{8,12},{9,13},{10,... | collective-permute-start | bytes 589832 | tf_op jit(solution)/shard_map/ppermute | solution.py:358
  34.0 14.1 %collective-permute-start.1 = (bf16[3,64,512]{2,1,0:T(8,128)(2,1)S(1)}, bf16[3,64,512]{2,1,0:T(8,128)(2,1)S(1)}, u32[]{:S(2)}, u32[]{:S(2)}) collective-permute-start(bf16[3,64,512]{2,1,0:T(8,128)(2,1)S(1)} %get-tuple-element.39), channel_id=1, source_target_pairs={{0,5},{1,6},{2,7},{3,0},{4,1},{5,2},{6,3},{7,4},{8,13},{9,14},{10,... | collective-permute-start | bytes 589832 | tf_op jit(solution)/shard_map/ppermute | solution.py:358
  39.0 9.9 %collective-permute-start.2 = (bf16[3,64,512]{2,1,0:T(8,128)(2,1)S(1)}, bf16[3,64,512]{2,1,0:T(8,128)(2,1)S(1)}, u32[]{:S(2)}, u32[]{:S(2)}) collective-permute-start(bf16[3,64,512]{2,1,0:T(8,128)(2,1)S(1)} %get-tuple-element.40), channel_id=1, source_target_pairs={{0,3},{1,4},{2,5},{3,6},{4,7},{5,0},{6,1},{7,2},{8,11},{9,12},{10,... | collective-permute-start | bytes 589832 | tf_op jit(solution)/shard_map/ppermute | solution.py:358
  41.2 9.7 %collective-permute-start.3 = (bf16[3,64,512]{2,1,0:T(8,128)(2,1)S(1)}, bf16[3,64,512]{2,1,0:T(8,128)(2,1)S(1)}, u32[]{:S(2)}, u32[]{:S(2)}) collective-permute-start(bf16[3,64,512]{2,1,0:T(8,128)(2,1)S(1)} %get-tuple-element.41), channel_id=1, source_target_pairs={{0,6},{1,7},{2,0},{3,1},{4,2},{5,3},{6,4},{7,5},{8,14},{9,15},{10,... | collective-permute-start | bytes 589832 | tf_op jit(solution)/shard_map/ppermute | solution.py:358
  44.6 7.9 %collective-permute-start.4 = (bf16[3,64,512]{2,1,0:T(8,128)(2,1)S(1)}, bf16[3,64,512]{2,1,0:T(8,128)(2,1)S(1)}, u32[]{:S(2)}, u32[]{:S(2)}) collective-permute-start(bf16[3,64,512]{2,1,0:T(8,128)(2,1)S(1)} %get-tuple-element.42), channel_id=1, source_target_pairs={{0,2},{1,3},{2,4},{3,5},{4,6},{5,7},{6,0},{7,1},{8,10},{9,11},{10,... | collective-permute-start | bytes 589832 | tf_op jit(solution)/shard_map/ppermute | solution.py:358
  46.5 6.0 %collective-permute-start.5 = (bf16[3,64,512]{2,1,0:T(8,128)(2,1)S(1)}, bf16[3,64,512]{2,1,0:T(8,128)(2,1)S(1)}, u32[]{:S(2)}, u32[]{:S(2)}) collective-permute-start(bf16[3,64,512]{2,1,0:T(8,128)(2,1)S(1)} %get-tuple-element.43), channel_id=1, source_target_pairs={{0,7},{1,0},{2,1},{3,2},{4,3},{5,4},{6,5},{7,6},{8,15},{9,8},{10,9... | collective-permute-start | bytes 589832 | tf_op jit(solution)/shard_map/ppermute | solution.py:358
  48.1 5.2 %collective-permute-start.6 = (bf16[3,64,512]{2,1,0:T(8,128)(2,1)S(1)}, bf16[3,64,512]{2,1,0:T(8,128)(2,1)S(1)}, u32[]{:S(2)}, u32[]{:S(2)}) collective-permute-start(bf16[3,64,512]{2,1,0:T(8,128)(2,1)S(1)} %get-tuple-element.44), channel_id=1, source_target_pairs={{0,1},{1,2},{2,3},{3,4},{4,5},{5,6},{6,7},{7,0},{8,9},{9,10},{10,1... | collective-permute-start | bytes 589832 | tf_op jit(solution)/shard_map/ppermute | solution.py:358
  54.4 24.6 %all-to-all-start.2 = ((bf16[32,9,8,128]{3,2,1,0:T(8,128)(2,1)}), bf16[32,9,8,128]{3,2,1,0:T(8,128)(2,1)S(1)}, u32[]{:S(2)}, u32[]{:S(2)}) async-start(bf16[32,9,8,128]{3,2,1,0:T(8,128)(2,1)} %plane.1), calls=%async_computation.2 | async-start | bytes 1179648 | tf_op jit(solution)/shard_map/all_to_all | solution.py:398
  68.1 0.9 copy-start.8
  81.2 16.4 %all-to-all-start.3 = ((bf16[32,9,8,128]{3,2,1,0:T(8,128)(2,1)}), bf16[32,9,8,128]{3,2,1,0:T(8,128)(2,1)S(1)}, u32[]{:S(2)}, u32[]{:S(2)}) async-start(bf16[32,9,8,128]{3,2,1,0:T(8,128)(2,1)} %block.1.moment), calls=%async_computation.3 | async-start | bytes 1179648 | tf_op jit(solution)/shard_map/all_to_all | solution.py:422
  98.6 31.6 %all-to-all-start.4 = ((bf16[16,17,8,128]{3,2,1,0:T(8,128)(2,1)}), bf16[16,17,8,128]{3,2,1,0:T(8,128)(2,1)S(1)}, u32[]{:S(2)}, u32[]{:S(2)}) async-start(bf16[16,17,8,128]{3,2,1,0:T(8,128)(2,1)} %get-tuple-element.56), calls=%async_computation.4 | async-start | bytes 1114112 | tf_op jit(solution)/shard_map/all_to_all | solution.py:441
  106.2 15.8 %collective-permute-start.7 = (bf16[3,64,512]{2,1,0:T(8,128)(2,1)S(1)}, bf16[3,64,512]{2,1,0:T(8,128)(2,1)S(1)}, u32[]{:S(2)}, u32[]{:S(2)}) collective-permute-start(bf16[3,64,512]{2,1,0:T(8,128)(2,1)S(1)} %get-tuple-element.57), channel_id=1, source_target_pairs={{0,4},{1,5},{2,6},{3,7},{4,0},{5,1},{6,2},{7,3},{8,12},{9,13},{10,... | collective-permute-start | bytes 589832 | tf_op jit(solution)/shard_map/ppermute | solution.py:358
  108.9 13.8 %collective-permute-start.8 = (bf16[3,64,512]{2,1,0:T(8,128)(2,1)S(1)}, bf16[3,64,512]{2,1,0:T(8,128)(2,1)S(1)}, u32[]{:S(2)}, u32[]{:S(2)}) collective-permute-start(bf16[3,64,512]{2,1,0:T(8,128)(2,1)S(1)} %get-tuple-element.58), channel_id=1, source_target_pairs={{0,5},{1,6},{2,7},{3,0},{4,1},{5,2},{6,3},{7,4},{8,13},{9,14},{10,... | collective-permute-start | bytes 589832 | tf_op jit(solution)/shard_map/ppermute | solution.py:358
  113.6 10.3 %collective-permute-start.9 = (bf16[3,64,512]{2,1,0:T(8,128)(2,1)S(1)}, bf16[3,64,512]{2,1,0:T(8,128)(2,1)S(1)}, u32[]{:S(2)}, u32[]{:S(2)}) collective-permute-start(bf16[3,64,512]{2,1,0:T(8,128)(2,1)S(1)} %get-tuple-element.59), channel_id=1, source_target_pairs={{0,3},{1,4},{2,5},{3,6},{4,7},{5,0},{6,1},{7,2},{8,11},{9,12},{10,... | collective-permute-start | bytes 589832 | tf_op jit(solution)/shard_map/ppermute | solution.py:358
  116.0 10.6 %collective-permute-start.10 = (bf16[3,64,512]{2,1,0:T(8,128)(2,1)S(1)}, bf16[3,64,512]{2,1,0:T(8,128)(2,1)S(1)}, u32[]{:S(2)}, u32[]{:S(2)}) collective-permute-start(bf16[3,64,512]{2,1,0:T(8,128)(2,1)S(1)} %get-tuple-element.60), channel_id=1, source_target_pairs={{0,6},{1,7},{2,0},{3,1},{4,2},{5,3},{6,4},{7,5},{8,14},{9,15},{10,... | collective-permute-start | bytes 589832 | tf_op jit(solution)/shard_map/ppermute | solution.py:358
  120.0 8.8 %collective-permute-start.11 = (bf16[3,64,512]{2,1,0:T(8,128)(2,1)S(1)}, bf16[3,64,512]{2,1,0:T(8,128)(2,1)S(1)}, u32[]{:S(2)}, u32[]{:S(2)}) collective-permute-start(bf16[3,64,512]{2,1,0:T(8,128)(2,1)S(1)} %get-tuple-element.61), channel_id=1, source_target_pairs={{0,2},{1,3},{2,4},{3,5},{4,6},{5,7},{6,0},{7,1},{8,10},{9,11},{10,... | collective-permute-start | bytes 589832 | tf_op jit(solution)/shard_map/ppermute | solution.py:358
  122.0 6.9 %collective-permute-start.12 = (bf16[3,64,512]{2,1,0:T(8,128)(2,1)S(1)}, bf16[3,64,512]{2,1,0:T(8,128)(2,1)S(1)}, u32[]{:S(2)}, u32[]{:S(2)}) collective-permute-start(bf16[3,64,512]{2,1,0:T(8,128)(2,1)S(1)} %get-tuple-element.62), channel_id=1, source_target_pairs={{0,7},{1,0},{2,1},{3,2},{4,3},{5,4},{6,5},{7,6},{8,15},{9,8},{10,9... | collective-permute-start | bytes 589832 | tf_op jit(solution)/shard_map/ppermute | solution.py:358
  122.7 6.2 %collective-permute-start.13 = (bf16[3,64,512]{2,1,0:T(8,128)(2,1)S(1)}, bf16[3,64,512]{2,1,0:T(8,128)(2,1)S(1)}, u32[]{:S(2)}, u32[]{:S(2)}) collective-permute-start(bf16[3,64,512]{2,1,0:T(8,128)(2,1)S(1)} %get-tuple-element.63), channel_id=1, source_target_pairs={{0,1},{1,2},{2,3},{3,4},{4,5},{5,6},{6,7},{7,0},{8,9},{9,10},{10,1... | collective-permute-start | bytes 589832 | tf_op jit(solution)/shard_map/ppermute | solution.py:358
  130.2 11.8 %copy-start.3 = (f32[1,4,64,512]{3,2,1,0:T(8,128)S(1)}, f32[1,4,64,512]{3,2,1,0:T(8,128)}, u32[]{:S(2)}) copy-start(f32[1,4,64,512]{3,2,1,0:T(8,128)} %param.12) | copy-start | bytes 1572868
  131.5 10.5 %copy-start.2 = (f32[1,4,64,512]{3,2,1,0:T(8,128)S(1)}, f32[1,4,64,512]{3,2,1,0:T(8,128)}, u32[]{:S(2)}) copy-start(f32[1,4,64,512]{3,2,1,0:T(8,128)} %param.11) | copy-start | bytes 1572868
  131.5 16.8 %all-to-all-start.5 = ((bf16[8,8,2048]{2,1,0:T(8,128)(2,1)}), bf16[8,8,2048]{2,1,0:T(8,128)(2,1)S(1)}, u32[]{:S(2)}, u32[]{:S(2)}) async-start(bf16[8,8,2048]{2,1,0:T(8,128)(2,1)} %place.1), calls=%async_computation.5 | async-start | bytes 524288 | tf_op jit(solution)/shard_map/all_to_all | solution.py:455

commit v4 on v3

--- a/solution.py
+++ b/solution.py
@@ -169,11 +169,11 @@
 
 
 def pack_body(to, left, right, moment, after, *outs):
-    for s in range(MD):
+    for s in range(1, MD):
         t = to[s]
-        outs[s][0] = left[t]
-        outs[s][1] = right[t]
-        outs[s][2] = moment[t]
+        outs[s - 1][0] = left[t]
+        outs[s - 1][1] = right[t]
+        outs[s - 1][2] = moment[t]
 
 
 def plane_body(got, *refs):
@@ -194,13 +194,13 @@
     stream(fill, out, buffer, sems)
 
 
-def roots_body(other, *refs):
-    parts, outs = refs[:MD], refs[MD:]
+def roots_body(other, to, left, right, moment, *refs):
+    parts, outs = refs[: MD - 1], refs[MD - 1 :]
     for s in range(MD):
         source = lax.rem(other[0] - s + MD, MD)
         rows = pl.ds(pl.multiple_of(source * ROW_DEV, ROW_DEV), ROW_DEV)
-        for i in range(3):
-            outs[i][rows, :] = parts[s][i]
+        for i, own in enumerate((left, right, moment)):
+            outs[i][rows, :] = parts[s - 1][i] if s else own[to[0]]
 
 
 def assemble(got, block):
@@ -378,15 +378,13 @@
     packed = call(
         pack_body,
         "svvva",
-        [struct(3, ROW_DEV, BLK)] * MD,
+        [struct(3, ROW_DEV, BLK)] * (MD - 1),
         [to, left_root[0], right_root[0], momentum[0], pay],
         name="pack",
         prefetch=True,
     )
     got = lax.all_to_all(pay, "z", 0, 0, tiled=True)
-    moved = {0: packed[0]}
-    for s in SHIFTS:
-        moved[s] = shift(packed[s], s)
+    moved = {s: shift(packed[s - 1], s) for s in SHIFTS}
     (pay,) = call(
         plane_body,
         "v" + "a" * len(SHIFTS),
@@ -398,9 +396,9 @@
     got = lax.all_to_all(pay, ("y", "m"), 0, 0, tiled=True)
     left, right, old = call(
         roots_body,
-        "s" + "v" * MD,
+        "ssvvv" + "v" * (MD - 1),
         [struct(*square)] * 3,
-        [other, *(moved[s] for s in range(MD))],
+        [other, to, left_root[0], right_root[0], momentum[0], *(moved[s] for s in range(1, MD))],
         name="roots",
     )
     whole = got

time: 150 us -> 152 us (1.013)
  local copies, waits for them, and re-layouts: 3.41 us -> 5.48 us
    unnamed x20 -> x24, local copies, waits for them, and re-layouts: 3.33 us -> 5.4 us
  transfers between devices with their start and end apart: 20 -> 20, of which waited for: 13 -> 13; matrix products, arithmetic and copies ran while one was open for 1% -> 1% of each run, Pallas kernels for 4% -> 5%
where the time goes in v4:
time: 152 us; the launch traced here: 150 us
  starting transfers between devices  89.3 us (59%)
  waiting for transfers between devices  37.7 us (25%)
  Pallas kernels  13.6 us (9%)
  local copies, waits for them, and re-layouts  5.48 us (4%)
  other arithmetic  2.82 us (2%)
  between operations  1.6 us (1%)
    ppermute x14, starting transfers between devices, shift(): return lax.ppermute(part, 'm', [(i, (i + s) % MD) for i in range(MD)])  34.7 us
    all_to_all x2, starting transfers between devices, shards(): got = lax.all_to_all(pay, 'z', 0, 0, tiled=True)  17.6 us
    all_to_all x1, starting transfers between devices, shards(): got = lax.all_to_all(pay, ('y', 'm'), 0, 0, tiled=True)  12.3 us
    pallas_call x10, Pallas kernels, call(): pl.pallas_call(body, out_shape=tuple(outs), grid_spec=pltpu.PrefetchScala...  11.8 us
    all_to_all x1, waiting for transfers between devices, shards(): got = lax.all_to_all(back, ('y', 'm'), 0, 0, tiled=True)  10.4 us
    all_to_all x1, starting transfers between devices, shards(): lax.all_to_all(gradient.reshape(MD, SUB, LOCAL), 'm', 0, 0, tiled=True)  10.3 us
    all_to_all x1, starting transfers between devices, shards(): placed = lax.all_to_all(pay, 'm', 0, 0, tiled=True).reshape(ROW_DEV, LOCAL)  10.3 us
    ppermute x14, waiting for transfers between devices, shift(): return lax.ppermute(part, 'm', [(i, (i + s) % MD) for i in range(MD)])  10.2 us
  transfers between devices with their start and end apart: 20, of which 13 were waited for; matrix products, arithmetic and copies ran while one was open for 1% of the time, Pallas kernels for 5%

profile of v4, /device:TPU:1, one launch (start us, length us, event | category | flops | bytes accessed | tf_op | source)
XLA Modules:
  0.0 150.5 jit_solution(742492306494980192)
XLA Ops:
  0.6 10.3 %all-to-all-start = ((bf16[8,8,2048]{2,1,0:T(8,128)(2,1)}), bf16[8,8,2048]{2,1,0:T(8,128)(2,1)S(1)}, u32[]{:S(2)}, u32[]{:S(2)}) async-start(bf16[8,8,2048]{2,1,0:T(8,128)(2,1)} %bitcast.16), calls=%async_computation | async-start | bytes 524288 | tf_op jit(solution)/shard_map/all_to_all | solution.py:367
  11.0 0.7 copy-done.11
  11.7 0.1 reshape.77
  11.7 0.1 convert_reduce_fusion
  11.9 0.1 select_reduce_fusion.3
  12.0 0.6 compare_select_fusion.4
  12.7 1.0 copy-done.4
  13.7 1.7 %adam.1 = (f32[64,2048]{1,0:T(8,128)}, bf16[8,128]{1,0:T(8,128)(2,1)S(1)}) custom-call(s32[1]{0:T(128)} %bitcast.1.index.other, bf16[64,2048]{1,0:T(8,128)(2,1)S(1)} %copy-done, f32[64,2048]{1,0:T(8,128)S(1)} %copy-done.4), custom_call_target="tpu_custom_call" | custom-call | tf_op jit(solution)/shard_map/adam/pallas_call | solution.py:146
  15.4 0.1 select_reduce_fusion.inverse
  15.5 0.2 select_reduce_fusion.2.before.to
  15.7 1.8 %all-to-all-done.got = bf16[8,8,2048]{2,1,0:T(8,128)(2,1)S(1)} async-done(((bf16[8,8,2048]{2,1,0:T(8,128)(2,1)}), bf16[8,8,2048]{2,1,0:T(8,128)(2,1)S(1)}, u32[]{:S(2)}, u32[]{:S(2)}) %all-to-all-start) | async-done | bytes 262176 | tf_op jit(solution)/shard_map/all_to_all | solution.py:367
  17.5 1.4 spread.1.after
  18.9 0.0 copy-start.1
  19.0 0.0 copy-start.2
  19.0 0.0 copy-start.3
  19.0 10.6 %all-to-all-start.1 = ((bf16[16,17,8,128]{3,2,1,0:T(8,128)(2,1)}), bf16[16,17,8,128]{3,2,1,0:T(8,128)(2,1)S(1)}, u32[]{:S(2)}, u32[]{:S(2)}) async-start(bf16[16,17,8,128]{3,2,1,0:T(8,128)(2,1)} %spread.1.after), calls=%async_computation.1 | async-start | bytes 1114112 | tf_op jit(solution)/shard_map/all_to_all | solution.py:386
  29.7 0.6 pack.1
  30.3 3.0 %collective-permute-start = (bf16[3,64,512]{2,1,0:T(8,128)(2,1)S(1)}, bf16[3,64,512]{2,1,0:T(8,128)(2,1)S(1)}, u32[]{:S(2)}, u32[]{:S(2)}) collective-permute-start(bf16[3,64,512]{2,1,0:T(8,128)(2,1)S(1)} %get-tuple-element.37), channel_id=1, source_target_pairs={{0,4},{1,5},{2,6},{3,7},{4,0},{5,1},{6,2},{7,3},{8,12},{9,13},{10,... | collective-permute-start | bytes 589832 | tf_op jit(solution)/shard_map/ppermute | solution.py:358
  33.3 5.0 %collective-permute-start.1 = (bf16[3,64,512]{2,1,0:T(8,128)(2,1)S(1)}, bf16[3,64,512]{2,1,0:T(8,128)(2,1)S(1)}, u32[]{:S(2)}, u32[]{:S(2)}) collective-permute-start(bf16[3,64,512]{2,1,0:T(8,128)(2,1)S(1)} %get-tuple-element.38), channel_id=1, source_target_pairs={{0,5},{1,6},{2,7},{3,0},{4,1},{5,2},{6,3},{7,4},{8,13},{9,14},{10,... | collective-permute-start | bytes 589832 | tf_op jit(solution)/shard_map/ppermute | solution.py:358
  38.3 2.2 %collective-permute-start.2 = (bf16[3,64,512]{2,1,0:T(8,128)(2,1)S(1)}, bf16[3,64,512]{2,1,0:T(8,128)(2,1)S(1)}, u32[]{:S(2)}, u32[]{:S(2)}) collective-permute-start(bf16[3,64,512]{2,1,0:T(8,128)(2,1)S(1)} %get-tuple-element.39), channel_id=1, source_target_pairs={{0,3},{1,4},{2,5},{3,6},{4,7},{5,0},{6,1},{7,2},{8,11},{9,12},{10,... | collective-permute-start | bytes 589832 | tf_op jit(solution)/shard_map/ppermute | solution.py:358
  40.5 3.4 %collective-permute-start.3 = (bf16[3,64,512]{2,1,0:T(8,128)(2,1)S(1)}, bf16[3,64,512]{2,1,0:T(8,128)(2,1)S(1)}, u32[]{:S(2)}, u32[]{:S(2)}) collective-permute-start(bf16[3,64,512]{2,1,0:T(8,128)(2,1)S(1)} %get-tuple-element.40), channel_id=1, source_target_pairs={{0,6},{1,7},{2,0},{3,1},{4,2},{5,3},{6,4},{7,5},{8,14},{9,15},{10,... | collective-permute-start | bytes 589832 | tf_op jit(solution)/shard_map/ppermute | solution.py:358
  43.9 1.9 %collective-permute-start.4 = (bf16[3,64,512]{2,1,0:T(8,128)(2,1)S(1)}, bf16[3,64,512]{2,1,0:T(8,128)(2,1)S(1)}, u32[]{:S(2)}, u32[]{:S(2)}) collective-permute-start(bf16[3,64,512]{2,1,0:T(8,128)(2,1)S(1)} %get-tuple-element.41), channel_id=1, source_target_pairs={{0,2},{1,3},{2,4},{3,5},{4,6},{5,7},{6,0},{7,1},{8,10},{9,11},{10,... | collective-permute-start | bytes 589832 | tf_op jit(solution)/shard_map/ppermute | solution.py:358
  45.8 0.0 collective-permute-done.refs_0_.refs_3_
  45.8 1.6 %collective-permute-start.5 = (bf16[3,64,512]{2,1,0:T(8,128)(2,1)S(1)}, bf16[3,64,512]{2,1,0:T(8,128)(2,1)S(1)}, u32[]{:S(2)}, u32[]{:S(2)}) collective-permute-start(bf16[3,64,512]{2,1,0:T(8,128)(2,1)S(1)} %get-tuple-element.42), channel_id=1, source_target_pairs={{0,7},{1,0},{2,1},{3,2},{4,3},{5,4},{6,5},{7,6},{8,15},{9,8},{10,9... | collective-permute-start | bytes 589832 | tf_op jit(solution)/shard_map/ppermute | solution.py:358
  47.4 0.2 collective-permute-start.6
  47.6 0.6 collective-permute-done.2.refs_2_
  48.2 2.1 %collective-permute-done.3.refs_3_.refs_5_ = bf16[3,64,512]{2,1,0:T(8,128)(2,1)S(1)} collective-permute-done((bf16[3,64,512]{2,1,0:T(8,128)(2,1)S(1)}, bf16[3,64,512]{2,1,0:T(8,128)(2,1)S(1)}, u32[]{:S(2)}, u32[]{:S(2)}) %collective-permute-start.3) | collective-permute-done | bytes 196640 | tf_op jit(solution)/shard_map/ppermute | solution.py:358
  50.2 1.6 %collective-permute-done.4.refs_4_.refs_1_ = bf16[3,64,512]{2,1,0:T(8,128)(2,1)S(1)} collective-permute-done((bf16[3,64,512]{2,1,0:T(8,128)(2,1)S(1)}, bf16[3,64,512]{2,1,0:T(8,128)(2,1)S(1)}, u32[]{:S(2)}, u32[]{:S(2)}) %collective-permute-start.4) | collective-permute-done | bytes 196640 | tf_op jit(solution)/shard_map/ppermute | solution.py:358
  51.8 0.8 collective-permute-done.6.refs_6_.refs_0_
  52.6 0.9 all-to-all-done.1.got
  53.5 0.9 plane.1
  54.4 12.3 %all-to-all-start.2 = ((bf16[32,9,8,128]{3,2,1,0:T(8,128)(2,1)}), bf16[32,9,8,128]{3,2,1,0:T(8,128)(2,1)S(1)}, u32[]{:S(2)}, u32[]{:S(2)}) async-start(bf16[32,9,8,128]{3,2,1,0:T(8,128)(2,1)} %plane.1), calls=%async_computation.2 | async-start | bytes 1179648 | tf_op jit(solution)/shard_map/all_to_all | solution.py:396
  67.4 0.7 compare_select_fusion.5
  68.1 0.7 roots.1
  68.7 0.0 copy-start.7
  68.8 0.8 copy-done.7
  69.5 0.8 copy-done.9
  70.3 8.7 %all-to-all-done.2.got = bf16[32,9,8,128]{3,2,1,0:T(8,128)(2,1)S(1)} async-done(((bf16[32,9,8,128]{3,2,1,0:T(8,128)(2,1)}), bf16[32,9,8,128]{3,2,1,0:T(8,128)(2,1)S(1)}, u32[]{:S(2)}, u32[]{:S(2)}) %all-to-all-start.2) | async-done | bytes 589856 | tf_op jit(solution)/shard_map/all_to_all | solution.py:396
  79.0 1.0 copy-done.8
  80.1 1.0 copy-done.10
  81.1 2.2 %block.1.moment = bf16[32,9,8,128]{3,2,1,0:T(8,128)(2,1)} custom-call(f32[8,128]{1,0:T(8,128)S(1)} %pad_select_fusion.masks, bf16[32,9,8,128]{3,2,1,0:T(8,128)(2,1)S(1)} %all-to-all-done.2.got, bf16[512,512]{1,0:T(8,128)(2,1)S(1)} %get-tuple-element.44.left, bf16[512,512]{1,0:T(8,128)(2,1)S(1)} %copy-done.8, bf16[512,512]{1,0:T(8,128)(2,1)S(1)} %copy-done.10), custom_call_target="tpu_custom_call" | custom-call | flops 536870912 | bytes 2756608 | tf_op jit(solution)/shard_map/block/pallas_call | solution.py:66
  83.3 4.1 %all-to-all-start.3 = ((bf16[32,9,8,128]{3,2,1,0:T(8,128)(2,1)}), bf16[32,9,8,128]{3,2,1,0:T(8,128)(2,1)S(1)}, u32[]{:S(2)}, u32[]{:S(2)}) async-start(bf16[32,9,8,128]{3,2,1,0:T(8,128)(2,1)} %block.1.moment), calls=%async_computation.3 | async-start | bytes 1179648 | tf_op jit(solution)/shard_map/all_to_all | solution.py:420
  87.4 2.0 %stats.1 = (bf16[3,64,512]{2,1,0:T(8,128)(2,1)S(1)}, bf16[3,64,512]{2,1,0:T(8,128)(2,1)S(1)}, bf16[3,64,512]{2,1,0:T(8,128)(2,1)S(1)}, bf16[3,64,512]{2,1,0:T(8,...) custom-call(s32[1]{0:T(128)} %bitcast.1.index.other, ...), custom_call_target="tpu_custom_call" | custom-call | flops 536870912 | bytes 2752512 | tf_op jit(solution)/shard_map/stats/pallas_call | solution.py:66
  89.3 10.4 %all-to-all-done.3.got = bf16[32,9,8,128]{3,2,1,0:T(8,128)(2,1)S(1)} async-done(((bf16[32,9,8,128]{3,2,1,0:T(8,128)(2,1)}), bf16[32,9,8,128]{3,2,1,0:T(8,128)(2,1)S(1)}, u32[]{:S(2)}, u32[]{:S(2)}) %all-to-all-start.3) | async-done | bytes 589856 | tf_op jit(solution)/shard_map/all_to_all | solution.py:420
  99.7 0.9 unplane.1
  100.6 6.9 %all-to-all-start.4 = ((bf16[16,17,8,128]{3,2,1,0:T(8,128)(2,1)}), bf16[16,17,8,128]{3,2,1,0:T(8,128)(2,1)S(1)}, u32[]{:S(2)}, u32[]{:S(2)}) async-start(bf16[16,17,8,128]{3,2,1,0:T(8,128)(2,1)} %get-tuple-element.54), calls=%async_computation.4 | async-start | bytes 1114112 | tf_op jit(solution)/shard_map/all_to_all | solution.py:439
  107.6 2.7 %collective-permute-start.7 = (bf16[3,64,512]{2,1,0:T(8,128)(2,1)S(1)}, bf16[3,64,512]{2,1,0:T(8,128)(2,1)S(1)}, u32[]{:S(2)}, u32[]{:S(2)}) collective-permute-start(bf16[3,64,512]{2,1,0:T(8,128)(2,1)S(1)} %get-tuple-element.55), channel_id=1, source_target_pairs={{0,4},{1,5},{2,6},{3,7},{4,0},{5,1},{6,2},{7,3},{8,12},{9,13},{10,... | collective-permute-start | bytes 589832 | tf_op jit(solution)/shard_map/ppermute | solution.py:358
  110.3 4.6 %collective-permute-start.8 = (bf16[3,64,512]{2,1,0:T(8,128)(2,1)S(1)}, bf16[3,64,512]{2,1,0:T(8,128)(2,1)S(1)}, u32[]{:S(2)}, u32[]{:S(2)}) collective-permute-start(bf16[3,64,512]{2,1,0:T(8,128)(2,1)S(1)} %get-tuple-element.56), channel_id=1, source_target_pairs={{0,5},{1,6},{2,7},{3,0},{4,1},{5,2},{6,3},{7,4},{8,13},{9,14},{10,... | collective-permute-start | bytes 589832 | tf_op jit(solution)/shard_map/ppermute | solution.py:358
  114.9 2.4 %collective-permute-start.9 = (bf16[3,64,512]{2,1,0:T(8,128)(2,1)S(1)}, bf16[3,64,512]{2,1,0:T(8,128)(2,1)S(1)}, u32[]{:S(2)}, u32[]{:S(2)}) collective-permute-start(bf16[3,64,512]{2,1,0:T(8,128)(2,1)S(1)} %get-tuple-element.57), channel_id=1, source_target_pairs={{0,3},{1,4},{2,5},{3,6},{4,7},{5,0},{6,1},{7,2},{8,11},{9,12},{10,... | collective-permute-start | bytes 589832 | tf_op jit(solution)/shard_map/ppermute | solution.py:358
  117.4 4.0 %collective-permute-start.10 = (bf16[3,64,512]{2,1,0:T(8,128)(2,1)S(1)}, bf16[3,64,512]{2,1,0:T(8,128)(2,1)S(1)}, u32[]{:S(2)}, u32[]{:S(2)}) collective-permute-start(bf16[3,64,512]{2,1,0:T(8,128)(2,1)S(1)} %get-tuple-element.58), channel_id=1, source_target_pairs={{0,6},{1,7},{2,0},{3,1},{4,2},{5,3},{6,4},{7,5},{8,14},{9,15},{10,... | collective-permute-start | bytes 589832 | tf_op jit(solution)/shard_map/ppermute | solution.py:358
  121.4 1.9 %collective-permute-start.11 = (bf16[3,64,512]{2,1,0:T(8,128)(2,1)S(1)}, bf16[3,64,512]{2,1,0:T(8,128)(2,1)S(1)}, u32[]{:S(2)}, u32[]{:S(2)}) collective-permute-start(bf16[3,64,512]{2,1,0:T(8,128)(2,1)S(1)} %get-tuple-element.59), channel_id=1, source_target_pairs={{0,2},{1,3},{2,4},{3,5},{4,6},{5,7},{6,0},{7,1},{8,10},{9,11},{10,... | collective-permute-start | bytes 589832 | tf_op jit(solution)/shard_map/ppermute | solution.py:358
  123.3 0.7 collective-permute-start.12
  124.1 1.0 collective-permute-start.13
  125.1 0.2 collective-permute-done.9.refs_2_.refs_3_
  125.3 2.7 %collective-permute-done.10.refs_3_.refs_6_ = bf16[3,64,512]{2,1,0:T(8,128)(2,1)S(1)} collective-permute-done((bf16[3,64,512]{2,1,0:T(8,128)(2,1)S(1)}, bf16[3,64,512]{2,1,0:T(8,128)(2,1)S(1)}, u32[]{:S(2)}, u32[]{:S(2)}) %collective-permute-start.10) | collective-permute-done | bytes 196640 | tf_op jit(solution)/shard_map/ppermute | solution.py:358
  128.0 2.3 %collective-permute-done.11.refs_4_.refs_2_ = bf16[3,64,512]{2,1,0:T(8,128)(2,1)S(1)} collective-permute-done((bf16[3,64,512]{2,1,0:T(8,128)(2,1)S(1)}, bf16[3,64,512]{2,1,0:T(8,128)(2,1)S(1)}, u32[]{:S(2)}, u32[]{:S(2)}) %collective-permute-start.11) | collective-permute-done | bytes 196640 | tf_op jit(solution)/shard_map/ppermute | solution.py:358
  130.2 1.3 all-to-all-done.4.got
  131.5 1.3 place.1
  132.8 0.0 copy-start.5
  132.9 10.3 %all-to-all-start.5 = ((bf16[8,8,2048]{2,1,0:T(8,128)(2,1)}), bf16[8,8,2048]{2,1,0:T(8,128)(2,1)S(1)}, u32[]{:S(2)}, u32[]{:S(2)}) async-start(bf16[8,8,2048]{2,1,0:T(8,128)(2,1)} %place.1), calls=%async_computation.5 | async-start | bytes 524288 | tf_op jit(solution)/shard_map/all_to_all | solution.py:453
  143.2 0.2 select_reduce_fusion.1.source
  143.4 1.8 %finish.1 = (f32[4,64,512]{2,1,0:T(8,128)}, f32[4,64,512]{2,1,0:T(8,128)}, bf16[4,64,512]{2,1,0:T(8,128)(2,1)}) custom-call(s32[8]{0:T(128)S(1)} %select_reduce_fusion.1.source, f32[4,64,512]{2,1,0:T(8,128)S(1)} %bitcast.23, f32[4,64,512]{2,1,0:T(8,128)S(1)} %bitcast.24, bf16[3,64,512]{2,1,0:T(8,128)(2,1)S(1)} %get-tuple-element.63.refs_0_, ...), custom_call_target="tpu_custom_call" | custom-call | bytes 3932160 | tf_op jit(solution)/shard_map/finish/pallas_call | solution.py:66
  145.2 4.5 %all-to-all-done.5 = bf16[8,8,2048]{2,1,0:T(8,128)(2,1)S(1)} async-done(((bf16[8,8,2048]{2,1,0:T(8,128)(2,1)}), bf16[8,8,2048]{2,1,0:T(8,128)(2,1)S(1)}, u32[]{:S(2)}, u32[]{:S(2)}) %all-to-all-start.5) | async-done | bytes 262176 | tf_op jit(solution)/shard_map/all_to_all | solution.py:453
  149.7 0.8 fusion
  (24 shorter events, 0.1 us)
Async XLA Ops:
  0.6 12.0 %copy-start = (bf16[64,2048]{1,0:T(8,128)(2,1)S(1)}, bf16[64,2048]{1,0:T(8,128)(2,1)}, u32[]{:S(2)}) copy-start(bf16[64,2048]{1,0:T(8,128)(2,1)} %grad.1) | copy-start | bytes 786436
  0.6 16.9 %all-to-all-start = ((bf16[8,8,2048]{2,1,0:T(8,128)(2,1)}), bf16[8,8,2048]{2,1,0:T(8,128)(2,1)S(1)}, u32[]{:S(2)}, u32[]{:S(2)}) async-start(bf16[8,8,2048]{2,1,0:T(8,128)(2,1)} %bitcast.16), calls=%async_computation | async-start | bytes 524288 | tf_op jit(solution)/shard_map/all_to_all | solution.py:367
  11.0 0.7 copy-start.11
  12.6 1.0 copy-start.4
  18.9 10.7 %copy-start.1 = (bf16[1,4,64,512]{3,2,1,0:T(8,128)(2,1)S(1)}, bf16[1,4,64,512]{3,2,1,0:T(8,128)(2,1)}, u32[]{:S(2)}) copy-start(bf16[1,4,64,512]{3,2,1,0:T(8,128)(2,1)} %param.13) | copy-start | bytes 786436
  19.0 10.7 %copy-start.2 = (bf16[1,4,64,512]{3,2,1,0:T(8,128)(2,1)S(1)}, bf16[1,4,64,512]{3,2,1,0:T(8,128)(2,1)}, u32[]{:S(2)}) copy-start(bf16[1,4,64,512]{3,2,1,0:T(8,128)(2,1)} %param.14) | copy-start | bytes 786436
  19.0 10.7 %copy-start.3 = (bf16[1,4,64,512]{3,2,1,0:T(8,128)(2,1)S(1)}, bf16[1,4,64,512]{3,2,1,0:T(8,128)(2,1)}, u32[]{:S(2)}) copy-start(bf16[1,4,64,512]{3,2,1,0:T(8,128)(2,1)} %param.15) | copy-start | bytes 786436
  19.0 34.5 %all-to-all-start.1 = ((bf16[16,17,8,128]{3,2,1,0:T(8,128)(2,1)}), bf16[16,17,8,128]{3,2,1,0:T(8,128)(2,1)S(1)}, u32[]{:S(2)}, u32[]{:S(2)}) async-start(bf16[16,17,8,128]{3,2,1,0:T(8,128)(2,1)} %spread.1.after), calls=%async_computation.1 | async-start | bytes 1114112 | tf_op jit(solution)/shard_map/all_to_all | solution.py:386
  30.3 15.5 %collective-permute-start = (bf16[3,64,512]{2,1,0:T(8,128)(2,1)S(1)}, bf16[3,64,512]{2,1,0:T(8,128)(2,1)S(1)}, u32[]{:S(2)}, u32[]{:S(2)}) collective-permute-start(bf16[3,64,512]{2,1,0:T(8,128)(2,1)S(1)} %get-tuple-element.37), channel_id=1, source_target_pairs={{0,4},{1,5},{2,6},{3,7},{4,0},{5,1},{6,2},{7,3},{8,12},{9,13},{10,... | collective-permute-start | bytes 589832 | tf_op jit(solution)/shard_map/ppermute | solution.py:358
  33.3 14.1 %collective-permute-start.1 = (bf16[3,64,512]{2,1,0:T(8,128)(2,1)S(1)}, bf16[3,64,512]{2,1,0:T(8,128)(2,1)S(1)}, u32[]{:S(2)}, u32[]{:S(2)}) collective-permute-start(bf16[3,64,512]{2,1,0:T(8,128)(2,1)S(1)} %get-tuple-element.38), channel_id=1, source_target_pairs={{0,5},{1,6},{2,7},{3,0},{4,1},{5,2},{6,3},{7,4},{8,13},{9,14},{10,... | collective-permute-start | bytes 589832 | tf_op jit(solution)/shard_map/ppermute | solution.py:358
  38.3 9.9 %collective-permute-start.2 = (bf16[3,64,512]{2,1,0:T(8,128)(2,1)S(1)}, bf16[3,64,512]{2,1,0:T(8,128)(2,1)S(1)}, u32[]{:S(2)}, u32[]{:S(2)}) collective-permute-start(bf16[3,64,512]{2,1,0:T(8,128)(2,1)S(1)} %get-tuple-element.39), channel_id=1, source_target_pairs={{0,3},{1,4},{2,5},{3,6},{4,7},{5,0},{6,1},{7,2},{8,11},{9,12},{10,... | collective-permute-start | bytes 589832 | tf_op jit(solution)/shard_map/ppermute | solution.py:358
  40.5 9.7 %collective-permute-start.3 = (bf16[3,64,512]{2,1,0:T(8,128)(2,1)S(1)}, bf16[3,64,512]{2,1,0:T(8,128)(2,1)S(1)}, u32[]{:S(2)}, u32[]{:S(2)}) collective-permute-start(bf16[3,64,512]{2,1,0:T(8,128)(2,1)S(1)} %get-tuple-element.40), channel_id=1, source_target_pairs={{0,6},{1,7},{2,0},{3,1},{4,2},{5,3},{6,4},{7,5},{8,14},{9,15},{10,... | collective-permute-start | bytes 589832 | tf_op jit(solution)/shard_map/ppermute | solution.py:358
  43.9 7.9 %collective-permute-start.4 = (bf16[3,64,512]{2,1,0:T(8,128)(2,1)S(1)}, bf16[3,64,512]{2,1,0:T(8,128)(2,1)S(1)}, u32[]{:S(2)}, u32[]{:S(2)}) collective-permute-start(bf16[3,64,512]{2,1,0:T(8,128)(2,1)S(1)} %get-tuple-element.41), channel_id=1, source_target_pairs={{0,2},{1,3},{2,4},{3,5},{4,6},{5,7},{6,0},{7,1},{8,10},{9,11},{10,... | collective-permute-start | bytes 589832 | tf_op jit(solution)/shard_map/ppermute | solution.py:358
  45.8 6.0 %collective-permute-start.5 = (bf16[3,64,512]{2,1,0:T(8,128)(2,1)S(1)}, bf16[3,64,512]{2,1,0:T(8,128)(2,1)S(1)}, u32[]{:S(2)}, u32[]{:S(2)}) collective-permute-start(bf16[3,64,512]{2,1,0:T(8,128)(2,1)S(1)} %get-tuple-element.42), channel_id=1, source_target_pairs={{0,7},{1,0},{2,1},{3,2},{4,3},{5,4},{6,5},{7,6},{8,15},{9,8},{10,9... | collective-permute-start | bytes 589832 | tf_op jit(solution)/shard_map/ppermute | solution.py:358
  47.4 5.2 %collective-permute-start.6 = (bf16[3,64,512]{2,1,0:T(8,128)(2,1)S(1)}, bf16[3,64,512]{2,1,0:T(8,128)(2,1)S(1)}, u32[]{:S(2)}, u32[]{:S(2)}) collective-permute-start(bf16[3,64,512]{2,1,0:T(8,128)(2,1)S(1)} %get-tuple-element.43), channel_id=1, source_target_pairs={{0,1},{1,2},{2,3},{3,4},{4,5},{5,6},{6,7},{7,0},{8,9},{9,10},{10,1... | collective-permute-start | bytes 589832 | tf_op jit(solution)/shard_map/ppermute | solution.py:358
  54.4 24.6 %all-to-all-start.2 = ((bf16[32,9,8,128]{3,2,1,0:T(8,128)(2,1)}), bf16[32,9,8,128]{3,2,1,0:T(8,128)(2,1)S(1)}, u32[]{:S(2)}, u32[]{:S(2)}) async-start(bf16[32,9,8,128]{3,2,1,0:T(8,128)(2,1)} %plane.1), calls=%async_computation.2 | async-start | bytes 1179648 | tf_op jit(solution)/shard_map/all_to_all | solution.py:396
  68.7 0.8 copy-start.7
  69.5 0.8 copy-start.9
  79.0 1.0 copy-start.8
  80.1 1.0 copy-start.10
  83.3 16.4 %all-to-all-start.3 = ((bf16[32,9,8,128]{3,2,1,0:T(8,128)(2,1)}), bf16[32,9,8,128]{3,2,1,0:T(8,128)(2,1)S(1)}, u32[]{:S(2)}, u32[]{:S(2)}) async-start(bf16[32,9,8,128]{3,2,1,0:T(8,128)(2,1)} %block.1.moment), calls=%async_computation.3 | async-start | bytes 1179648 | tf_op jit(solution)/shard_map/all_to_all | solution.py:420
  100.6 30.9 %all-to-all-start.4 = ((bf16[16,17,8,128]{3,2,1,0:T(8,128)(2,1)}), bf16[16,17,8,128]{3,2,1,0:T(8,128)(2,1)S(1)}, u32[]{:S(2)}, u32[]{:S(2)}) async-start(bf16[16,17,8,128]{3,2,1,0:T(8,128)(2,1)} %get-tuple-element.54), calls=%async_computation.4 | async-start | bytes 1114112 | tf_op jit(solution)/shard_map/all_to_all | solution.py:439
  107.6 15.8 %collective-permute-start.7 = (bf16[3,64,512]{2,1,0:T(8,128)(2,1)S(1)}, bf16[3,64,512]{2,1,0:T(8,128)(2,1)S(1)}, u32[]{:S(2)}, u32[]{:S(2)}) collective-permute-start(bf16[3,64,512]{2,1,0:T(8,128)(2,1)S(1)} %get-tuple-element.55), channel_id=1, source_target_pairs={{0,4},{1,5},{2,6},{3,7},{4,0},{5,1},{6,2},{7,3},{8,12},{9,13},{10,... | collective-permute-start | bytes 589832 | tf_op jit(solution)/shard_map/ppermute | solution.py:358
  110.3 13.8 %collective-permute-start.8 = (bf16[3,64,512]{2,1,0:T(8,128)(2,1)S(1)}, bf16[3,64,512]{2,1,0:T(8,128)(2,1)S(1)}, u32[]{:S(2)}, u32[]{:S(2)}) collective-permute-start(bf16[3,64,512]{2,1,0:T(8,128)(2,1)S(1)} %get-tuple-element.56), channel_id=1, source_target_pairs={{0,5},{1,6},{2,7},{3,0},{4,1},{5,2},{6,3},{7,4},{8,13},{9,14},{10,... | collective-permute-start | bytes 589832 | tf_op jit(solution)/shard_map/ppermute | solution.py:358
  114.9 10.3 %collective-permute-start.9 = (bf16[3,64,512]{2,1,0:T(8,128)(2,1)S(1)}, bf16[3,64,512]{2,1,0:T(8,128)(2,1)S(1)}, u32[]{:S(2)}, u32[]{:S(2)}) collective-permute-start(bf16[3,64,512]{2,1,0:T(8,128)(2,1)S(1)} %get-tuple-element.57), channel_id=1, source_target_pairs={{0,3},{1,4},{2,5},{3,6},{4,7},{5,0},{6,1},{7,2},{8,11},{9,12},{10,... | collective-permute-start | bytes 589832 | tf_op jit(solution)/shard_map/ppermute | solution.py:358
  117.4 10.6 %collective-permute-start.10 = (bf16[3,64,512]{2,1,0:T(8,128)(2,1)S(1)}, bf16[3,64,512]{2,1,0:T(8,128)(2,1)S(1)}, u32[]{:S(2)}, u32[]{:S(2)}) collective-permute-start(bf16[3,64,512]{2,1,0:T(8,128)(2,1)S(1)} %get-tuple-element.58), channel_id=1, source_target_pairs={{0,6},{1,7},{2,0},{3,1},{4,2},{5,3},{6,4},{7,5},{8,14},{9,15},{10,... | collective-permute-start | bytes 589832 | tf_op jit(solution)/shard_map/ppermute | solution.py:358
  121.4 8.8 %collective-permute-start.11 = (bf16[3,64,512]{2,1,0:T(8,128)(2,1)S(1)}, bf16[3,64,512]{2,1,0:T(8,128)(2,1)S(1)}, u32[]{:S(2)}, u32[]{:S(2)}) collective-permute-start(bf16[3,64,512]{2,1,0:T(8,128)(2,1)S(1)} %get-tuple-element.59), channel_id=1, source_target_pairs={{0,2},{1,3},{2,4},{3,5},{4,6},{5,7},{6,0},{7,1},{8,10},{9,11},{10,... | collective-permute-start | bytes 589832 | tf_op jit(solution)/shard_map/ppermute | solution.py:358
  123.3 6.9 %collective-permute-start.12 = (bf16[3,64,512]{2,1,0:T(8,128)(2,1)S(1)}, bf16[3,64,512]{2,1,0:T(8,128)(2,1)S(1)}, u32[]{:S(2)}, u32[]{:S(2)}) collective-permute-start(bf16[3,64,512]{2,1,0:T(8,128)(2,1)S(1)} %get-tuple-element.60), channel_id=1, source_target_pairs={{0,7},{1,0},{2,1},{3,2},{4,3},{5,4},{6,5},{7,6},{8,15},{9,8},{10,9... | collective-permute-start | bytes 589832 | tf_op jit(solution)/shard_map/ppermute | solution.py:358
  124.1 6.2 %collective-permute-start.13 = (bf16[3,64,512]{2,1,0:T(8,128)(2,1)S(1)}, bf16[3,64,512]{2,1,0:T(8,128)(2,1)S(1)}, u32[]{:S(2)}, u32[]{:S(2)}) collective-permute-start(bf16[3,64,512]{2,1,0:T(8,128)(2,1)S(1)} %get-tuple-element.61), channel_id=1, source_target_pairs={{0,1},{1,2},{2,3},{3,4},{4,5},{5,6},{6,7},{7,0},{8,9},{9,10},{10,1... | collective-permute-start | bytes 589832 | tf_op jit(solution)/shard_map/ppermute | solution.py:358
  131.5 11.8 %copy-start.6 = (f32[1,4,64,512]{3,2,1,0:T(8,128)S(1)}, f32[1,4,64,512]{3,2,1,0:T(8,128)}, u32[]{:S(2)}) copy-start(f32[1,4,64,512]{3,2,1,0:T(8,128)} %param.12) | copy-start | bytes 1572868
  132.8 10.5 %copy-start.5 = (f32[1,4,64,512]{3,2,1,0:T(8,128)S(1)}, f32[1,4,64,512]{3,2,1,0:T(8,128)}, u32[]{:S(2)}) copy-start(f32[1,4,64,512]{3,2,1,0:T(8,128)} %param.11) | copy-start | bytes 1572868
  132.9 16.8 %all-to-all-start.5 = ((bf16[8,8,2048]{2,1,0:T(8,128)(2,1)}), bf16[8,8,2048]{2,1,0:T(8,128)(2,1)S(1)}, u32[]{:S(2)}, u32[]{:S(2)}) async-start(bf16[8,8,2048]{2,1,0:T(8,128)(2,1)} %place.1), calls=%async_computation.5 | async-start | bytes 524288 | tf_op jit(solution)/shard_map/all_to_all | solution.py:453

commit v5 on v4

--- a/solution.py
+++ b/solution.py
@@ -195,12 +195,19 @@
 
 
 def roots_body(other, to, left, right, moment, *refs):
-    parts, outs = refs[: MD - 1], refs[MD - 1 :]
+    parts, outs, sems = refs[: MD - 1], refs[MD - 1 : -1], refs[-1]
+    copies = []
     for s in range(MD):
         source = lax.rem(other[0] - s + MD, MD)
         rows = pl.ds(pl.multiple_of(source * ROW_DEV, ROW_DEV), ROW_DEV)
         for i, own in enumerate((left, right, moment)):
-            outs[i][rows, :] = parts[s - 1][i] if s else own[to[0]]
+            if s:
+                outs[i][rows, :] = parts[s - 1][i]
+            else:
+                copies.append(pltpu.make_async_copy(own.at[to[0]], outs[i].at[rows], sems.at[i]))
+                copies[-1].start()
+    for copy in copies:
+        copy.wait()
 
 
 def assemble(got, block):
@@ -214,13 +221,23 @@
                     )
 
 
-def block_body(masks, got, left, right, old, out, block, applied, prod, buffer, sems):
+def block_body(
+    masks, got, left, right_in, old_in, out, block, applied, prod, right, old, fetch, buffer, sems
+):
+    fetches = [
+        pltpu.make_async_copy(right_in, right, fetch.at[0]),
+        pltpu.make_async_copy(old_in, old, fetch.at[1]),
+    ]
+    for copy in fetches:
+        copy.start()
     assemble(got, block)
     adam = got[0, ZZ * TB].astype(F32)
     for i in range(1, YDIM * MD):
         adam += got[i, ZZ * TB].astype(F32)
     adam = jnp.sum(jnp.where(masks[:1, :] > 0, decode(adam), 0.0), keepdims=True)
     applied[...] = jnp.dot(left[...], block[...], preferred_element_type=F32).astype(BF16)
+    for copy in fetches:
+        copy.wait()
     p = jnp.dot(applied[...], right[...], preferred_element_type=F32)
     prod[...] = p
     norm = jnp.sum(p * p, keepdims=True)
@@ -396,21 +413,25 @@
     got = lax.all_to_all(pay, ("y", "m"), 0, 0, tiled=True)
     left, right, old = call(
         roots_body,
-        "ssvvv" + "v" * (MD - 1),
+        "ssaaa" + "v" * (MD - 1),
         [struct(*square)] * 3,
         [other, to, left_root[0], right_root[0], momentum[0], *(moved[s] for s in range(1, MD))],
+        scratch=[pltpu.SemaphoreType.DMA((3,))],
         name="roots",
     )
     whole = got
     (back,) = call(
         block_body,
-        "vvvvv",
+        "vvvaa",
         [struct(YDIM * MD, ZZ * TB + 1, SUB, LANES)],
         [masks, whole, left, right, old],
         scratch=[
             pltpu.VMEM(square, BF16),
             pltpu.VMEM(square, BF16),
             pltpu.VMEM(square, F32),
+            pltpu.VMEM(square, BF16),
+            pltpu.VMEM(square, BF16),
+            pltpu.SemaphoreType.DMA((2,)),
         ],
         flops=4 * BLK**3,
         vmem=24,

time: 152 us -> 152 us (level)
  no operation moved by 1% of the time
where the time goes in v5:
time: 152 us; the launch traced here: 151 us
  starting transfers between devices  89.3 us (59%)
  waiting for transfers between devices  37.4 us (25%)
  Pallas kernels  14.1 us (9%)
  local copies, waits for them, and re-layouts  5.48 us (4%)
  other arithmetic  2.82 us (2%)
  between operations  1.6 us (1%)
    ppermute x14, starting transfers between devices, shift(): return lax.ppermute(part, 'm', [(i, (i + s) % MD) for i in range(MD)])  34.7 us
    all_to_all x2, starting transfers between devices, shards(): got = lax.all_to_all(pay, 'z', 0, 0, tiled=True)  17.6 us
    pallas_call x10, Pallas kernels, call(): pl.pallas_call(body, out_shape=tuple(outs), grid_spec=pltpu.PrefetchScala...  12.4 us
    all_to_all x1, starting transfers between devices, shards(): got = lax.all_to_all(pay, ('y', 'm'), 0, 0, tiled=True)  12.3 us
    all_to_all x1, waiting for transfers between devices, shards(): got = lax.all_to_all(back, ('y', 'm'), 0, 0, tiled=True)  10.4 us
    all_to_all x1, starting transfers between devices, shards(): lax.all_to_all(gradient.reshape(MD, SUB, LOCAL), 'm', 0, 0, tiled=True)  10.3 us
    all_to_all x1, starting transfers between devices, shards(): placed = lax.all_to_all(pay, 'm', 0, 0, tiled=True).reshape(ROW_DEV, LOCAL)  10.3 us
    ppermute x14, waiting for transfers between devices, shift(): return lax.ppermute(part, 'm', [(i, (i + s) % MD) for i in range(MD)])  10.2 us
  transfers between devices with their start and end apart: 20, of which 13 were waited for; matrix products, arithmetic and copies ran while one was open for 1% of the time, Pallas kernels for 5%

profile of v5, /device:TPU:1, one launch (start us, length us, event | category | flops | bytes accessed | tf_op | source)
XLA Modules:
  0.0 150.7 jit_solution(11021195544605089340)
XLA Ops:
  0.6 10.3 %all-to-all-start = ((bf16[8,8,2048]{2,1,0:T(8,128)(2,1)}), bf16[8,8,2048]{2,1,0:T(8,128)(2,1)S(1)}, u32[]{:S(2)}, u32[]{:S(2)}) async-start(bf16[8,8,2048]{2,1,0:T(8,128)(2,1)} %bitcast.16), calls=%async_computation | async-start | bytes 524288 | tf_op jit(solution)/shard_map/all_to_all | solution.py:384
  11.0 0.7 copy-done.11
  11.7 0.1 reshape.77
  11.7 0.1 convert_reduce_fusion
  11.9 0.1 select_reduce_fusion.3
  12.0 0.6 compare_select_fusion.4
  12.7 1.0 copy-done.4
  13.7 1.7 %adam.1 = (f32[64,2048]{1,0:T(8,128)}, bf16[8,128]{1,0:T(8,128)(2,1)S(1)}) custom-call(s32[1]{0:T(128)} %bitcast.1.index.other, bf16[64,2048]{1,0:T(8,128)(2,1)S(1)} %copy-done, f32[64,2048]{1,0:T(8,128)S(1)} %copy-done.4), custom_call_target="tpu_custom_call" | custom-call | tf_op jit(solution)/shard_map/adam/pallas_call | solution.py:146
  15.4 0.1 select_reduce_fusion.inverse
  15.5 0.2 select_reduce_fusion.2.before.to
  15.7 1.8 %all-to-all-done.got = bf16[8,8,2048]{2,1,0:T(8,128)(2,1)S(1)} async-done(((bf16[8,8,2048]{2,1,0:T(8,128)(2,1)}), bf16[8,8,2048]{2,1,0:T(8,128)(2,1)S(1)}, u32[]{:S(2)}, u32[]{:S(2)}) %all-to-all-start) | async-done | bytes 262176 | tf_op jit(solution)/shard_map/all_to_all | solution.py:384
  17.5 1.4 spread.1.after
  18.9 0.0 copy-start.1
  19.0 0.0 copy-start.2
  19.0 0.0 copy-start.3
  19.0 10.6 %all-to-all-start.1 = ((bf16[16,17,8,128]{3,2,1,0:T(8,128)(2,1)}), bf16[16,17,8,128]{3,2,1,0:T(8,128)(2,1)S(1)}, u32[]{:S(2)}, u32[]{:S(2)}) async-start(bf16[16,17,8,128]{3,2,1,0:T(8,128)(2,1)} %spread.1.after), calls=%async_computation.1 | async-start | bytes 1114112 | tf_op jit(solution)/shard_map/all_to_all | solution.py:403
  29.7 0.6 pack.1
  30.3 3.0 %collective-permute-start = (bf16[3,64,512]{2,1,0:T(8,128)(2,1)S(1)}, bf16[3,64,512]{2,1,0:T(8,128)(2,1)S(1)}, u32[]{:S(2)}, u32[]{:S(2)}) collective-permute-start(bf16[3,64,512]{2,1,0:T(8,128)(2,1)S(1)} %get-tuple-element.37), channel_id=1, source_target_pairs={{0,4},{1,5},{2,6},{3,7},{4,0},{5,1},{6,2},{7,3},{8,12},{9,13},{10,... | collective-permute-start | bytes 589832 | tf_op jit(solution)/shard_map/ppermute | solution.py:375
  33.3 5.0 %collective-permute-start.1 = (bf16[3,64,512]{2,1,0:T(8,128)(2,1)S(1)}, bf16[3,64,512]{2,1,0:T(8,128)(2,1)S(1)}, u32[]{:S(2)}, u32[]{:S(2)}) collective-permute-start(bf16[3,64,512]{2,1,0:T(8,128)(2,1)S(1)} %get-tuple-element.38), channel_id=1, source_target_pairs={{0,5},{1,6},{2,7},{3,0},{4,1},{5,2},{6,3},{7,4},{8,13},{9,14},{10,... | collective-permute-start | bytes 589832 | tf_op jit(solution)/shard_map/ppermute | solution.py:375
  38.3 2.2 %collective-permute-start.2 = (bf16[3,64,512]{2,1,0:T(8,128)(2,1)S(1)}, bf16[3,64,512]{2,1,0:T(8,128)(2,1)S(1)}, u32[]{:S(2)}, u32[]{:S(2)}) collective-permute-start(bf16[3,64,512]{2,1,0:T(8,128)(2,1)S(1)} %get-tuple-element.39), channel_id=1, source_target_pairs={{0,3},{1,4},{2,5},{3,6},{4,7},{5,0},{6,1},{7,2},{8,11},{9,12},{10,... | collective-permute-start | bytes 589832 | tf_op jit(solution)/shard_map/ppermute | solution.py:375
  40.5 3.4 %collective-permute-start.3 = (bf16[3,64,512]{2,1,0:T(8,128)(2,1)S(1)}, bf16[3,64,512]{2,1,0:T(8,128)(2,1)S(1)}, u32[]{:S(2)}, u32[]{:S(2)}) collective-permute-start(bf16[3,64,512]{2,1,0:T(8,128)(2,1)S(1)} %get-tuple-element.40), channel_id=1, source_target_pairs={{0,6},{1,7},{2,0},{3,1},{4,2},{5,3},{6,4},{7,5},{8,14},{9,15},{10,... | collective-permute-start | bytes 589832 | tf_op jit(solution)/shard_map/ppermute | solution.py:375
  43.9 1.9 %collective-permute-start.4 = (bf16[3,64,512]{2,1,0:T(8,128)(2,1)S(1)}, bf16[3,64,512]{2,1,0:T(8,128)(2,1)S(1)}, u32[]{:S(2)}, u32[]{:S(2)}) collective-permute-start(bf16[3,64,512]{2,1,0:T(8,128)(2,1)S(1)} %get-tuple-element.41), channel_id=1, source_target_pairs={{0,2},{1,3},{2,4},{3,5},{4,6},{5,7},{6,0},{7,1},{8,10},{9,11},{10,... | collective-permute-start | bytes 589832 | tf_op jit(solution)/shard_map/ppermute | solution.py:375
  45.8 0.0 collective-permute-done.refs_0_.refs_3_
  45.8 1.6 %collective-permute-start.5 = (bf16[3,64,512]{2,1,0:T(8,128)(2,1)S(1)}, bf16[3,64,512]{2,1,0:T(8,128)(2,1)S(1)}, u32[]{:S(2)}, u32[]{:S(2)}) collective-permute-start(bf16[3,64,512]{2,1,0:T(8,128)(2,1)S(1)} %get-tuple-element.42), channel_id=1, source_target_pairs={{0,7},{1,0},{2,1},{3,2},{4,3},{5,4},{6,5},{7,6},{8,15},{9,8},{10,9... | collective-permute-start | bytes 589832 | tf_op jit(solution)/shard_map/ppermute | solution.py:375
  47.4 0.2 collective-permute-start.6
  47.6 0.6 collective-permute-done.2.refs_2_
  48.2 2.1 %collective-permute-done.3.refs_3_.refs_5_ = bf16[3,64,512]{2,1,0:T(8,128)(2,1)S(1)} collective-permute-done((bf16[3,64,512]{2,1,0:T(8,128)(2,1)S(1)}, bf16[3,64,512]{2,1,0:T(8,128)(2,1)S(1)}, u32[]{:S(2)}, u32[]{:S(2)}) %collective-permute-start.3) | collective-permute-done | bytes 196640 | tf_op jit(solution)/shard_map/ppermute | solution.py:375
  50.2 1.6 %collective-permute-done.4.refs_4_.refs_1_ = bf16[3,64,512]{2,1,0:T(8,128)(2,1)S(1)} collective-permute-done((bf16[3,64,512]{2,1,0:T(8,128)(2,1)S(1)}, bf16[3,64,512]{2,1,0:T(8,128)(2,1)S(1)}, u32[]{:S(2)}, u32[]{:S(2)}) %collective-permute-start.4) | collective-permute-done | bytes 196640 | tf_op jit(solution)/shard_map/ppermute | solution.py:375
  51.8 0.8 collective-permute-done.6.refs_6_.refs_0_
  52.6 0.9 all-to-all-done.1.got
  53.5 0.9 plane.1
  54.4 12.3 %all-to-all-start.2 = ((bf16[32,9,8,128]{3,2,1,0:T(8,128)(2,1)}), bf16[32,9,8,128]{3,2,1,0:T(8,128)(2,1)S(1)}, u32[]{:S(2)}, u32[]{:S(2)}) async-start(bf16[32,9,8,128]{3,2,1,0:T(8,128)(2,1)} %plane.1), calls=%async_computation.2 | async-start | bytes 1179648 | tf_op jit(solution)/shard_map/all_to_all | solution.py:413
  67.4 0.7 compare_select_fusion.5
  68.1 0.9 roots.1
  69.0 0.0 copy-start.7
  69.0 0.8 copy-done.7
  69.8 0.8 copy-done.9
  70.6 8.4 %all-to-all-done.2.got = bf16[32,9,8,128]{3,2,1,0:T(8,128)(2,1)S(1)} async-done(((bf16[32,9,8,128]{3,2,1,0:T(8,128)(2,1)}), bf16[32,9,8,128]{3,2,1,0:T(8,128)(2,1)S(1)}, u32[]{:S(2)}, u32[]{:S(2)}) %all-to-all-start.2) | async-done | bytes 589856 | tf_op jit(solution)/shard_map/all_to_all | solution.py:413
  79.0 1.0 copy-done.8
  80.1 1.0 copy-done.10
  81.1 2.5 %block.1.moment = bf16[32,9,8,128]{3,2,1,0:T(8,128)(2,1)} custom-call(f32[8,128]{1,0:T(8,128)S(1)} %pad_select_fusion.masks, bf16[32,9,8,128]{3,2,1,0:T(8,128)(2,1)S(1)} %all-to-all-done.2.got, bf16[512,512]{1,0:T(8,128)(2,1)S(1)} %get-tuple-element.44.left, bf16[512,512]{1,0:T(8,128)(2,1)S(1)} %copy-done.8, bf16[512,512]{1,0:T(8,128)(2,1)S(1)} %copy-done.10), custom_call_target="tpu_custom_call" | custom-call | flops 536870912 | bytes 1708032 | tf_op jit(solution)/shard_map/block/pallas_call | solution.py:66
  83.6 4.1 %all-to-all-start.3 = ((bf16[32,9,8,128]{3,2,1,0:T(8,128)(2,1)}), bf16[32,9,8,128]{3,2,1,0:T(8,128)(2,1)S(1)}, u32[]{:S(2)}, u32[]{:S(2)}) async-start(bf16[32,9,8,128]{3,2,1,0:T(8,128)(2,1)} %block.1.moment), calls=%async_computation.3 | async-start | bytes 1179648 | tf_op jit(solution)/shard_map/all_to_all | solution.py:441
  87.6 2.0 %stats.1 = (bf16[3,64,512]{2,1,0:T(8,128)(2,1)S(1)}, bf16[3,64,512]{2,1,0:T(8,128)(2,1)S(1)}, bf16[3,64,512]{2,1,0:T(8,128)(2,1)S(1)}, bf16[3,64,512]{2,1,0:T(8,...) custom-call(s32[1]{0:T(128)} %bitcast.1.index.other, ...), custom_call_target="tpu_custom_call" | custom-call | flops 536870912 | bytes 2752512 | tf_op jit(solution)/shard_map/stats/pallas_call | solution.py:66
  89.6 10.4 %all-to-all-done.3.got = bf16[32,9,8,128]{3,2,1,0:T(8,128)(2,1)S(1)} async-done(((bf16[32,9,8,128]{3,2,1,0:T(8,128)(2,1)}), bf16[32,9,8,128]{3,2,1,0:T(8,128)(2,1)S(1)}, u32[]{:S(2)}, u32[]{:S(2)}) %all-to-all-start.3) | async-done | bytes 589856 | tf_op jit(solution)/shard_map/all_to_all | solution.py:441
  100.0 0.9 unplane.1
  100.9 6.9 %all-to-all-start.4 = ((bf16[16,17,8,128]{3,2,1,0:T(8,128)(2,1)}), bf16[16,17,8,128]{3,2,1,0:T(8,128)(2,1)S(1)}, u32[]{:S(2)}, u32[]{:S(2)}) async-start(bf16[16,17,8,128]{3,2,1,0:T(8,128)(2,1)} %get-tuple-element.54), calls=%async_computation.4 | async-start | bytes 1114112 | tf_op jit(solution)/shard_map/all_to_all | solution.py:460
  107.9 2.7 %collective-permute-start.7 = (bf16[3,64,512]{2,1,0:T(8,128)(2,1)S(1)}, bf16[3,64,512]{2,1,0:T(8,128)(2,1)S(1)}, u32[]{:S(2)}, u32[]{:S(2)}) collective-permute-start(bf16[3,64,512]{2,1,0:T(8,128)(2,1)S(1)} %get-tuple-element.55), channel_id=1, source_target_pairs={{0,4},{1,5},{2,6},{3,7},{4,0},{5,1},{6,2},{7,3},{8,12},{9,13},{10,... | collective-permute-start | bytes 589832 | tf_op jit(solution)/shard_map/ppermute | solution.py:375
  110.6 4.6 %collective-permute-start.8 = (bf16[3,64,512]{2,1,0:T(8,128)(2,1)S(1)}, bf16[3,64,512]{2,1,0:T(8,128)(2,1)S(1)}, u32[]{:S(2)}, u32[]{:S(2)}) collective-permute-start(bf16[3,64,512]{2,1,0:T(8,128)(2,1)S(1)} %get-tuple-element.56), channel_id=1, source_target_pairs={{0,5},{1,6},{2,7},{3,0},{4,1},{5,2},{6,3},{7,4},{8,13},{9,14},{10,... | collective-permute-start | bytes 589832 | tf_op jit(solution)/shard_map/ppermute | solution.py:375
  115.2 2.4 %collective-permute-start.9 = (bf16[3,64,512]{2,1,0:T(8,128)(2,1)S(1)}, bf16[3,64,512]{2,1,0:T(8,128)(2,1)S(1)}, u32[]{:S(2)}, u32[]{:S(2)}) collective-permute-start(bf16[3,64,512]{2,1,0:T(8,128)(2,1)S(1)} %get-tuple-element.57), channel_id=1, source_target_pairs={{0,3},{1,4},{2,5},{3,6},{4,7},{5,0},{6,1},{7,2},{8,11},{9,12},{10,... | collective-permute-start | bytes 589832 | tf_op jit(solution)/shard_map/ppermute | solution.py:375
  117.7 4.0 %collective-permute-start.10 = (bf16[3,64,512]{2,1,0:T(8,128)(2,1)S(1)}, bf16[3,64,512]{2,1,0:T(8,128)(2,1)S(1)}, u32[]{:S(2)}, u32[]{:S(2)}) collective-permute-start(bf16[3,64,512]{2,1,0:T(8,128)(2,1)S(1)} %get-tuple-element.58), channel_id=1, source_target_pairs={{0,6},{1,7},{2,0},{3,1},{4,2},{5,3},{6,4},{7,5},{8,14},{9,15},{10,... | collective-permute-start | bytes 589832 | tf_op jit(solution)/shard_map/ppermute | solution.py:375
  121.7 1.9 %collective-permute-start.11 = (bf16[3,64,512]{2,1,0:T(8,128)(2,1)S(1)}, bf16[3,64,512]{2,1,0:T(8,128)(2,1)S(1)}, u32[]{:S(2)}, u32[]{:S(2)}) collective-permute-start(bf16[3,64,512]{2,1,0:T(8,128)(2,1)S(1)} %get-tuple-element.59), channel_id=1, source_target_pairs={{0,2},{1,3},{2,4},{3,5},{4,6},{5,7},{6,0},{7,1},{8,10},{9,11},{10,... | collective-permute-start | bytes 589832 | tf_op jit(solution)/shard_map/ppermute | solution.py:375
  123.6 0.7 collective-permute-start.12
  124.4 1.0 collective-permute-start.13
  125.4 0.2 collective-permute-done.9.refs_2_.refs_3_
  125.5 2.7 %collective-permute-done.10.refs_3_.refs_6_ = bf16[3,64,512]{2,1,0:T(8,128)(2,1)S(1)} collective-permute-done((bf16[3,64,512]{2,1,0:T(8,128)(2,1)S(1)}, bf16[3,64,512]{2,1,0:T(8,128)(2,1)S(1)}, u32[]{:S(2)}, u32[]{:S(2)}) %collective-permute-start.10) | collective-permute-done | bytes 196640 | tf_op jit(solution)/shard_map/ppermute | solution.py:375
  128.2 2.3 %collective-permute-done.11.refs_4_.refs_2_ = bf16[3,64,512]{2,1,0:T(8,128)(2,1)S(1)} collective-permute-done((bf16[3,64,512]{2,1,0:T(8,128)(2,1)S(1)}, bf16[3,64,512]{2,1,0:T(8,128)(2,1)S(1)}, u32[]{:S(2)}, u32[]{:S(2)}) %collective-permute-start.11) | collective-permute-done | bytes 196640 | tf_op jit(solution)/shard_map/ppermute | solution.py:375
  130.5 1.3 all-to-all-done.4.got
  131.8 1.3 place.1
  133.1 0.0 copy-start.5
  133.1 10.3 %all-to-all-start.5 = ((bf16[8,8,2048]{2,1,0:T(8,128)(2,1)}), bf16[8,8,2048]{2,1,0:T(8,128)(2,1)S(1)}, u32[]{:S(2)}, u32[]{:S(2)}) async-start(bf16[8,8,2048]{2,1,0:T(8,128)(2,1)} %place.1), calls=%async_computation.5 | async-start | bytes 524288 | tf_op jit(solution)/shard_map/all_to_all | solution.py:474
  143.5 0.2 select_reduce_fusion.1.source
  143.6 1.8 %finish.1 = (f32[4,64,512]{2,1,0:T(8,128)}, f32[4,64,512]{2,1,0:T(8,128)}, bf16[4,64,512]{2,1,0:T(8,128)(2,1)}) custom-call(s32[8]{0:T(128)S(1)} %select_reduce_fusion.1.source, f32[4,64,512]{2,1,0:T(8,128)S(1)} %bitcast.23, f32[4,64,512]{2,1,0:T(8,128)S(1)} %bitcast.24, bf16[3,64,512]{2,1,0:T(8,128)(2,1)S(1)} %get-tuple-element.63.refs_0_, ...), custom_call_target="tpu_custom_call" | custom-call | bytes 3932160 | tf_op jit(solution)/shard_map/finish/pallas_call | solution.py:66
  145.5 4.5 %all-to-all-done.5 = bf16[8,8,2048]{2,1,0:T(8,128)(2,1)S(1)} async-done(((bf16[8,8,2048]{2,1,0:T(8,128)(2,1)}), bf16[8,8,2048]{2,1,0:T(8,128)(2,1)S(1)}, u32[]{:S(2)}, u32[]{:S(2)}) %all-to-all-start.5) | async-done | bytes 262176 | tf_op jit(solution)/shard_map/all_to_all | solution.py:474
  150.0 0.8 fusion
  (24 shorter events, 0.1 us)
Async XLA Ops:
  0.6 12.0 %copy-start = (bf16[64,2048]{1,0:T(8,128)(2,1)S(1)}, bf16[64,2048]{1,0:T(8,128)(2,1)}, u32[]{:S(2)}) copy-start(bf16[64,2048]{1,0:T(8,128)(2,1)} %grad.1) | copy-start | bytes 786436
  0.6 16.9 %all-to-all-start = ((bf16[8,8,2048]{2,1,0:T(8,128)(2,1)}), bf16[8,8,2048]{2,1,0:T(8,128)(2,1)S(1)}, u32[]{:S(2)}, u32[]{:S(2)}) async-start(bf16[8,8,2048]{2,1,0:T(8,128)(2,1)} %bitcast.16), calls=%async_computation | async-start | bytes 524288 | tf_op jit(solution)/shard_map/all_to_all | solution.py:384
  11.0 0.7 copy-start.11
  12.6 1.0 copy-start.4
  18.9 10.7 %copy-start.1 = (bf16[1,4,64,512]{3,2,1,0:T(8,128)(2,1)S(1)}, bf16[1,4,64,512]{3,2,1,0:T(8,128)(2,1)}, u32[]{:S(2)}) copy-start(bf16[1,4,64,512]{3,2,1,0:T(8,128)(2,1)} %param.13) | copy-start | bytes 786436
  19.0 10.7 %copy-start.2 = (bf16[1,4,64,512]{3,2,1,0:T(8,128)(2,1)S(1)}, bf16[1,4,64,512]{3,2,1,0:T(8,128)(2,1)}, u32[]{:S(2)}) copy-start(bf16[1,4,64,512]{3,2,1,0:T(8,128)(2,1)} %param.14) | copy-start | bytes 786436
  19.0 10.7 %copy-start.3 = (bf16[1,4,64,512]{3,2,1,0:T(8,128)(2,1)S(1)}, bf16[1,4,64,512]{3,2,1,0:T(8,128)(2,1)}, u32[]{:S(2)}) copy-start(bf16[1,4,64,512]{3,2,1,0:T(8,128)(2,1)} %param.15) | copy-start | bytes 786436
  19.0 34.5 %all-to-all-start.1 = ((bf16[16,17,8,128]{3,2,1,0:T(8,128)(2,1)}), bf16[16,17,8,128]{3,2,1,0:T(8,128)(2,1)S(1)}, u32[]{:S(2)}, u32[]{:S(2)}) async-start(bf16[16,17,8,128]{3,2,1,0:T(8,128)(2,1)} %spread.1.after), calls=%async_computation.1 | async-start | bytes 1114112 | tf_op jit(solution)/shard_map/all_to_all | solution.py:403
  30.3 15.5 %collective-permute-start = (bf16[3,64,512]{2,1,0:T(8,128)(2,1)S(1)}, bf16[3,64,512]{2,1,0:T(8,128)(2,1)S(1)}, u32[]{:S(2)}, u32[]{:S(2)}) collective-permute-start(bf16[3,64,512]{2,1,0:T(8,128)(2,1)S(1)} %get-tuple-element.37), channel_id=1, source_target_pairs={{0,4},{1,5},{2,6},{3,7},{4,0},{5,1},{6,2},{7,3},{8,12},{9,13},{10,... | collective-permute-start | bytes 589832 | tf_op jit(solution)/shard_map/ppermute | solution.py:375
  33.3 14.1 %collective-permute-start.1 = (bf16[3,64,512]{2,1,0:T(8,128)(2,1)S(1)}, bf16[3,64,512]{2,1,0:T(8,128)(2,1)S(1)}, u32[]{:S(2)}, u32[]{:S(2)}) collective-permute-start(bf16[3,64,512]{2,1,0:T(8,128)(2,1)S(1)} %get-tuple-element.38), channel_id=1, source_target_pairs={{0,5},{1,6},{2,7},{3,0},{4,1},{5,2},{6,3},{7,4},{8,13},{9,14},{10,... | collective-permute-start | bytes 589832 | tf_op jit(solution)/shard_map/ppermute | solution.py:375
  38.3 9.9 %collective-permute-start.2 = (bf16[3,64,512]{2,1,0:T(8,128)(2,1)S(1)}, bf16[3,64,512]{2,1,0:T(8,128)(2,1)S(1)}, u32[]{:S(2)}, u32[]{:S(2)}) collective-permute-start(bf16[3,64,512]{2,1,0:T(8,128)(2,1)S(1)} %get-tuple-element.39), channel_id=1, source_target_pairs={{0,3},{1,4},{2,5},{3,6},{4,7},{5,0},{6,1},{7,2},{8,11},{9,12},{10,... | collective-permute-start | bytes 589832 | tf_op jit(solution)/shard_map/ppermute | solution.py:375
  40.5 9.7 %collective-permute-start.3 = (bf16[3,64,512]{2,1,0:T(8,128)(2,1)S(1)}, bf16[3,64,512]{2,1,0:T(8,128)(2,1)S(1)}, u32[]{:S(2)}, u32[]{:S(2)}) collective-permute-start(bf16[3,64,512]{2,1,0:T(8,128)(2,1)S(1)} %get-tuple-element.40), channel_id=1, source_target_pairs={{0,6},{1,7},{2,0},{3,1},{4,2},{5,3},{6,4},{7,5},{8,14},{9,15},{10,... | collective-permute-start | bytes 589832 | tf_op jit(solution)/shard_map/ppermute | solution.py:375
  43.9 7.9 %collective-permute-start.4 = (bf16[3,64,512]{2,1,0:T(8,128)(2,1)S(1)}, bf16[3,64,512]{2,1,0:T(8,128)(2,1)S(1)}, u32[]{:S(2)}, u32[]{:S(2)}) collective-permute-start(bf16[3,64,512]{2,1,0:T(8,128)(2,1)S(1)} %get-tuple-element.41), channel_id=1, source_target_pairs={{0,2},{1,3},{2,4},{3,5},{4,6},{5,7},{6,0},{7,1},{8,10},{9,11},{10,... | collective-permute-start | bytes 589832 | tf_op jit(solution)/shard_map/ppermute | solution.py:375
  45.8 6.0 %collective-permute-start.5 = (bf16[3,64,512]{2,1,0:T(8,128)(2,1)S(1)}, bf16[3,64,512]{2,1,0:T(8,128)(2,1)S(1)}, u32[]{:S(2)}, u32[]{:S(2)}) collective-permute-start(bf16[3,64,512]{2,1,0:T(8,128)(2,1)S(1)} %get-tuple-element.42), channel_id=1, source_target_pairs={{0,7},{1,0},{2,1},{3,2},{4,3},{5,4},{6,5},{7,6},{8,15},{9,8},{10,9... | collective-permute-start | bytes 589832 | tf_op jit(solution)/shard_map/ppermute | solution.py:375
  47.4 5.2 %collective-permute-start.6 = (bf16[3,64,512]{2,1,0:T(8,128)(2,1)S(1)}, bf16[3,64,512]{2,1,0:T(8,128)(2,1)S(1)}, u32[]{:S(2)}, u32[]{:S(2)}) collective-permute-start(bf16[3,64,512]{2,1,0:T(8,128)(2,1)S(1)} %get-tuple-element.43), channel_id=1, source_target_pairs={{0,1},{1,2},{2,3},{3,4},{4,5},{5,6},{6,7},{7,0},{8,9},{9,10},{10,1... | collective-permute-start | bytes 589832 | tf_op jit(solution)/shard_map/ppermute | solution.py:375
  54.4 24.6 %all-to-all-start.2 = ((bf16[32,9,8,128]{3,2,1,0:T(8,128)(2,1)}), bf16[32,9,8,128]{3,2,1,0:T(8,128)(2,1)S(1)}, u32[]{:S(2)}, u32[]{:S(2)}) async-start(bf16[32,9,8,128]{3,2,1,0:T(8,128)(2,1)} %plane.1), calls=%async_computation.2 | async-start | bytes 1179648 | tf_op jit(solution)/shard_map/all_to_all | solution.py:413
  69.0 0.8 copy-start.7
  69.8 0.8 copy-start.9
  79.0 1.0 copy-start.8
  80.1 1.0 copy-start.10
  83.6 16.4 %all-to-all-start.3 = ((bf16[32,9,8,128]{3,2,1,0:T(8,128)(2,1)}), bf16[32,9,8,128]{3,2,1,0:T(8,128)(2,1)S(1)}, u32[]{:S(2)}, u32[]{:S(2)}) async-start(bf16[32,9,8,128]{3,2,1,0:T(8,128)(2,1)} %block.1.moment), calls=%async_computation.3 | async-start | bytes 1179648 | tf_op jit(solution)/shard_map/all_to_all | solution.py:441
  100.9 30.9 %all-to-all-start.4 = ((bf16[16,17,8,128]{3,2,1,0:T(8,128)(2,1)}), bf16[16,17,8,128]{3,2,1,0:T(8,128)(2,1)S(1)}, u32[]{:S(2)}, u32[]{:S(2)}) async-start(bf16[16,17,8,128]{3,2,1,0:T(8,128)(2,1)} %get-tuple-element.54), calls=%async_computation.4 | async-start | bytes 1114112 | tf_op jit(solution)/shard_map/all_to_all | solution.py:460
  107.9 15.8 %collective-permute-start.7 = (bf16[3,64,512]{2,1,0:T(8,128)(2,1)S(1)}, bf16[3,64,512]{2,1,0:T(8,128)(2,1)S(1)}, u32[]{:S(2)}, u32[]{:S(2)}) collective-permute-start(bf16[3,64,512]{2,1,0:T(8,128)(2,1)S(1)} %get-tuple-element.55), channel_id=1, source_target_pairs={{0,4},{1,5},{2,6},{3,7},{4,0},{5,1},{6,2},{7,3},{8,12},{9,13},{10,... | collective-permute-start | bytes 589832 | tf_op jit(solution)/shard_map/ppermute | solution.py:375
  110.6 13.8 %collective-permute-start.8 = (bf16[3,64,512]{2,1,0:T(8,128)(2,1)S(1)}, bf16[3,64,512]{2,1,0:T(8,128)(2,1)S(1)}, u32[]{:S(2)}, u32[]{:S(2)}) collective-permute-start(bf16[3,64,512]{2,1,0:T(8,128)(2,1)S(1)} %get-tuple-element.56), channel_id=1, source_target_pairs={{0,5},{1,6},{2,7},{3,0},{4,1},{5,2},{6,3},{7,4},{8,13},{9,14},{10,... | collective-permute-start | bytes 589832 | tf_op jit(solution)/shard_map/ppermute | solution.py:375
  115.2 10.3 %collective-permute-start.9 = (bf16[3,64,512]{2,1,0:T(8,128)(2,1)S(1)}, bf16[3,64,512]{2,1,0:T(8,128)(2,1)S(1)}, u32[]{:S(2)}, u32[]{:S(2)}) collective-permute-start(bf16[3,64,512]{2,1,0:T(8,128)(2,1)S(1)} %get-tuple-element.57), channel_id=1, source_target_pairs={{0,3},{1,4},{2,5},{3,6},{4,7},{5,0},{6,1},{7,2},{8,11},{9,12},{10,... | collective-permute-start | bytes 589832 | tf_op jit(solution)/shard_map/ppermute | solution.py:375
  117.7 10.6 %collective-permute-start.10 = (bf16[3,64,512]{2,1,0:T(8,128)(2,1)S(1)}, bf16[3,64,512]{2,1,0:T(8,128)(2,1)S(1)}, u32[]{:S(2)}, u32[]{:S(2)}) collective-permute-start(bf16[3,64,512]{2,1,0:T(8,128)(2,1)S(1)} %get-tuple-element.58), channel_id=1, source_target_pairs={{0,6},{1,7},{2,0},{3,1},{4,2},{5,3},{6,4},{7,5},{8,14},{9,15},{10,... | collective-permute-start | bytes 589832 | tf_op jit(solution)/shard_map/ppermute | solution.py:375
  121.7 8.8 %collective-permute-start.11 = (bf16[3,64,512]{2,1,0:T(8,128)(2,1)S(1)}, bf16[3,64,512]{2,1,0:T(8,128)(2,1)S(1)}, u32[]{:S(2)}, u32[]{:S(2)}) collective-permute-start(bf16[3,64,512]{2,1,0:T(8,128)(2,1)S(1)} %get-tuple-element.59), channel_id=1, source_target_pairs={{0,2},{1,3},{2,4},{3,5},{4,6},{5,7},{6,0},{7,1},{8,10},{9,11},{10,... | collective-permute-start | bytes 589832 | tf_op jit(solution)/shard_map/ppermute | solution.py:375
  123.6 6.9 %collective-permute-start.12 = (bf16[3,64,512]{2,1,0:T(8,128)(2,1)S(1)}, bf16[3,64,512]{2,1,0:T(8,128)(2,1)S(1)}, u32[]{:S(2)}, u32[]{:S(2)}) collective-permute-start(bf16[3,64,512]{2,1,0:T(8,128)(2,1)S(1)} %get-tuple-element.60), channel_id=1, source_target_pairs={{0,7},{1,0},{2,1},{3,2},{4,3},{5,4},{6,5},{7,6},{8,15},{9,8},{10,9... | collective-permute-start | bytes 589832 | tf_op jit(solution)/shard_map/ppermute | solution.py:375
  124.4 6.2 %collective-permute-start.13 = (bf16[3,64,512]{2,1,0:T(8,128)(2,1)S(1)}, bf16[3,64,512]{2,1,0:T(8,128)(2,1)S(1)}, u32[]{:S(2)}, u32[]{:S(2)}) collective-permute-start(bf16[3,64,512]{2,1,0:T(8,128)(2,1)S(1)} %get-tuple-element.61), channel_id=1, source_target_pairs={{0,1},{1,2},{2,3},{3,4},{4,5},{5,6},{6,7},{7,0},{8,9},{9,10},{10,1... | collective-permute-start | bytes 589832 | tf_op jit(solution)/shard_map/ppermute | solution.py:375
  131.8 11.8 %copy-start.6 = (f32[1,4,64,512]{3,2,1,0:T(8,128)S(1)}, f32[1,4,64,512]{3,2,1,0:T(8,128)}, u32[]{:S(2)}) copy-start(f32[1,4,64,512]{3,2,1,0:T(8,128)} %param.12) | copy-start | bytes 1572868
  133.1 10.5 %copy-start.5 = (f32[1,4,64,512]{3,2,1,0:T(8,128)S(1)}, f32[1,4,64,512]{3,2,1,0:T(8,128)}, u32[]{:S(2)}) copy-start(f32[1,4,64,512]{3,2,1,0:T(8,128)} %param.11) | copy-start | bytes 1572868
  133.1 16.8 %all-to-all-start.5 = ((bf16[8,8,2048]{2,1,0:T(8,128)(2,1)}), bf16[8,8,2048]{2,1,0:T(8,128)(2,1)S(1)}, u32[]{:S(2)}, u32[]{:S(2)}) async-start(bf16[8,8,2048]{2,1,0:T(8,128)(2,1)} %place.1), calls=%async_computation.5 | async-start | bytes 524288 | tf_op jit(solution)/shard_map/all_to_all | solution.py:474

commit v6 on v3

--- a/solution.py
+++ b/solution.py
@@ -27,7 +27,7 @@
 TB = BLK // LANES
 SLOTS = 4
 AREA = BLK * BLK
-SHIFTS = (4, 5, 3, 6, 2, 7, 1)
+SHIFTS = (2, 6, 4, 5, 3, 7, 1)
 CHUNKS = 4
 
 BF16, F32 = jnp.bfloat16, jnp.float32

time: 150 us -> 151 us (level)
    all_to_all x1, starting transfers between devices: 12.3 us -> 9.52 us  [shards(): got = lax.all_to_all(pay, ('y', 'm'), 0, 0, tiled=True)]
    ppermute x14, starting transfers between devices: 34.7 us -> 37.4 us  [shift(): return lax.ppermute(part, 'm', [(i, (i + s) % MD) for i in range(MD)])]
    ppermute x14, waiting for transfers between devices: 10.2 us -> 12.8 us  [shift(): return lax.ppermute(part, 'm', [(i, (i + s) % MD) for i in range(MD)])]
  transfers between devices with their start and end apart: 20 -> 20, of which waited for: 13 -> 8; matrix products, arithmetic and copies ran while one was open for 1% -> 1% of each run, Pallas kernels for 4% -> 4%
where the time goes in v6:
time: 151 us; the launch traced here: 150 us
  starting transfers between devices  89.4 us (59%)
  waiting for transfers between devices  39.3 us (26%)
  Pallas kernels  13.1 us (9%)
  local copies, waits for them, and re-layouts  3.42 us (2%)
  other arithmetic  2.82 us (2%)
  between operations  1.64 us (1%)
    ppermute x14, starting transfers between devices, shift(): return lax.ppermute(part, 'm', [(i, (i + s) % MD) for i in range(MD)])  37.4 us
    all_to_all x2, starting transfers between devices, shards(): got = lax.all_to_all(pay, 'z', 0, 0, tiled=True)  18.9 us
    ppermute x14, waiting for transfers between devices, shift(): return lax.ppermute(part, 'm', [(i, (i + s) % MD) for i in range(MD)])  12.8 us
    pallas_call x10, Pallas kernels, call(): pl.pallas_call(body, out_shape=tuple(outs), grid_spec=pltpu.PrefetchScala...  11.4 us
    all_to_all x1, waiting for transfers between devices, shards(): got = lax.all_to_all(back, ('y', 'm'), 0, 0, tiled=True)  10.4 us
    all_to_all x1, starting transfers between devices, shards(): lax.all_to_all(gradient.reshape(MD, SUB, LOCAL), 'm', 0, 0, tiled=True)  10.3 us
    all_to_all x1, waiting for transfers between devices, shards(): got = lax.all_to_all(pay, ('y', 'm'), 0, 0, tiled=True)  9.86 us
    all_to_all x1, starting transfers between devices, shards(): got = lax.all_to_all(pay, ('y', 'm'), 0, 0, tiled=True)  9.52 us
  transfers between devices with their start and end apart: 20, of which 8 were waited for; matrix products, arithmetic and copies ran while one was open for 1% of the time, Pallas kernels for 4%

profile of v6, /device:TPU:1, one launch (start us, length us, event | category | flops | bytes accessed | tf_op | source)
XLA Modules:
  0.0 149.7 jit_solution(7923149288483427954)
XLA Ops:
  0.6 10.3 %all-to-all-start = ((bf16[8,8,2048]{2,1,0:T(8,128)(2,1)}), bf16[8,8,2048]{2,1,0:T(8,128)(2,1)S(1)}, u32[]{:S(2)}, u32[]{:S(2)}) async-start(bf16[8,8,2048]{2,1,0:T(8,128)(2,1)} %bitcast.16), calls=%async_computation | async-start | bytes 524288 | tf_op jit(solution)/shard_map/all_to_all | solution.py:367
  11.0 0.7 copy-done.9
  11.7 0.1 reshape.77
  11.7 0.1 convert_reduce_fusion
  11.9 0.1 select_reduce_fusion.3
  12.0 0.6 compare_select_fusion.4
  12.7 1.0 copy-done.1
  13.7 1.7 %adam.1 = (f32[64,2048]{1,0:T(8,128)}, bf16[8,128]{1,0:T(8,128)(2,1)S(1)}) custom-call(s32[1]{0:T(128)} %bitcast.1.index.other, bf16[64,2048]{1,0:T(8,128)(2,1)S(1)} %copy-done, f32[64,2048]{1,0:T(8,128)S(1)} %copy-done.1), custom_call_target="tpu_custom_call" | custom-call | tf_op jit(solution)/shard_map/adam/pallas_call | solution.py:146
  15.4 0.1 select_reduce_fusion.inverse
  15.5 0.2 select_reduce_fusion.2.before.to
  15.7 1.8 %all-to-all-done.got = bf16[8,8,2048]{2,1,0:T(8,128)(2,1)S(1)} async-done(((bf16[8,8,2048]{2,1,0:T(8,128)(2,1)}), bf16[8,8,2048]{2,1,0:T(8,128)(2,1)S(1)}, u32[]{:S(2)}, u32[]{:S(2)}) %all-to-all-start) | async-done | bytes 262176 | tf_op jit(solution)/shard_map/all_to_all | solution.py:367
  17.5 1.4 spread.1.after
  18.9 0.0 copy-start.4
  19.0 0.0 copy-start.5
  19.0 0.0 copy-start.6
  19.0 10.6 %all-to-all-start.1 = ((bf16[16,17,8,128]{3,2,1,0:T(8,128)(2,1)}), bf16[16,17,8,128]{3,2,1,0:T(8,128)(2,1)S(1)}, u32[]{:S(2)}, u32[]{:S(2)}) async-start(bf16[16,17,8,128]{3,2,1,0:T(8,128)(2,1)} %spread.1.after), calls=%async_computation.1 | async-start | bytes 1114112 | tf_op jit(solution)/shard_map/all_to_all | solution.py:386
  29.7 0.6 pack.1
  30.3 0.0 copy-start.7
  30.3 0.7 copy-done.7
  31.0 2.2 %collective-permute-start = (bf16[3,64,512]{2,1,0:T(8,128)(2,1)S(1)}, bf16[3,64,512]{2,1,0:T(8,128)(2,1)S(1)}, u32[]{:S(2)}, u32[]{:S(2)}) collective-permute-start(bf16[3,64,512]{2,1,0:T(8,128)(2,1)S(1)} %get-tuple-element.38), channel_id=1, source_target_pairs={{0,2},{1,3},{2,4},{3,5},{4,6},{5,7},{6,0},{7,1},{8,10},{9,11},{10,... | collective-permute-start | bytes 589832 | tf_op jit(solution)/shard_map/ppermute | solution.py:358
  33.2 4.3 %collective-permute-start.1 = (bf16[3,64,512]{2,1,0:T(8,128)(2,1)S(1)}, bf16[3,64,512]{2,1,0:T(8,128)(2,1)S(1)}, u32[]{:S(2)}, u32[]{:S(2)}) collective-permute-start(bf16[3,64,512]{2,1,0:T(8,128)(2,1)S(1)} %get-tuple-element.39), channel_id=1, source_target_pairs={{0,6},{1,7},{2,0},{3,1},{4,2},{5,3},{6,4},{7,5},{8,14},{9,15},{10,... | collective-permute-start | bytes 589832 | tf_op jit(solution)/shard_map/ppermute | solution.py:358
  37.5 1.9 %collective-permute-start.2 = (bf16[3,64,512]{2,1,0:T(8,128)(2,1)S(1)}, bf16[3,64,512]{2,1,0:T(8,128)(2,1)S(1)}, u32[]{:S(2)}, u32[]{:S(2)}) collective-permute-start(bf16[3,64,512]{2,1,0:T(8,128)(2,1)S(1)} %get-tuple-element.40), channel_id=1, source_target_pairs={{0,4},{1,5},{2,6},{3,7},{4,0},{5,1},{6,2},{7,3},{8,12},{9,13},{10,... | collective-permute-start | bytes 589832 | tf_op jit(solution)/shard_map/ppermute | solution.py:358
  39.4 5.4 %collective-permute-start.3 = (bf16[3,64,512]{2,1,0:T(8,128)(2,1)S(1)}, bf16[3,64,512]{2,1,0:T(8,128)(2,1)S(1)}, u32[]{:S(2)}, u32[]{:S(2)}) collective-permute-start(bf16[3,64,512]{2,1,0:T(8,128)(2,1)S(1)} %get-tuple-element.41), channel_id=1, source_target_pairs={{0,5},{1,6},{2,7},{3,0},{4,1},{5,2},{6,3},{7,4},{8,13},{9,14},{10,... | collective-permute-start | bytes 589832 | tf_op jit(solution)/shard_map/ppermute | solution.py:358
  44.8 3.4 %collective-permute-start.4 = (bf16[3,64,512]{2,1,0:T(8,128)(2,1)S(1)}, bf16[3,64,512]{2,1,0:T(8,128)(2,1)S(1)}, u32[]{:S(2)}, u32[]{:S(2)}) collective-permute-start(bf16[3,64,512]{2,1,0:T(8,128)(2,1)S(1)} %get-tuple-element.42), channel_id=1, source_target_pairs={{0,3},{1,4},{2,5},{3,6},{4,7},{5,0},{6,1},{7,2},{8,11},{9,12},{10,... | collective-permute-start | bytes 589832 | tf_op jit(solution)/shard_map/ppermute | solution.py:358
  48.3 0.0 collective-permute-done.refs_0_.refs_2_
  48.3 0.0 collective-permute-start.5
  48.3 0.0 collective-permute-done.1.refs_1_.refs_6_
  48.3 1.7 %collective-permute-start.6 = (bf16[3,64,512]{2,1,0:T(8,128)(2,1)S(1)}, bf16[3,64,512]{2,1,0:T(8,128)(2,1)S(1)}, u32[]{:S(2)}, u32[]{:S(2)}) collective-permute-start(bf16[3,64,512]{2,1,0:T(8,128)(2,1)S(1)} %get-tuple-element.44), channel_id=1, source_target_pairs={{0,1},{1,2},{2,3},{3,4},{4,5},{5,6},{6,7},{7,0},{8,9},{9,10},{10,1... | collective-permute-start | bytes 589832 | tf_op jit(solution)/shard_map/ppermute | solution.py:358
  50.1 0.0 collective-permute-done.2.refs_2_.refs_4_
  50.1 3.6 %collective-permute-done.3.refs_3_.refs_5_ = bf16[3,64,512]{2,1,0:T(8,128)(2,1)S(1)} collective-permute-done((bf16[3,64,512]{2,1,0:T(8,128)(2,1)S(1)}, bf16[3,64,512]{2,1,0:T(8,128)(2,1)S(1)}, u32[]{:S(2)}, u32[]{:S(2)}) %collective-permute-start.3) | collective-permute-done | bytes 196640 | tf_op jit(solution)/shard_map/ppermute | solution.py:358
  53.6 2.7 %collective-permute-done.4.refs_4_.refs_3_ = bf16[3,64,512]{2,1,0:T(8,128)(2,1)S(1)} collective-permute-done((bf16[3,64,512]{2,1,0:T(8,128)(2,1)S(1)}, bf16[3,64,512]{2,1,0:T(8,128)(2,1)S(1)}, u32[]{:S(2)}, u32[]{:S(2)}) %collective-permute-start.4) | collective-permute-done | bytes 196640 | tf_op jit(solution)/shard_map/ppermute | solution.py:358
  56.3 0.0 collective-permute-done.5.refs_5_.refs_7_
  56.3 0.0 collective-permute-done.6.refs_6_.refs_1_
  56.3 0.0 all-to-all-done.1.got
  56.3 0.9 plane.1
  57.2 9.5 %all-to-all-start.2 = ((bf16[32,9,8,128]{3,2,1,0:T(8,128)(2,1)}), bf16[32,9,8,128]{3,2,1,0:T(8,128)(2,1)S(1)}, u32[]{:S(2)}, u32[]{:S(2)}) async-start(bf16[32,9,8,128]{3,2,1,0:T(8,128)(2,1)} %plane.1), calls=%async_computation.2 | async-start | bytes 1179648 | tf_op jit(solution)/shard_map/all_to_all | solution.py:398
  67.4 0.7 compare_select_fusion.5
  68.1 0.0 copy-start.8
  68.1 0.9 copy-done.8
  69.0 0.1 roots.1
  69.2 9.9 %all-to-all-done.2.got = bf16[32,9,8,128]{3,2,1,0:T(8,128)(2,1)S(1)} async-done(((bf16[32,9,8,128]{3,2,1,0:T(8,128)(2,1)}), bf16[32,9,8,128]{3,2,1,0:T(8,128)(2,1)S(1)}, u32[]{:S(2)}, u32[]{:S(2)}) %all-to-all-start.2) | async-done | bytes 589856 | tf_op jit(solution)/shard_map/all_to_all | solution.py:398
  79.0 2.2 %block.1.moment = bf16[32,9,8,128]{3,2,1,0:T(8,128)(2,1)} custom-call(f32[8,128]{1,0:T(8,128)S(1)} %pad_select_fusion.masks, bf16[32,9,8,128]{3,2,1,0:T(8,128)(2,1)S(1)} %all-to-all-done.2.got, bf16[512,512]{1,0:T(8,128)(2,1)S(1)} %get-tuple-element.46.left, bf16[512,512]{1,0:T(8,128)(2,1)S(1)} %get-tuple-element.47.right, ...), custom_call_target="tpu_custom_call" | custom-call | flops 536870912 | bytes 2756608 | tf_op jit(solution)/shard_map/block/pallas_call | solution.py:66
  81.2 4.1 %all-to-all-start.3 = ((bf16[32,9,8,128]{3,2,1,0:T(8,128)(2,1)}), bf16[32,9,8,128]{3,2,1,0:T(8,128)(2,1)S(1)}, u32[]{:S(2)}, u32[]{:S(2)}) async-start(bf16[32,9,8,128]{3,2,1,0:T(8,128)(2,1)} %block.1.moment), calls=%async_computation.3 | async-start | bytes 1179648 | tf_op jit(solution)/shard_map/all_to_all | solution.py:422
  85.3 2.0 %stats.1 = (bf16[3,64,512]{2,1,0:T(8,128)(2,1)S(1)}, bf16[3,64,512]{2,1,0:T(8,128)(2,1)S(1)}, bf16[3,64,512]{2,1,0:T(8,128)(2,1)S(1)}, bf16[3,64,512]{2,1,0:T(8,...) custom-call(s32[1]{0:T(128)} %bitcast.1.index.other, ...), custom_call_target="tpu_custom_call" | custom-call | flops 536870912 | bytes 2752512 | tf_op jit(solution)/shard_map/stats/pallas_call | solution.py:66
  87.3 10.4 %all-to-all-done.3.got = bf16[32,9,8,128]{3,2,1,0:T(8,128)(2,1)S(1)} async-done(((bf16[32,9,8,128]{3,2,1,0:T(8,128)(2,1)}), bf16[32,9,8,128]{3,2,1,0:T(8,128)(2,1)S(1)}, u32[]{:S(2)}, u32[]{:S(2)}) %all-to-all-start.3) | async-done | bytes 589856 | tf_op jit(solution)/shard_map/all_to_all | solution.py:422
  97.7 0.9 unplane.1
  98.6 8.2 %all-to-all-start.4 = ((bf16[16,17,8,128]{3,2,1,0:T(8,128)(2,1)}), bf16[16,17,8,128]{3,2,1,0:T(8,128)(2,1)S(1)}, u32[]{:S(2)}, u32[]{:S(2)}) async-start(bf16[16,17,8,128]{3,2,1,0:T(8,128)(2,1)} %get-tuple-element.56), calls=%async_computation.4 | async-start | bytes 1114112 | tf_op jit(solution)/shard_map/all_to_all | solution.py:441
  106.8 2.4 %collective-permute-start.7 = (bf16[3,64,512]{2,1,0:T(8,128)(2,1)S(1)}, bf16[3,64,512]{2,1,0:T(8,128)(2,1)S(1)}, u32[]{:S(2)}, u32[]{:S(2)}) collective-permute-start(bf16[3,64,512]{2,1,0:T(8,128)(2,1)S(1)} %get-tuple-element.57), channel_id=1, source_target_pairs={{0,2},{1,3},{2,4},{3,5},{4,6},{5,7},{6,0},{7,1},{8,10},{9,11},{10,... | collective-permute-start | bytes 589832 | tf_op jit(solution)/shard_map/ppermute | solution.py:358
  109.3 4.1 %collective-permute-start.8 = (bf16[3,64,512]{2,1,0:T(8,128)(2,1)S(1)}, bf16[3,64,512]{2,1,0:T(8,128)(2,1)S(1)}, u32[]{:S(2)}, u32[]{:S(2)}) collective-permute-start(bf16[3,64,512]{2,1,0:T(8,128)(2,1)S(1)} %get-tuple-element.58), channel_id=1, source_target_pairs={{0,6},{1,7},{2,0},{3,1},{4,2},{5,3},{6,4},{7,5},{8,14},{9,15},{10,... | collective-permute-start | bytes 589832 | tf_op jit(solution)/shard_map/ppermute | solution.py:358
  113.3 1.9 %collective-permute-start.9 = (bf16[3,64,512]{2,1,0:T(8,128)(2,1)S(1)}, bf16[3,64,512]{2,1,0:T(8,128)(2,1)S(1)}, u32[]{:S(2)}, u32[]{:S(2)}) collective-permute-start(bf16[3,64,512]{2,1,0:T(8,128)(2,1)S(1)} %get-tuple-element.59), channel_id=1, source_target_pairs={{0,4},{1,5},{2,6},{3,7},{4,0},{5,1},{6,2},{7,3},{8,12},{9,13},{10,... | collective-permute-start | bytes 589832 | tf_op jit(solution)/shard_map/ppermute | solution.py:358
  115.3 4.8 %collective-permute-start.10 = (bf16[3,64,512]{2,1,0:T(8,128)(2,1)S(1)}, bf16[3,64,512]{2,1,0:T(8,128)(2,1)S(1)}, u32[]{:S(2)}, u32[]{:S(2)}) collective-permute-start(bf16[3,64,512]{2,1,0:T(8,128)(2,1)S(1)} %get-tuple-element.60), channel_id=1, source_target_pairs={{0,5},{1,6},{2,7},{3,0},{4,1},{5,2},{6,3},{7,4},{8,13},{9,14},{10,... | collective-permute-start | bytes 589832 | tf_op jit(solution)/shard_map/ppermute | solution.py:358
  120.1 3.5 %collective-permute-start.11 = (bf16[3,64,512]{2,1,0:T(8,128)(2,1)S(1)}, bf16[3,64,512]{2,1,0:T(8,128)(2,1)S(1)}, u32[]{:S(2)}, u32[]{:S(2)}) collective-permute-start(bf16[3,64,512]{2,1,0:T(8,128)(2,1)S(1)} %get-tuple-element.61), channel_id=1, source_target_pairs={{0,3},{1,4},{2,5},{3,6},{4,7},{5,0},{6,1},{7,2},{8,11},{9,12},{10,... | collective-permute-start | bytes 589832 | tf_op jit(solution)/shard_map/ppermute | solution.py:358
  123.6 0.0 collective-permute-start.12
  123.6 1.7 %collective-permute-start.13 = (bf16[3,64,512]{2,1,0:T(8,128)(2,1)S(1)}, bf16[3,64,512]{2,1,0:T(8,128)(2,1)S(1)}, u32[]{:S(2)}, u32[]{:S(2)}) collective-permute-start(bf16[3,64,512]{2,1,0:T(8,128)(2,1)S(1)} %get-tuple-element.63), channel_id=1, source_target_pairs={{0,1},{1,2},{2,3},{3,4},{4,5},{5,6},{6,7},{7,0},{8,9},{9,10},{10,1... | collective-permute-start | bytes 589832 | tf_op jit(solution)/shard_map/ppermute | solution.py:358
  125.4 3.9 %collective-permute-done.10.refs_3_.refs_5_ = bf16[3,64,512]{2,1,0:T(8,128)(2,1)S(1)} collective-permute-done((bf16[3,64,512]{2,1,0:T(8,128)(2,1)S(1)}, bf16[3,64,512]{2,1,0:T(8,128)(2,1)S(1)}, u32[]{:S(2)}, u32[]{:S(2)}) %collective-permute-start.10) | collective-permute-done | bytes 196640 | tf_op jit(solution)/shard_map/ppermute | solution.py:358
  129.2 2.7 %collective-permute-done.11.refs_4_.refs_3_ = bf16[3,64,512]{2,1,0:T(8,128)(2,1)S(1)} collective-permute-done((bf16[3,64,512]{2,1,0:T(8,128)(2,1)S(1)}, bf16[3,64,512]{2,1,0:T(8,128)(2,1)S(1)}, u32[]{:S(2)}, u32[]{:S(2)}) %collective-permute-start.11) | collective-permute-done | bytes 196640 | tf_op jit(solution)/shard_map/ppermute | solution.py:358
  131.9 0.0 copy-start.3
  131.9 1.3 place.1
  133.2 0.0 copy-start.2
  133.2 9.2 %all-to-all-start.5 = ((bf16[8,8,2048]{2,1,0:T(8,128)(2,1)}), bf16[8,8,2048]{2,1,0:T(8,128)(2,1)S(1)}, u32[]{:S(2)}, u32[]{:S(2)}) async-start(bf16[8,8,2048]{2,1,0:T(8,128)(2,1)} %place.1), calls=%async_computation.5 | async-start | bytes 524288 | tf_op jit(solution)/shard_map/all_to_all | solution.py:455
  142.4 0.2 select_reduce_fusion.1.source
  142.6 1.8 %finish.1 = (f32[4,64,512]{2,1,0:T(8,128)}, f32[4,64,512]{2,1,0:T(8,128)}, bf16[4,64,512]{2,1,0:T(8,128)(2,1)}) custom-call(s32[8]{0:T(128)S(1)} %select_reduce_fusion.1.source, f32[4,64,512]{2,1,0:T(8,128)S(1)} %bitcast.17, f32[4,64,512]{2,1,0:T(8,128)S(1)} %bitcast.18, bf16[3,64,512]{2,1,0:T(8,128)(2,1)S(1)} %get-tuple-element.65.refs_0_, ...), custom_call_target="tpu_custom_call" | custom-call | bytes 3932160 | tf_op jit(solution)/shard_map/finish/pallas_call | solution.py:66
  144.5 4.5 %all-to-all-done.5 = bf16[8,8,2048]{2,1,0:T(8,128)(2,1)S(1)} async-done(((bf16[8,8,2048]{2,1,0:T(8,128)(2,1)}), bf16[8,8,2048]{2,1,0:T(8,128)(2,1)S(1)}, u32[]{:S(2)}, u32[]{:S(2)}) %all-to-all-start.5) | async-done | bytes 262176 | tf_op jit(solution)/shard_map/all_to_all | solution.py:455
  148.9 0.8 fusion
  (20 shorter events, 0.1 us)
Async XLA Ops:
  0.6 12.0 %copy-start = (bf16[64,2048]{1,0:T(8,128)(2,1)S(1)}, bf16[64,2048]{1,0:T(8,128)(2,1)}, u32[]{:S(2)}) copy-start(bf16[64,2048]{1,0:T(8,128)(2,1)} %grad.1) | copy-start | bytes 786436
  0.6 16.9 %all-to-all-start = ((bf16[8,8,2048]{2,1,0:T(8,128)(2,1)}), bf16[8,8,2048]{2,1,0:T(8,128)(2,1)S(1)}, u32[]{:S(2)}, u32[]{:S(2)}) async-start(bf16[8,8,2048]{2,1,0:T(8,128)(2,1)} %bitcast.16), calls=%async_computation | async-start | bytes 524288 | tf_op jit(solution)/shard_map/all_to_all | solution.py:367
  11.0 0.7 copy-start.9
  12.6 1.0 copy-start.1
  18.9 10.7 %copy-start.4 = (bf16[1,4,64,512]{3,2,1,0:T(8,128)(2,1)S(1)}, bf16[1,4,64,512]{3,2,1,0:T(8,128)(2,1)}, u32[]{:S(2)}) copy-start(bf16[1,4,64,512]{3,2,1,0:T(8,128)(2,1)} %param.13) | copy-start | bytes 786436
  19.0 10.7 %copy-start.5 = (bf16[1,4,64,512]{3,2,1,0:T(8,128)(2,1)S(1)}, bf16[1,4,64,512]{3,2,1,0:T(8,128)(2,1)}, u32[]{:S(2)}) copy-start(bf16[1,4,64,512]{3,2,1,0:T(8,128)(2,1)} %param.14) | copy-start | bytes 786436
  19.0 10.7 %copy-start.6 = (bf16[1,4,64,512]{3,2,1,0:T(8,128)(2,1)S(1)}, bf16[1,4,64,512]{3,2,1,0:T(8,128)(2,1)}, u32[]{:S(2)}) copy-start(bf16[1,4,64,512]{3,2,1,0:T(8,128)(2,1)} %param.15) | copy-start | bytes 786436
  19.0 37.3 %all-to-all-start.1 = ((bf16[16,17,8,128]{3,2,1,0:T(8,128)(2,1)}), bf16[16,17,8,128]{3,2,1,0:T(8,128)(2,1)S(1)}, u32[]{:S(2)}, u32[]{:S(2)}) async-start(bf16[16,17,8,128]{3,2,1,0:T(8,128)(2,1)} %spread.1.after), calls=%async_computation.1 | async-start | bytes 1114112 | tf_op jit(solution)/shard_map/all_to_all | solution.py:386
  30.3 0.7 copy-start.7
  31.0 17.3 %collective-permute-start = (bf16[3,64,512]{2,1,0:T(8,128)(2,1)S(1)}, bf16[3,64,512]{2,1,0:T(8,128)(2,1)S(1)}, u32[]{:S(2)}, u32[]{:S(2)}) collective-permute-start(bf16[3,64,512]{2,1,0:T(8,128)(2,1)S(1)} %get-tuple-element.38), channel_id=1, source_target_pairs={{0,2},{1,3},{2,4},{3,5},{4,6},{5,7},{6,0},{7,1},{8,10},{9,11},{10,... | collective-permute-start | bytes 589832 | tf_op jit(solution)/shard_map/ppermute | solution.py:358
  33.2 15.1 %collective-permute-start.1 = (bf16[3,64,512]{2,1,0:T(8,128)(2,1)S(1)}, bf16[3,64,512]{2,1,0:T(8,128)(2,1)S(1)}, u32[]{:S(2)}, u32[]{:S(2)}) collective-permute-start(bf16[3,64,512]{2,1,0:T(8,128)(2,1)S(1)} %get-tuple-element.39), channel_id=1, source_target_pairs={{0,6},{1,7},{2,0},{3,1},{4,2},{5,3},{6,4},{7,5},{8,14},{9,15},{10,... | collective-permute-start | bytes 589832 | tf_op jit(solution)/shard_map/ppermute | solution.py:358
  37.5 12.6 %collective-permute-start.2 = (bf16[3,64,512]{2,1,0:T(8,128)(2,1)S(1)}, bf16[3,64,512]{2,1,0:T(8,128)(2,1)S(1)}, u32[]{:S(2)}, u32[]{:S(2)}) collective-permute-start(bf16[3,64,512]{2,1,0:T(8,128)(2,1)S(1)} %get-tuple-element.40), channel_id=1, source_target_pairs={{0,4},{1,5},{2,6},{3,7},{4,0},{5,1},{6,2},{7,3},{8,12},{9,13},{10,... | collective-permute-start | bytes 589832 | tf_op jit(solution)/shard_map/ppermute | solution.py:358
  39.4 14.2 %collective-permute-start.3 = (bf16[3,64,512]{2,1,0:T(8,128)(2,1)S(1)}, bf16[3,64,512]{2,1,0:T(8,128)(2,1)S(1)}, u32[]{:S(2)}, u32[]{:S(2)}) collective-permute-start(bf16[3,64,512]{2,1,0:T(8,128)(2,1)S(1)} %get-tuple-element.41), channel_id=1, source_target_pairs={{0,5},{1,6},{2,7},{3,0},{4,1},{5,2},{6,3},{7,4},{8,13},{9,14},{10,... | collective-permute-start | bytes 589832 | tf_op jit(solution)/shard_map/ppermute | solution.py:358
  44.8 11.5 %collective-permute-start.4 = (bf16[3,64,512]{2,1,0:T(8,128)(2,1)S(1)}, bf16[3,64,512]{2,1,0:T(8,128)(2,1)S(1)}, u32[]{:S(2)}, u32[]{:S(2)}) collective-permute-start(bf16[3,64,512]{2,1,0:T(8,128)(2,1)S(1)} %get-tuple-element.42), channel_id=1, source_target_pairs={{0,3},{1,4},{2,5},{3,6},{4,7},{5,0},{6,1},{7,2},{8,11},{9,12},{10,... | collective-permute-start | bytes 589832 | tf_op jit(solution)/shard_map/ppermute | solution.py:358
  48.3 8.0 %collective-permute-start.5 = (bf16[3,64,512]{2,1,0:T(8,128)(2,1)S(1)}, bf16[3,64,512]{2,1,0:T(8,128)(2,1)S(1)}, u32[]{:S(2)}, u32[]{:S(2)}) collective-permute-start(bf16[3,64,512]{2,1,0:T(8,128)(2,1)S(1)} %get-tuple-element.43), channel_id=1, source_target_pairs={{0,7},{1,0},{2,1},{3,2},{4,3},{5,4},{6,5},{7,6},{8,15},{9,8},{10,9... | collective-permute-start | bytes 589832 | tf_op jit(solution)/shard_map/ppermute | solution.py:358
  48.3 8.0 %collective-permute-start.6 = (bf16[3,64,512]{2,1,0:T(8,128)(2,1)S(1)}, bf16[3,64,512]{2,1,0:T(8,128)(2,1)S(1)}, u32[]{:S(2)}, u32[]{:S(2)}) collective-permute-start(bf16[3,64,512]{2,1,0:T(8,128)(2,1)S(1)} %get-tuple-element.44), channel_id=1, source_target_pairs={{0,1},{1,2},{2,3},{3,4},{4,5},{5,6},{6,7},{7,0},{8,9},{9,10},{10,1... | collective-permute-start | bytes 589832 | tf_op jit(solution)/shard_map/ppermute | solution.py:358
  57.2 21.8 %all-to-all-start.2 = ((bf16[32,9,8,128]{3,2,1,0:T(8,128)(2,1)}), bf16[32,9,8,128]{3,2,1,0:T(8,128)(2,1)S(1)}, u32[]{:S(2)}, u32[]{:S(2)}) async-start(bf16[32,9,8,128]{3,2,1,0:T(8,128)(2,1)} %plane.1), calls=%async_computation.2 | async-start | bytes 1179648 | tf_op jit(solution)/shard_map/all_to_all | solution.py:398
  68.1 0.9 copy-start.8
  81.2 16.4 %all-to-all-start.3 = ((bf16[32,9,8,128]{3,2,1,0:T(8,128)(2,1)}), bf16[32,9,8,128]{3,2,1,0:T(8,128)(2,1)S(1)}, u32[]{:S(2)}, u32[]{:S(2)}) async-start(bf16[32,9,8,128]{3,2,1,0:T(8,128)(2,1)} %block.1.moment), calls=%async_computation.3 | async-start | bytes 1179648 | tf_op jit(solution)/shard_map/all_to_all | solution.py:422
  98.6 33.3 %all-to-all-start.4 = ((bf16[16,17,8,128]{3,2,1,0:T(8,128)(2,1)}), bf16[16,17,8,128]{3,2,1,0:T(8,128)(2,1)S(1)}, u32[]{:S(2)}, u32[]{:S(2)}) async-start(bf16[16,17,8,128]{3,2,1,0:T(8,128)(2,1)} %get-tuple-element.56), calls=%async_computation.4 | async-start | bytes 1114112 | tf_op jit(solution)/shard_map/all_to_all | solution.py:441
  106.8 16.8 %collective-permute-start.7 = (bf16[3,64,512]{2,1,0:T(8,128)(2,1)S(1)}, bf16[3,64,512]{2,1,0:T(8,128)(2,1)S(1)}, u32[]{:S(2)}, u32[]{:S(2)}) collective-permute-start(bf16[3,64,512]{2,1,0:T(8,128)(2,1)S(1)} %get-tuple-element.57), channel_id=1, source_target_pairs={{0,2},{1,3},{2,4},{3,5},{4,6},{5,7},{6,0},{7,1},{8,10},{9,11},{10,... | collective-permute-start | bytes 589832 | tf_op jit(solution)/shard_map/ppermute | solution.py:358
  109.3 14.4 %collective-permute-start.8 = (bf16[3,64,512]{2,1,0:T(8,128)(2,1)S(1)}, bf16[3,64,512]{2,1,0:T(8,128)(2,1)S(1)}, u32[]{:S(2)}, u32[]{:S(2)}) collective-permute-start(bf16[3,64,512]{2,1,0:T(8,128)(2,1)S(1)} %get-tuple-element.58), channel_id=1, source_target_pairs={{0,6},{1,7},{2,0},{3,1},{4,2},{5,3},{6,4},{7,5},{8,14},{9,15},{10,... | collective-permute-start | bytes 589832 | tf_op jit(solution)/shard_map/ppermute | solution.py:358
  113.3 12.0 %collective-permute-start.9 = (bf16[3,64,512]{2,1,0:T(8,128)(2,1)S(1)}, bf16[3,64,512]{2,1,0:T(8,128)(2,1)S(1)}, u32[]{:S(2)}, u32[]{:S(2)}) collective-permute-start(bf16[3,64,512]{2,1,0:T(8,128)(2,1)S(1)} %get-tuple-element.59), channel_id=1, source_target_pairs={{0,4},{1,5},{2,6},{3,7},{4,0},{5,1},{6,2},{7,3},{8,12},{9,13},{10,... | collective-permute-start | bytes 589832 | tf_op jit(solution)/shard_map/ppermute | solution.py:358
  115.3 14.0 %collective-permute-start.10 = (bf16[3,64,512]{2,1,0:T(8,128)(2,1)S(1)}, bf16[3,64,512]{2,1,0:T(8,128)(2,1)S(1)}, u32[]{:S(2)}, u32[]{:S(2)}) collective-permute-start(bf16[3,64,512]{2,1,0:T(8,128)(2,1)S(1)} %get-tuple-element.60), channel_id=1, source_target_pairs={{0,5},{1,6},{2,7},{3,0},{4,1},{5,2},{6,3},{7,4},{8,13},{9,14},{10,... | collective-permute-start | bytes 589832 | tf_op jit(solution)/shard_map/ppermute | solution.py:358
  120.1 11.8 %collective-permute-start.11 = (bf16[3,64,512]{2,1,0:T(8,128)(2,1)S(1)}, bf16[3,64,512]{2,1,0:T(8,128)(2,1)S(1)}, u32[]{:S(2)}, u32[]{:S(2)}) collective-permute-start(bf16[3,64,512]{2,1,0:T(8,128)(2,1)S(1)} %get-tuple-element.61), channel_id=1, source_target_pairs={{0,3},{1,4},{2,5},{3,6},{4,7},{5,0},{6,1},{7,2},{8,11},{9,12},{10,... | collective-permute-start | bytes 589832 | tf_op jit(solution)/shard_map/ppermute | solution.py:358
  123.6 8.3 %collective-permute-start.12 = (bf16[3,64,512]{2,1,0:T(8,128)(2,1)S(1)}, bf16[3,64,512]{2,1,0:T(8,128)(2,1)S(1)}, u32[]{:S(2)}, u32[]{:S(2)}) collective-permute-start(bf16[3,64,512]{2,1,0:T(8,128)(2,1)S(1)} %get-tuple-element.62), channel_id=1, source_target_pairs={{0,7},{1,0},{2,1},{3,2},{4,3},{5,4},{6,5},{7,6},{8,15},{9,8},{10,9... | collective-permute-start | bytes 589832 | tf_op jit(solution)/shard_map/ppermute | solution.py:358
  123.6 8.3 %collective-permute-start.13 = (bf16[3,64,512]{2,1,0:T(8,128)(2,1)S(1)}, bf16[3,64,512]{2,1,0:T(8,128)(2,1)S(1)}, u32[]{:S(2)}, u32[]{:S(2)}) collective-permute-start(bf16[3,64,512]{2,1,0:T(8,128)(2,1)S(1)} %get-tuple-element.63), channel_id=1, source_target_pairs={{0,1},{1,2},{2,3},{3,4},{4,5},{5,6},{6,7},{7,0},{8,9},{9,10},{10,1... | collective-permute-start | bytes 589832 | tf_op jit(solution)/shard_map/ppermute | solution.py:358
  131.9 10.7 %copy-start.3 = (f32[1,4,64,512]{3,2,1,0:T(8,128)S(1)}, f32[1,4,64,512]{3,2,1,0:T(8,128)}, u32[]{:S(2)}) copy-start(f32[1,4,64,512]{3,2,1,0:T(8,128)} %param.12) | copy-start | bytes 1572868
  133.2 9.4 %copy-start.2 = (f32[1,4,64,512]{3,2,1,0:T(8,128)S(1)}, f32[1,4,64,512]{3,2,1,0:T(8,128)}, u32[]{:S(2)}) copy-start(f32[1,4,64,512]{3,2,1,0:T(8,128)} %param.11) | copy-start | bytes 1572868
  133.2 15.7 %all-to-all-start.5 = ((bf16[8,8,2048]{2,1,0:T(8,128)(2,1)}), bf16[8,8,2048]{2,1,0:T(8,128)(2,1)S(1)}, u32[]{:S(2)}, u32[]{:S(2)}) async-start(bf16[8,8,2048]{2,1,0:T(8,128)(2,1)} %place.1), calls=%async_computation.5 | async-start | bytes 524288 | tf_op jit(solution)/shard_map/all_to_all | solution.py:455
